TPU v7x, 32 devices: a whole 2x2x4 slice. The times are simulated.
32 devices in a mesh: pipe: 2 (over core), group: 4 (over y, x), local: 4 (over z).
Axes of the slice: x: 2, y: 2, z: 4, core: 2. Of those that a mesh axis runs over, the one named last changes fastest.
Arguments:
- output_grad: bfloat16 [2, 512, 2048], P(None, ('group', 'local')), may hold values from -6 to 6
- carried_grad: bfloat16 [512, 2048], P(('group', 'local')), may hold values from -6 to 6
- layer_inputs: bfloat16 [2, 2, 512, 2048], P('pipe', None, ('group', 'local')), may hold values from -6 to 6
- expert_ids: int32 [2, 2, 512, 6], P('pipe', None, ('group', 'local')), may hold values from 0 to 7, all different within a row; in each aligned block of 32 rows (0 to 31, 32 to 63, ..., all dimensions but the last counted through in order) at most 32 rows name the same one
- gate_prob: bfloat16 [2, 2, 512, 6], P('pipe', None, ('group', 'local')), may hold values from 0.099609375 to 0.796875
- gate_weight: bfloat16 [2, 16, 2048, 704], P('pipe', ('group', 'local')), may hold values from -0.125 to 0.125
- up_weight: bfloat16 [2, 16, 2048, 704], P('pipe', ('group', 'local')), may hold values from -0.125 to 0.125
- down_weight: bfloat16 [2, 16, 704, 2048], P('pipe', ('group', 'local')), may hold values from -0.15625 to 0.15625
Outputs:
- input_grad: bfloat16 [2, 2, 512, 2048], P('pipe', None, ('group', 'local'))
- gate_grad: bfloat16 [2, 2, 512, 6], P('pipe', None, ('group', 'local'))
Inputs may be any that keep to these rules, and one draw needn't show every extreme that they name: `expert_ids`: each token names 6 different experts. Within each section and microbatch, the 32 tokens of one device (aligned blocks of rows) name any one expert at most 32 times.
All inputs are finite; a program needn't handle non-finite values.
Results may differ from a plain program's by a relative error of at most 0.0065.
Values may be sent and summed in bfloat16 or wider, within the bound.
No kernel may reach another device: no remote copies, remote signals or barrier semaphores. Data moves between devices by JAX's collectives and lax.ppermute only.
A program may use at most 128 MiB of HBM per device.

v0:
```python
import jax
import jax.numpy as jnp
from jax import lax
from jax.sharding import PartitionSpec as P

CONTRACT_LAST = (((1,), (1,)), ((), ()))
CONTRACT_FIRST = (((0,), (0,)), ((), ()))


def swapped(value, axis, bit):
    mask = 2**bit
    pairs = [(source, source ^ mask) for source in range(lax.axis_size(axis))]
    return lax.ppermute(value, axis, pairs)


def from_behind(block, axis, distance):
    devices = range(lax.axis_size(axis))
    route = [(i - distance, i) for i in devices if i - distance in devices]
    return lax.ppermute(block, axis, route)


def expert_backward(rows_in, rows_grad, row_probs, gate_full, up_full, down_full):
    gate_pre = jnp.dot(rows_in, gate_full, preferred_element_type=jnp.float32)
    up_pre = jnp.dot(rows_in, up_full, preferred_element_type=jnp.float32)
    back_proj = lax.dot_general(
        rows_grad, down_full, CONTRACT_LAST, preferred_element_type=jnp.float32
    )
    sigmoid_gate = jax.nn.sigmoid(gate_pre)
    activated = gate_pre * sigmoid_gate
    gate_part = jnp.sum(activated * up_pre * back_proj, axis=1)
    scaled = row_probs.astype(jnp.float32)[:, None] * back_proj
    grad_gate = (scaled * up_pre * sigmoid_gate * (1.0 + gate_pre * (1.0 - sigmoid_gate))).astype(
        jnp.bfloat16
    )
    grad_up = (scaled * activated).astype(jnp.bfloat16)
    grad_rows = lax.dot_general(
        grad_gate, gate_full, CONTRACT_LAST, preferred_element_type=jnp.float32
    )
    grad_rows = grad_rows + lax.dot_general(
        grad_up, up_full, CONTRACT_LAST, preferred_element_type=jnp.float32
    )
    return (grad_rows, gate_part)


def route_tables(choice_ids, choice_probs, expert_count, capacity):
    expert_range = jnp.arange(expert_count, dtype=jnp.int32)
    matches = (choice_ids[:, :, None] == expert_range[None, None, :]).astype(jnp.int32)
    chosen = jnp.sum(matches, axis=1)
    before = jnp.cumsum(chosen, axis=0) - chosen
    slot_range = jnp.arange(capacity, dtype=jnp.int32)
    placed = (before[:, :, None] == slot_range[None, None, :]) & (chosen[:, :, None] > 0)
    slot_map = jnp.transpose(placed, (1, 2, 0)).astype(jnp.float32)
    token_probs = jnp.sum(
        matches.astype(jnp.float32) * choice_probs.astype(jnp.float32)[:, :, None], axis=1
    )
    slot_probs = jnp.einsum("ect,te->ec", slot_map, token_probs)
    return (matches, slot_map, slot_probs)


def layer_backward(incoming, inputs, choice_ids, choice_probs, weights_local, expert_count):
    tokens_here = incoming.shape[0]
    model_width = incoming.shape[1]
    top_count = choice_ids.shape[1]
    capacity = 2 * ((tokens_here * top_count * 2 + 3 * expert_count - 1) // (3 * expert_count))
    half_slots = capacity // 2
    devices = 2 * expert_count
    matches, slot_map, slot_probs = route_tables(choice_ids, choice_probs, expert_count, capacity)
    flat_map = slot_map.reshape(expert_count * capacity, tokens_here).astype(jnp.bfloat16)
    sent_inputs = jnp.dot(flat_map, inputs, preferred_element_type=jnp.float32).astype(jnp.bfloat16)
    sent_grads = jnp.dot(flat_map, incoming, preferred_element_type=jnp.float32).astype(
        jnp.bfloat16
    )
    sent_probs = slot_probs.reshape(expert_count * capacity).astype(jnp.bfloat16)
    gate_full, up_full, down_full = weights_local
    got_inputs, got_grads, got_probs = (
        lax.all_to_all(sent_inputs, ("group", "local"), split_axis=0, concat_axis=0, tiled=True),
        lax.all_to_all(sent_grads, ("group", "local"), split_axis=0, concat_axis=0, tiled=True),
        lax.all_to_all(sent_probs, ("group", "local"), split_axis=0, concat_axis=0, tiled=True),
    )
    grad_rows, gate_part = expert_backward(
        got_inputs, got_grads, got_probs, gate_full, up_full, down_full
    )
    kept_grad = grad_rows.reshape(devices, half_slots, model_width)
    kept_part = gate_part.reshape(devices, half_slots)
    back_grad, back_part = (
        lax.all_to_all(
            kept_grad.astype(jnp.bfloat16),
            ("group", "local"),
            split_axis=0,
            concat_axis=0,
            tiled=True,
        ),
        lax.all_to_all(
            kept_part.astype(jnp.bfloat16),
            ("group", "local"),
            split_axis=0,
            concat_axis=0,
            tiled=True,
        ),
    )
    back_grad = back_grad.reshape(expert_count * capacity, model_width)
    summed = incoming.astype(jnp.float32) + lax.dot_general(
        flat_map, back_grad, CONTRACT_FIRST, preferred_element_type=jnp.float32
    )
    per_expert = jnp.einsum(
        "ect,ec->te", slot_map, back_part.reshape(expert_count, capacity).astype(jnp.float32)
    )
    gate_values = jnp.sum(matches.astype(jnp.float32) * per_expert[:, None, :], axis=2)
    return (summed.astype(jnp.bfloat16), gate_values.astype(jnp.bfloat16))


def local(
    output_grad,
    carried_grad,
    layer_inputs,
    expert_ids,
    gate_prob,
    gate_weight,
    up_weight,
    down_weight,
):
    expert_count = lax.axis_size("group") * lax.axis_size("local") // 2
    gate_local = gate_weight[0, 0]
    up_local = up_weight[0, 0]
    down_local = down_weight[0, 0]
    gate_other, up_other, down_other = swapped((gate_local, up_local, down_local), "local", 0)
    weights_local = (
        jnp.concatenate([gate_local, gate_other], axis=1),
        jnp.concatenate([up_local, up_other], axis=1),
        jnp.concatenate([down_local, down_other], axis=0),
    )
    last_section = lax.axis_index("pipe") == lax.axis_size("pipe") - 1
    micro_count = output_grad.shape[0]
    grads_out = []
    gates_out = []
    previous = carried_grad
    for micro_index in range(micro_count):
        if micro_index == 0:
            earlier = carried_grad
        else:
            earlier = from_behind(previous, "pipe", -1)
        incoming = jnp.where(last_section, output_grad[micro_index], earlier)
        result_grad, result_gate = layer_backward(
            incoming,
            layer_inputs[0, micro_index],
            expert_ids[0, micro_index],
            gate_prob[0, micro_index],
            weights_local,
            expert_count,
        )
        grads_out.append(result_grad)
        gates_out.append(result_gate)
        previous = result_grad
    return (jnp.stack(grads_out)[None], jnp.stack(gates_out)[None])


def solution(mesh):
    return jax.shard_map(
        local,
        mesh=mesh,
        in_specs=(
            P(None, ("group", "local"), None),
            P(("group", "local"), None),
            P("pipe", None, ("group", "local"), None),
            P("pipe", None, ("group", "local"), None),
            P("pipe", None, ("group", "local"), None),
            P("pipe", ("group", "local"), None, None),
            P("pipe", ("group", "local"), None, None),
            P("pipe", ("group", "local"), None, None),
        ),
        out_specs=(
            P("pipe", None, ("group", "local"), None),
            P("pipe", None, ("group", "local"), None),
        ),
        check_vma=False,
    )
```

profile of v0, /device:TPU:0, one launch (start us, length us, event | category | flops | bytes accessed | tf_op | source)
XLA Modules:
  0.0 429.9 jit_solution(11672225794712982336)
XLA Ops:
  4.1 8.4 %all-to-all-start.2 = ((bf16[16,16,2048]{2,1,0:T(8,128)(2,1)}), bf16[16,16,2048]{2,1,0:T(8,128)(2,1)S(1)}, u32[]{:S(2)}, u32[]{:S(2)}) async-start(bf16[16,16,2048]{2,1,0:T(8,128)(2,1)} %bitcast.16), calls=%async_computation.2 | async-start | bytes 2097152 | tf_op jit(solution)/shard_map/all_to_all | solution.py:76
  18.3 21.8 %all-to-all-done.2 = bf16[16,16,2048]{2,1,0:T(8,128)(2,1)S(1)} async-done(((bf16[16,16,2048]{2,1,0:T(8,128)(2,1)}), bf16[16,16,2048]{2,1,0:T(8,128)(2,1)S(1)}, u32[]{:S(2)}, u32[]{:S(2)}) %all-to-all-start.2) | async-done | bytes 1048608 | tf_op jit(solution)/shard_map/all_to_all | solution.py:76
  43.8 56.5 %collective-permute-done.2 = bf16[2048,704]{0,1:T(8,128)(2,1)} collective-permute-done((bf16[2048,704]{0,1:T(8,128)(2,1)}, bf16[2048,704]{0,1:T(8,128)(2,1)}, u32[]{:S(2)}, u32[]{:S(2)}) %collective-permute-start.2) | collective-permute-done | bytes 2883616 | tf_op jit(solution)/shard_map/ppermute | solution.py:13
  100.3 5.8 %fusion.59 = f32[256,1408]{1,0:T(8,128)} fusion(bf16[256,2048]{1,0:T(8,128)(2,1)S(1)} %bitcast.122, bf16[2048,704]{0,1:T(8,128)(2,1)} %collective-permute-done.2, bf16[2048,704]{0,1:T(8,128)(2,1)} %bitcast.150), kind=kOutput, calls=%fused_computation.102 | convolution fusion | flops 1487929344 | bytes 8257536 | tf_op jit(solution)/shard_map/dot_general | solution.py:23
  106.0 56.0 %collective-permute-done.1 = bf16[2048,704]{0,1:T(8,128)(2,1)} collective-permute-done((bf16[2048,704]{0,1:T(8,128)(2,1)}, bf16[2048,704]{0,1:T(8,128)(2,1)}, u32[]{:S(2)}, u32[]{:S(2)}) %collective-permute-start.1) | collective-permute-done | bytes 2883616 | tf_op jit(solution)/shard_map/ppermute | solution.py:13
  162.0 4.9 %fusion.61 = f32[256,1408]{1,0:T(8,128)} fusion(bf16[256,2048]{1,0:T(8,128)(2,1)S(1)} %bitcast.123, bf16[2048,704]{0,1:T(8,128)(2,1)} %collective-permute-done.1, bf16[2048,704]{0,1:T(8,128)(2,1)S(1)} %bitcast.147), kind=kOutput, calls=%fused_computation.104 | convolution fusion | flops 1487929344 | bytes 8257536 | tf_op jit(solution)/shard_map/dot_general | solution.py:24
  167.0 67.5 %all-to-all-done.1 = bf16[16,16,2048]{2,1,0:T(8,128)(2,1)S(1)} async-done(((bf16[16,16,2048]{2,1,0:T(8,128)(2,1)}), bf16[16,16,2048]{2,1,0:T(8,128)(2,1)S(1)}, u32[]{:S(2)}, u32[]{:S(2)}) %all-to-all-start.1) | async-done | bytes 1048608 | tf_op jit(solution)/shard_map/all_to_all | solution.py:77
  234.4 6.5 %multiply_reduce_fusion.1 = (bf16[256]{0:T(256)(128)(2,1)S(1)}, f32[256,1408]{1,0:T(8,128)}) fusion(f32[256,1408]{1,0:T(8,128)} %fusion.61, f32[256,1408]{1,0:T(8,128)} %fusion.59, bf16[256,2048]{1,0:T(8,128)(2,1)S(1)} %bitcast.126, bf16[704,2048]{1,0:T(8,128)(2,1)} %collective-permute-done, bf16[704,2048]{1,0:T(8,128)(2,1)} %bitcast.142), kind=kOutput, calls=%fused_computation.16 | convolution fusion | flops 1490452224 | bytes 11141632 | tf_op jit(solution)/shard_map/dot_general | solution.py:25
  241.7 5.2 %all-to-all-start.8 = ((bf16[16,1,16]{2,1,0:T(2,128)(2,1)}), bf16[16,1,16]{2,1,0:T(2,128)(2,1)S(1)}, u32[]{:S(2)}, u32[]{:S(2)}) async-start(bf16[16,1,16]{2,1,0:T(2,128)(2,1)} %convert_element_type.308), calls=%async_computation.8 | async-start | bytes 16384 | tf_op jit(solution)/shard_map/all_to_all | solution.py:93
  246.9 7.2 %all-to-all-done.8 = bf16[16,1,16]{2,1,0:T(2,128)(2,1)S(1)} async-done(((bf16[16,1,16]{2,1,0:T(2,128)(2,1)}), bf16[16,1,16]{2,1,0:T(2,128)(2,1)S(1)}, u32[]{:S(2)}, u32[]{:S(2)}) %all-to-all-start.8) | async-done | bytes 544 | tf_op jit(solution)/shard_map/all_to_all | solution.py:93
  254.6 9.8 %all_to_all.82 = bf16[16,16,1]{1,2,0:T(2,128)(2,1)S(1)} all-to-all(bf16[16,16,1]{1,2,0:T(2,128)(2,1)S(1)} %convert_element_type.306), channel_id=1, replica_groups=mesh['pipe'=2,'group'=4,'local'=4] {'group','local'}, dimensions={0} | all-to-all | bytes 1024 | tf_op jit(solution)/shard_map/all_to_all | solution.py:78
  264.5 5.0 %fusion.7 = f32[256,2048]{1,0:T(8,128)S(1)} fusion(f32[256,1408]{1,0:T(8,128)} %get-tuple-element.21, f32[256]{0:T(256)S(1)} %reshape.287, f32[256,1408]{1,0:T(8,128)} %fusion.59, bf16[2048,704]{0,1:T(8,128)(2,1)} %collective-permute-done.1, bf16[2048,704]{0,1:T(8,128)(2,1)} %bitcast.145), kind=kOutput, calls=%fused_computation.25 | convolution fusion | flops 1490452480 | bytes 10748928 | tf_op jit(solution)/shard_map/dot_general | solution.py:39
  270.2 5.0 %fusion.2 = bf16[256,2048]{1,0:T(8,128)(2,1)} fusion(f32[256,2048]{1,0:T(8,128)S(1)} %fusion.7, f32[256,1408]{1,0:T(8,128)S(1)} %copy-done.8, f32[256,1408]{1,0:T(8,128)S(1)} %copy-done.9, f32[256,1408]{1,0:T(8,128)S(1)} %copy-done.12, f32[256]{0:T(256)S(1)} %reshape.287, bf16[2048,704]{0,1:T(8,128)(2,1)} %collective-permute-done.2, ...), kind=kOutput, calls=%fused_computation.7 | convolution fusion | flops 1492942848 | bytes 13239296 | tf_op jit(solution)/shard_map/dot_general | solution.py:36
  280.4 22.1 %all-to-all-done.3 = bf16[16,16,2048]{2,1,0:T(8,128)(2,1)S(1)} async-done(((bf16[16,16,2048]{2,1,0:T(8,128)(2,1)}), bf16[16,16,2048]{2,1,0:T(8,128)(2,1)S(1)}, u32[]{:S(2)}, u32[]{:S(2)}) %all-to-all-start.3) | async-done | bytes 1048608 | tf_op jit(solution)/shard_map/all_to_all | solution.py:86
  311.1 20.9 %all-to-all-done.6 = bf16[16,16,2048]{2,1,0:T(8,128)(2,1)S(1)} async-done(((bf16[16,16,2048]{2,1,0:T(8,128)(2,1)}), bf16[16,16,2048]{2,1,0:T(8,128)(2,1)S(1)}, u32[]{:S(2)}, u32[]{:S(2)}) %all-to-all-start.6) | async-done | bytes 1048608 | tf_op jit(solution)/shard_map/all_to_all | solution.py:76
  335.9 5.8 %fusion.58 = f32[256,1408]{1,0:T(8,128)} fusion(bf16[256,2048]{1,0:T(8,128)(2,1)S(1)} %bitcast.124, bf16[2048,704]{0,1:T(8,128)(2,1)} %collective-permute-done.2, bf16[2048,704]{0,1:T(8,128)(2,1)} %bitcast.151), kind=kOutput, calls=%fused_computation.101 | convolution fusion | flops 1487929344 | bytes 8257536 | tf_op jit(solution)/shard_map/dot_general | solution.py:23
  341.6 4.8 %fusion.60 = f32[256,1408]{1,0:T(8,128)} fusion(bf16[256,2048]{1,0:T(8,128)(2,1)S(1)} %bitcast.125, bf16[2048,704]{0,1:T(8,128)(2,1)} %collective-permute-done.1, bf16[2048,704]{0,1:T(8,128)(2,1)S(1)} %bitcast.148), kind=kOutput, calls=%fused_computation.103 | convolution fusion | flops 1487929344 | bytes 8257536 | tf_op jit(solution)/shard_map/dot_general | solution.py:24
  346.4 15.8 %all-to-all-done.5 = bf16[16,16,2048]{2,1,0:T(8,128)(2,1)S(1)} async-done(((bf16[16,16,2048]{2,1,0:T(8,128)(2,1)}), bf16[16,16,2048]{2,1,0:T(8,128)(2,1)S(1)}, u32[]{:S(2)}, u32[]{:S(2)}) %all-to-all-start.5) | async-done | bytes 1048608 | tf_op jit(solution)/shard_map/all_to_all | solution.py:77
  362.3 6.5 %multiply_reduce_fusion = (bf16[256]{0:T(256)(128)(2,1)S(1)}, f32[256,1408]{1,0:T(8,128)}) fusion(f32[256,1408]{1,0:T(8,128)} %fusion.60, f32[256,1408]{1,0:T(8,128)} %fusion.58, bf16[256,2048]{1,0:T(8,128)(2,1)S(1)} %bitcast.127, bf16[704,2048]{1,0:T(8,128)(2,1)} %collective-permute-done, bf16[704,2048]{1,0:T(8,128)(2,1)} %bitcast.143), kind=kOutput, calls=%fused_computation.15 | convolution fusion | flops 1490452224 | bytes 11141632 | tf_op jit(solution)/shard_map/dot_general | solution.py:25
  368.9 9.9 %all_to_all.83 = bf16[16,1,16]{2,1,0:T(2,128)(2,1)S(1)} all-to-all(bf16[16,1,16]{2,1,0:T(2,128)(2,1)S(1)} %convert_element_type.309), channel_id=1, replica_groups=mesh['pipe'=2,'group'=4,'local'=4] {'group','local'}, dimensions={0} | all-to-all | bytes 1024 | tf_op jit(solution)/shard_map/all_to_all | solution.py:93
  379.3 9.8 %all_to_all.84 = bf16[16,16,1]{1,2,0:T(2,128)(2,1)S(1)} all-to-all(bf16[16,16,1]{1,2,0:T(2,128)(2,1)S(1)} %convert_element_type.307), channel_id=1, replica_groups=mesh['pipe'=2,'group'=4,'local'=4] {'group','local'}, dimensions={0} | all-to-all | bytes 1024 | tf_op jit(solution)/shard_map/all_to_all | solution.py:78
  389.3 5.0 %fusion.8 = f32[256,2048]{1,0:T(8,128)S(1)} fusion(f32[256,1408]{1,0:T(8,128)} %get-tuple-element.23, f32[256]{0:T(256)S(1)} %reshape.289, f32[256,1408]{1,0:T(8,128)} %fusion.58, bf16[2048,704]{0,1:T(8,128)(2,1)} %collective-permute-done.1, bf16[2048,704]{0,1:T(8,128)(2,1)} %bitcast.146), kind=kOutput, calls=%fused_computation.26 | convolution fusion | flops 1490452480 | bytes 10748928 | tf_op jit(solution)/shard_map/dot_general | solution.py:39
  394.9 5.0 %fusion.3 = bf16[256,2048]{1,0:T(8,128)(2,1)} fusion(f32[256,2048]{1,0:T(8,128)S(1)} %fusion.8, f32[256,1408]{1,0:T(8,128)S(1)} %copy-done.10, f32[256,1408]{1,0:T(8,128)S(1)} %copy-done.11, f32[256,1408]{1,0:T(8,128)S(1)} %copy-done.13, f32[256]{0:T(256)S(1)} %reshape.289, bf16[2048,704]{0,1:T(8,128)(2,1)} %collective-permute-done.2, ...), kind=kOutput, calls=%fused_computation.8 | convolution fusion | flops 1492942848 | bytes 13239296 | tf_op jit(solution)/shard_map/dot_general | solution.py:36
  404.1 24.7 %all-to-all-done.7 = bf16[16,16,2048]{2,1,0:T(8,128)(2,1)S(1)} async-done(((bf16[16,16,2048]{2,1,0:T(8,128)(2,1)}), bf16[16,16,2048]{2,1,0:T(8,128)(2,1)S(1)}, u32[]{:S(2)}, u32[]{:S(2)}) %all-to-all-start.7) | async-done | bytes 1048608 | tf_op jit(solution)/shard_map/all_to_all | solution.py:86
  (89 shorter events, 38.9 us)
Async XLA Ops:
  0.6 16.3 %copy-start = (bf16[2,32,2048]{2,1,0:T(8,128)(2,1)S(1)}, bf16[2,32,2048]{2,1,0:T(8,128)(2,1)}, u32[]{:S(2)}) copy-start(bf16[2,32,2048]{2,1,0:T(8,128)(2,1)} %param.8) | copy-start | bytes 786436
  0.6 16.3 %copy-start.1 = (bf16[32,2048]{1,0:T(8,128)(2,1)S(1)}, bf16[32,2048]{1,0:T(8,128)(2,1)}, u32[]{:S(2)}) copy-start(bf16[32,2048]{1,0:T(8,128)(2,1)} %param.9) | copy-start | bytes 393220
  4.1 39.7 %copy-start.3 = (bf16[1,2,32,6]{2,1,3,0:T(2,128)(2,1)S(1)}, bf16[1,2,32,6]{2,1,3,0:T(2,128)(2,1)}, u32[]{:S(2)}) copy-start(bf16[1,2,32,6]{2,1,3,0:T(2,128)(2,1)} %param.12) | copy-start | bytes 2308
  4.1 36.0 %all-to-all-start.2 = ((bf16[16,16,2048]{2,1,0:T(8,128)(2,1)}), bf16[16,16,2048]{2,1,0:T(8,128)(2,1)S(1)}, u32[]{:S(2)}, u32[]{:S(2)}) async-start(bf16[16,16,2048]{2,1,0:T(8,128)(2,1)} %bitcast.16), calls=%async_computation.2 | async-start | bytes 2097152 | tf_op jit(solution)/shard_map/all_to_all | solution.py:76
  12.5 87.7 %collective-permute-start.2 = (bf16[2048,704]{0,1:T(8,128)(2,1)}, bf16[2048,704]{0,1:T(8,128)(2,1)}, u32[]{:S(2)}, u32[]{:S(2)}) collective-permute-start(bf16[2048,704]{0,1:T(8,128)(2,1)} %bitcast.149), channel_id=1, source_target_pairs={{0,1},{1,0},{2,3},{3,2},{4,5},{5,4},{6,7},{7,6},{8,9},{9,8},{10,11... | collective-permute-start | bytes 8650760 | tf_op jit(solution)/shard_map/ppermute | solution.py:13
  14.5 147.6 %collective-permute-start.1 = (bf16[2048,704]{0,1:T(8,128)(2,1)}, bf16[2048,704]{0,1:T(8,128)(2,1)}, u32[]{:S(2)}, u32[]{:S(2)}) collective-permute-start(bf16[2048,704]{0,1:T(8,128)(2,1)} %bitcast.144), channel_id=1, source_target_pairs={{0,1},{1,0},{2,3},{3,2},{4,5},{5,4},{6,7},{7,6},{8,9},{9,8},{10,11... | collective-permute-start | bytes 8650760 | tf_op jit(solution)/shard_map/ppermute | solution.py:13
  14.6 219.8 %collective-permute-start = (bf16[704,2048]{1,0:T(8,128)(2,1)}, bf16[704,2048]{1,0:T(8,128)(2,1)}, u32[]{:S(2)}, u32[]{:S(2)}) collective-permute-start(bf16[704,2048]{1,0:T(8,128)(2,1)} %bitcast.141), channel_id=1, source_target_pairs={{0,1},{1,0},{2,3},{3,2},{4,5},{5,4},{6,7},{7,6},{8,9},{9,8},{10,11... | collective-permute-start | bytes 8650760 | tf_op jit(solution)/shard_map/ppermute | solution.py:13
  40.1 194.3 %all-to-all-start.1 = ((bf16[16,16,2048]{2,1,0:T(8,128)(2,1)}), bf16[16,16,2048]{2,1,0:T(8,128)(2,1)S(1)}, u32[]{:S(2)}, u32[]{:S(2)}) async-start(bf16[16,16,2048]{2,1,0:T(8,128)(2,1)} %bitcast.12), calls=%async_computation.1 | async-start | bytes 2097152 | tf_op jit(solution)/shard_map/all_to_all | solution.py:77
  100.2 61.8 %copy-start.4 = (bf16[1,1,2048,704]{2,3,1,0:T(8,128)(2,1)S(1)}, bf16[1,1,2048,704]{2,3,1,0:T(8,128)(2,1)}, u32[]{:S(2)}) copy-start(bf16[1,1,2048,704]{2,3,1,0:T(8,128)(2,1)} %param.14) | copy-start | bytes 8650756
  241.7 12.4 %all-to-all-start.8 = ((bf16[16,1,16]{2,1,0:T(2,128)(2,1)}), bf16[16,1,16]{2,1,0:T(2,128)(2,1)S(1)}, u32[]{:S(2)}, u32[]{:S(2)}) async-start(bf16[16,1,16]{2,1,0:T(2,128)(2,1)} %convert_element_type.308), calls=%async_computation.8 | async-start | bytes 16384 | tf_op jit(solution)/shard_map/all_to_all | solution.py:93
  264.5 5.1 %copy-start.6 = (bf16[1,1,2048,704]{2,3,1,0:T(8,128)(2,1)S(1)}, bf16[1,1,2048,704]{2,3,1,0:T(8,128)(2,1)}, u32[]{:S(2)}) copy-start(bf16[1,1,2048,704]{2,3,1,0:T(8,128)(2,1)} %param.13) | copy-start | bytes 8650756
  264.5 5.1 %copy-start.8 = (f32[256,1408]{1,0:T(8,128)S(1)}, f32[256,1408]{1,0:T(8,128)}, u32[]{:S(2)}) copy-start(f32[256,1408]{1,0:T(8,128)} %fusion.59) | copy-start | bytes 4325380
  264.5 5.2 %copy-start.9 = (f32[256,1408]{1,0:T(8,128)S(1)}, f32[256,1408]{1,0:T(8,128)}, u32[]{:S(2)}) copy-start(f32[256,1408]{1,0:T(8,128)} %fusion.61) | copy-start | bytes 4325380
  264.5 5.6 %copy-start.12 = (f32[256,1408]{1,0:T(8,128)S(1)}, f32[256,1408]{1,0:T(8,128)}, u32[]{:S(2)}) copy-start(f32[256,1408]{1,0:T(8,128)} %get-tuple-element.21) | copy-start | bytes 4325380
  270.2 8.7 %copy-start.2 = (bf16[1,2,32,2048]{3,2,1,0:T(8,128)(2,1)S(1)}, bf16[1,2,32,2048]{3,2,1,0:T(8,128)(2,1)}, u32[]{:S(2)}) copy-start(bf16[1,2,32,2048]{3,2,1,0:T(8,128)(2,1)} %param.10) | copy-start | bytes 786436
  275.2 27.3 %all-to-all-start.3 = ((bf16[16,16,2048]{2,1,0:T(8,128)(2,1)}), bf16[16,16,2048]{2,1,0:T(8,128)(2,1)S(1)}, u32[]{:S(2)}, u32[]{:S(2)}) async-start(bf16[16,16,2048]{2,1,0:T(8,128)(2,1)} %bitcast.20), calls=%async_computation.3 | async-start | bytes 2097152 | tf_op jit(solution)/shard_map/all_to_all | solution.py:86
  302.5 29.5 %all-to-all-start.6 = ((bf16[16,16,2048]{2,1,0:T(8,128)(2,1)}), bf16[16,16,2048]{2,1,0:T(8,128)(2,1)S(1)}, u32[]{:S(2)}, u32[]{:S(2)}) async-start(bf16[16,16,2048]{2,1,0:T(8,128)(2,1)} %bitcast.38), calls=%async_computation.6 | async-start | bytes 2097152 | tf_op jit(solution)/shard_map/all_to_all | solution.py:76
  306.5 3.2 collective-permute-start.3
  332.0 30.2 %all-to-all-start.5 = ((bf16[16,16,2048]{2,1,0:T(8,128)(2,1)}), bf16[16,16,2048]{2,1,0:T(8,128)(2,1)S(1)}, u32[]{:S(2)}, u32[]{:S(2)}) async-start(bf16[16,16,2048]{2,1,0:T(8,128)(2,1)} %bitcast.35), calls=%async_computation.5 | async-start | bytes 2097152 | tf_op jit(solution)/shard_map/all_to_all | solution.py:77
  335.9 5.8 %copy-start.5 = (bf16[1,1,2048,704]{2,3,1,0:T(8,128)(2,1)S(1)}, bf16[1,1,2048,704]{2,3,1,0:T(8,128)(2,1)}, u32[]{:S(2)}) copy-start(bf16[1,1,2048,704]{2,3,1,0:T(8,128)(2,1)} %param.14) | copy-start | bytes 8650756
  389.3 5.1 %copy-start.10 = (f32[256,1408]{1,0:T(8,128)S(1)}, f32[256,1408]{1,0:T(8,128)}, u32[]{:S(2)}) copy-start(f32[256,1408]{1,0:T(8,128)} %fusion.58) | copy-start | bytes 4325380
  389.3 5.2 %copy-start.11 = (f32[256,1408]{1,0:T(8,128)S(1)}, f32[256,1408]{1,0:T(8,128)}, u32[]{:S(2)}) copy-start(f32[256,1408]{1,0:T(8,128)} %fusion.60) | copy-start | bytes 4325380
  389.3 5.6 %copy-start.13 = (f32[256,1408]{1,0:T(8,128)S(1)}, f32[256,1408]{1,0:T(8,128)}, u32[]{:S(2)}) copy-start(f32[256,1408]{1,0:T(8,128)} %get-tuple-element.23) | copy-start | bytes 4325380
  399.9 28.9 %all-to-all-start.7 = ((bf16[16,16,2048]{2,1,0:T(8,128)(2,1)}), bf16[16,16,2048]{2,1,0:T(8,128)(2,1)S(1)}, u32[]{:S(2)}, u32[]{:S(2)}) async-start(bf16[16,16,2048]{2,1,0:T(8,128)(2,1)} %bitcast.40), calls=%async_computation.7 | async-start | bytes 2097152 | tf_op jit(solution)/shard_map/all_to_all | solution.py:86
  (1 other events, 5.1 us)
where the time goes:
time: 431 us; the launch traced here: 430 us
  waiting for transfers between devices  294 us (68%)
  matrix products  62.3 us (14%)
  starting transfers between devices  37.3 us (9%)
  blocking collectives  29.6 us (7%)
    ppermute x3, waiting for transfers between devices, swapped(): return lax.ppermute(value, axis, pairs)  112 us
    all_to_all x2, waiting for transfers between devices, layer_backward(): lax.all_to_all(sent_grads, ('group', 'local'), split_axis=0, concat_axis=...  83.3 us
    all_to_all x2, waiting for transfers between devices, layer_backward(): lax.all_to_all(kept_grad.astype(jnp.bfloat16), ('group', 'local'), split_...  46.8 us
    all_to_all x2, waiting for transfers between devices, layer_backward(): lax.all_to_all(sent_inputs, ('group', 'local'), split_axis=0, concat_axis...  42.7 us
    all_to_all x2, blocking collectives, layer_backward(): lax.all_to_all(sent_probs, ('group', 'local'), split_axis=0, concat_axis=...  19.7 us
    dot_general x2, matrix products, expert_backward(): lax.dot_general(rows_grad, down_full, CONTRACT_LAST, preferred_element_ty...  13.1 us
    all_to_all x2, starting transfers between devices, layer_backward(): lax.all_to_all(sent_inputs, ('group', 'local'), split_axis=0, concat_axis...  12.1 us
    dot_general x2, matrix products, expert_backward(): gate_pre = jnp.dot(rows_in, gate_full, preferred_element_type=jnp.float32)  11.5 us
  transfers between devices with their start and end apart: 11, of which 10 were waited for; matrix products, arithmetic and copies ran while one was open for 6% of the time, Pallas kernels for 0%

commit v1 on v0

--- a/solution.py
+++ b/solution.py
@@ -1,6 +1,10 @@
+import functools
+
 import jax
 import jax.numpy as jnp
 from jax import lax
+from jax.experimental import pallas as pl
+from jax.experimental.pallas import tpu as pltpu
 from jax.sharding import PartitionSpec as P
 
 CONTRACT_LAST = (((1,), (1,)), ((), ()))
@@ -46,7 +50,9 @@
     expert_range = jnp.arange(expert_count, dtype=jnp.int32)
     matches = (choice_ids[:, :, None] == expert_range[None, None, :]).astype(jnp.int32)
     chosen = jnp.sum(matches, axis=1)
-    before = jnp.cumsum(chosen, axis=0) - chosen
+    rows = jnp.arange(choice_ids.shape[0])
+    earlier = (rows[:, None] > rows[None, :]).astype(jnp.float32)
+    before = jnp.dot(earlier, chosen.astype(jnp.float32)).astype(jnp.int32)
     slot_range = jnp.arange(capacity, dtype=jnp.int32)
     placed = (before[:, :, None] == slot_range[None, None, :]) & (chosen[:, :, None] > 0)
     slot_map = jnp.transpose(placed, (1, 2, 0)).astype(jnp.float32)
@@ -109,7 +115,7 @@
     return (summed.astype(jnp.bfloat16), gate_values.astype(jnp.bfloat16))
 
 
-def local(
+def routed_local(
     output_grad,
     carried_grad,
     layer_inputs,
@@ -154,6 +160,297 @@
     return (jnp.stack(grads_out)[None], jnp.stack(gates_out)[None])
 
 
+VMEM_LIMIT = 56 * 2**20
+HIDDEN_TILE = 256
+WIDTH_TILE = 256
+
+
+def tiles(total, step):
+    return [(start, min(step, total - start)) for start in range(0, total, step)]
+
+
+def load_pieces(pieces, target, sems):
+    copies = []
+    for number, (ref, begin, rows, place) in enumerate(pieces):
+        copy = pltpu.make_async_copy(
+            ref.at[pl.ds(begin, rows)], target.at[pl.ds(place, rows)], sems.at[number]
+        )
+        copy.start()
+        copies.append(copy)
+    for copy in copies:
+        copy.wait()
+
+
+def forward_kernel(plan, *refs):
+    count = len(plan)
+    piece_refs = refs[:count]
+    probs_ref, gate_ref, up_ref, product_ref, gate_factor_ref, up_factor_ref, rows_ref, sems = refs[
+        count:
+    ]
+    load_pieces(
+        [(ref,) + place for ref, place in zip(piece_refs, plan)], rows_ref, sems
+    )
+    rows = rows_ref[...]
+    probs = probs_ref[...]
+    for start, size in tiles(gate_ref.shape[1], HIDDEN_TILE):
+        columns = pl.ds(start, size)
+        gate_pre = jnp.dot(rows, gate_ref[:, columns], preferred_element_type=jnp.float32)
+        up_pre = jnp.dot(rows, up_ref[:, columns], preferred_element_type=jnp.float32)
+        sigmoid_gate = jax.nn.sigmoid(gate_pre)
+        activated = gate_pre * sigmoid_gate
+        product_ref[:, columns] = activated * up_pre
+        up_factor_ref[:, columns] = probs * activated
+        gate_factor_ref[:, columns] = (
+            probs * up_pre * sigmoid_gate * (1.0 + gate_pre * (1.0 - sigmoid_gate))
+        )
+
+
+def backward_kernel(plan, blocks, *refs):
+    count = len(plan)
+    piece_refs = refs[:count]
+    product_ref, gate_factor_ref, up_factor_ref, gate_ref, up_ref, down_ref = refs[count : count + 6]
+    out_refs = refs[count + 6 : count + 6 + len(blocks)]
+    part_ref, rows_ref, grad_gate_ref, grad_up_ref, sems = refs[count + 6 + len(blocks) :]
+    load_pieces(
+        [(ref,) + place for ref, place in zip(piece_refs, plan)], rows_ref, sems
+    )
+    rows = rows_ref[...]
+    part = jnp.zeros(part_ref.shape, jnp.float32)
+    for start, size in tiles(down_ref.shape[0], HIDDEN_TILE):
+        columns = pl.ds(start, size)
+        back_proj = lax.dot_general(
+            rows, down_ref[columns, :], CONTRACT_LAST, preferred_element_type=jnp.float32
+        )
+        part = part + jnp.sum(product_ref[:, columns] * back_proj, axis=1, keepdims=True)
+        grad_gate_ref[:, columns] = (gate_factor_ref[:, columns] * back_proj).astype(jnp.bfloat16)
+        grad_up_ref[:, columns] = (up_factor_ref[:, columns] * back_proj).astype(jnp.bfloat16)
+    part_ref[...] = part
+    grad_gate = grad_gate_ref[...]
+    grad_up = grad_up_ref[...]
+    for start, size in tiles(gate_ref.shape[0], WIDTH_TILE):
+        columns = pl.ds(start, size)
+        grads = lax.dot_general(
+            grad_gate, gate_ref[columns, :], CONTRACT_LAST, preferred_element_type=jnp.float32
+        )
+        grads = grads + lax.dot_general(
+            grad_up, up_ref[columns, :], CONTRACT_LAST, preferred_element_type=jnp.float32
+        )
+        grads = grads.astype(jnp.bfloat16)
+        for out_ref, (place, amount) in zip(out_refs, blocks):
+            out_ref[:, columns] = grads[place : place + amount]
+
+
+ANYWHERE = pl.BlockSpec(memory_space=pl.ANY)
+IN_VMEM = pl.BlockSpec(memory_space=pltpu.VMEM)
+
+
+def forward_part(pieces, plan, probs, gate_half, up_half):
+    rows = probs.shape[0]
+    width, hidden = gate_half.shape
+    factor = jax.ShapeDtypeStruct((rows, hidden), jnp.float32)
+    return pl.pallas_call(
+        functools.partial(forward_kernel, plan),
+        out_shape=(factor, factor, factor),
+        in_specs=[ANYWHERE] * len(pieces) + [IN_VMEM] * 3,
+        out_specs=(IN_VMEM,) * 3,
+        scratch_shapes=[
+            pltpu.VMEM((rows, width), jnp.bfloat16),
+            pltpu.SemaphoreType.DMA((len(pieces),)),
+        ],
+        compiler_params=pltpu.CompilerParams(vmem_limit_bytes=VMEM_LIMIT),
+        cost_estimate=pl.CostEstimate(
+            flops=4 * rows * width * hidden,
+            bytes_accessed=4 * width * hidden + 2 * rows * width + 12 * rows * hidden,
+            transcendentals=rows * hidden,
+        ),
+        name="forward_part",
+    )(*pieces, probs, gate_half, up_half)
+
+
+def backward_part(pieces, plan, blocks, factors, gate_half, up_half, down_half):
+    rows = factors[0].shape[0]
+    width, hidden = gate_half.shape
+    outs = [jax.ShapeDtypeStruct((amount, width), jnp.bfloat16) for _, amount in blocks]
+    outs.append(jax.ShapeDtypeStruct((rows, 1), jnp.float32))
+    return pl.pallas_call(
+        functools.partial(backward_kernel, plan, blocks),
+        out_shape=tuple(outs),
+        in_specs=[ANYWHERE] * len(pieces) + [IN_VMEM] * 6,
+        out_specs=(IN_VMEM,) * len(outs),
+        scratch_shapes=[
+            pltpu.VMEM((rows, width), jnp.bfloat16),
+            pltpu.VMEM((rows, hidden), jnp.bfloat16),
+            pltpu.VMEM((rows, hidden), jnp.bfloat16),
+            pltpu.SemaphoreType.DMA((len(pieces),)),
+        ],
+        compiler_params=pltpu.CompilerParams(vmem_limit_bytes=VMEM_LIMIT),
+        cost_estimate=pl.CostEstimate(
+            flops=6 * rows * width * hidden,
+            bytes_accessed=6 * width * hidden + 4 * rows * width + 12 * rows * hidden,
+            transcendentals=0,
+        ),
+        name="backward_part",
+    )(*pieces, *factors, gate_half, up_half, down_half)
+
+
+def toggled(value, axis, mask):
+    pairs = [(source, source ^ mask) for source in range(lax.axis_size(axis))]
+    return lax.ppermute(value, axis, pairs)
+
+
+def spread(block):
+    near = toggled(block, "local", 1)
+    far = toggled(block, "local", 2)
+    corner = toggled(far, "local", 1)
+    half = block.shape[0] // 2
+    found = []
+    for column in (block, near, far, corner):
+        first = toggled(column, "group", 1)
+        second = toggled(column, "group", 2)
+        low = toggled(first[:half], "group", 2)
+        high = toggled(second[half:], "group", 1)
+        found.append((column, first, second, low, high))
+    return found
+
+
+def piece_plan(found, begin, rows):
+    half = found[0][0].shape[0] // 2
+    arrays, plan = [], []
+    for level, (column, first, second, low, high) in enumerate(found):
+        for slot, array in ((0, column), (1, first), (2, second)):
+            arrays.append(array)
+            plan.append((begin, rows, (4 * slot + level) * rows))
+        place = (12 + level) * rows
+        upto = min(half, begin + rows)
+        if begin < upto:
+            arrays.append(low)
+            plan.append((begin, upto - begin, place))
+        since = max(half, begin)
+        if since < begin + rows:
+            arrays.append(high)
+            plan.append((since - half, begin + rows - since, place + since - begin))
+    return arrays, tuple(plan)
+
+
+def added(*values):
+    total = values[0].astype(jnp.float32)
+    for value in values[1:]:
+        total = total + value.astype(jnp.float32)
+    return total
+
+
+def brought_back(blocks, incoming):
+    diag_low, diag_high, first_low, first_high, second_low, second_high, own = blocks
+    rows = incoming.shape[0]
+    got_low = toggled(diag_low, "group", 1)
+    got_high = toggled(diag_high, "group", 2)
+    from_second_high = toggled(second_high, "group", 2)
+    from_first_low = toggled(first_low, "group", 1)
+    from_first_high = toggled(added(first_high, got_high).astype(jnp.bfloat16), "group", 1)
+    from_second_low = toggled(added(second_low, got_low).astype(jnp.bfloat16), "group", 2)
+    high = added(own[2 * rows :], from_first_high, from_second_high)
+    low = added(own[: 2 * rows], from_first_low, from_second_low)
+    got_corner = toggled(high[rows:].astype(jnp.bfloat16), "local", 1)
+    got_far = toggled(added(high[:rows], got_corner).astype(jnp.bfloat16), "local", 2)
+    got_near = toggled(low[rows:].astype(jnp.bfloat16), "local", 1)
+    return added(incoming, low[:rows], got_near, got_far).astype(jnp.bfloat16)
+
+
+def by_difference(values):
+    own = lax.axis_index("group") * lax.axis_size("local") + lax.axis_index("local")
+    count = values.shape[0]
+    bit = 1
+    while bit < count:
+        split = values.reshape((count // (2 * bit), 2, bit) + values.shape[1:])
+        flipped = split[:, ::-1].reshape(values.shape)
+        values = jnp.where((own & bit) != 0, flipped, values)
+        bit *= 2
+    return values
+
+
+def dense_local(
+    output_grad,
+    carried_grad,
+    layer_inputs,
+    expert_ids,
+    gate_prob,
+    gate_weight,
+    up_weight,
+    down_weight,
+):
+    devices = lax.axis_size("group") * lax.axis_size("local")
+    expert_count = devices // 2
+    micro_count, rows = output_grad.shape[:2]
+    gate_half, up_half, down_half = gate_weight[0, 0], up_weight[0, 0], down_weight[0, 0]
+    everywhere = ("group", "local")
+    experts = jnp.arange(expert_count, dtype=jnp.int32)
+    matches = (expert_ids[0][..., None] == experts).astype(jnp.float32)
+    token_probs = jnp.sum(matches * gate_prob[0].astype(jnp.float32)[..., None], axis=2)
+    sent_probs = jnp.repeat(
+        jnp.transpose(token_probs, (2, 0, 1)).reshape(expert_count, micro_count * rows), 2, axis=0
+    )
+    got_probs = lax.all_to_all(
+        sent_probs.astype(jnp.bfloat16), everywhere, split_axis=0, concat_axis=0, tiled=True
+    )
+    got_probs = by_difference(got_probs.astype(jnp.float32)).reshape(devices, micro_count, rows)
+    slot_probs = [got_probs[:, m].reshape(devices * rows, 1) for m in range(micro_count)]
+    last_section = lax.axis_index("pipe") == lax.axis_size("pipe") - 1
+    inputs = layer_inputs[0]
+    quarter = 4 * rows
+    blocks = (
+        (3 * quarter, 2 * rows),
+        (3 * quarter + 2 * rows, 2 * rows),
+        (quarter, 2 * rows),
+        (quarter + 2 * rows, 2 * rows),
+        (2 * quarter, 2 * rows),
+        (2 * quarter + 2 * rows, 2 * rows),
+        (0, quarter),
+    )
+    incoming = jnp.where(last_section, output_grad[0], carried_grad)
+    found = spread(jnp.concatenate([inputs[0], incoming], axis=0))
+    factors = []
+    grads_pieces = piece_plan(found, rows, rows)
+    arrays, plan = piece_plan(found, 0, rows)
+    factors.append(forward_part(arrays, plan, slot_probs[0], gate_half, up_half))
+    later = inputs[1:]
+    found[-1], later = lax.optimization_barrier((found[-1], later))
+    for m in range(1, micro_count):
+        arrays, plan = piece_plan(spread(later[m - 1]), 0, rows)
+        factors.append(forward_part(arrays, plan, slot_probs[m], gate_half, up_half))
+    grads_out, parts = [], []
+    for m in range(micro_count):
+        if m > 0:
+            earlier = from_behind(grads_out[-1], "pipe", -1)
+            incoming = jnp.where(last_section, output_grad[m], earlier)
+            grads_pieces = piece_plan(spread(incoming), 0, rows)
+        *pieces, part = backward_part(
+            *grads_pieces, blocks, factors[m], gate_half, up_half, down_half
+        )
+        grads_out.append(brought_back(pieces, incoming))
+        parts.append(
+            lax.all_to_all(
+                by_difference(part.reshape(devices, rows)),
+                everywhere,
+                split_axis=0,
+                concat_axis=0,
+                tiled=True,
+            )
+        )
+    per_expert = jnp.stack(parts).reshape(micro_count, expert_count, 2, rows).sum(axis=2)
+    gates = jnp.sum(matches * jnp.transpose(per_expert, (0, 2, 1))[:, :, None, :], axis=3)
+    return (jnp.stack(grads_out)[None], gates.astype(jnp.bfloat16)[None])
+
+
+def local(*arguments):
+    group, ring = lax.axis_size("group"), lax.axis_size("local")
+    top_count = arguments[3].shape[-1]
+    expert_count = group * ring // 2
+    crowded = 3 * expert_count <= 4 * top_count
+    if group == 4 and ring == 4 and crowded:
+        return dense_local(*arguments)
+    return routed_local(*arguments)
+
+
 def solution(mesh):
     return jax.shard_map(
         local,

time: 431 us -> 235 us (0.55)
  waiting for transfers between devices: 294 us -> 49.1 us
  matrix products: 62.3 us -> 0 us
  starting transfers between devices: 37.3 us -> 96.2 us
  Pallas kernels: 0 us -> 49.7 us
  blocking collectives: 29.6 us -> 11.6 us
  local copies, waits for them, and re-layouts: 4.14 us -> 17.3 us
  other arithmetic: 1.27 us -> 9.1 us
    all_to_all x7 -> x2, waiting for transfers between devices: 180 us -> 0.01 us  [the longest x1 0.01 us: dense_local(): lax.all_to_all(sent_probs.astype(jnp.bfloat16), everywhere, split_axis=0,...]
    ppermute x3 -> x75, starting transfers between devices: 3.95 us -> 85.5 us  [toggled(): return lax.ppermute(value, axis, pairs)]
    ppermute x3 -> x75, waiting for transfers between devices: 112 us -> 49 us  [toggled(): return lax.ppermute(value, axis, pairs)]
    dot_general x20 -> x0, matrix products: 62.3 us -> none  [the longest x2 13.1 us: expert_backward(): lax.dot_general(rows_grad, down_full, CONTRACT_LAST, preferred_element_ty...]
    pallas_call x0 -> x4, Pallas kernels: none -> 49.7 us  [the longest x2 29.1 us: backward_part(): pl.pallas_call(functools.partial(backward_kernel, plan, blocks), out_shap...]
    all_to_all x7 -> x2, starting transfers between devices: 32 us -> 9.24 us  [the longest x1 4.84 us: dense_local(): lax.all_to_all(sent_probs.astype(jnp.bfloat16), everywhere, split_axis=0,...]
    all_to_all x3 -> x1, blocking collectives: 29.6 us -> 11.6 us  [dense_local(): lax.all_to_all(by_difference(part.reshape(devices, rows)), everywhere, sp...]
    unnamed x29 -> x109, local copies, waits for them, and re-layouts: 1.7 us -> 9.73 us
  transfers between devices with their start and end apart: 11 -> 78, of which waited for: 10 -> 27; matrix products, arithmetic and copies ran while one was open for 6% -> 9% of each run, Pallas kernels for 0% -> 9%
where the time goes in v1:
time: 235 us
  starting transfers between devices  96.2 us (41%)
  Pallas kernels  49.7 us (21%)
  waiting for transfers between devices  49.1 us (21%)
  local copies, waits for them, and re-layouts  17.3 us (7%)
  blocking collectives  11.6 us (5%)
  other arithmetic  9.1 us (4%)
    ppermute x75, starting transfers between devices, toggled(): return lax.ppermute(value, axis, pairs)  85.5 us
    ppermute x75, waiting for transfers between devices, toggled(): return lax.ppermute(value, axis, pairs)  49 us
    pallas_call x2, Pallas kernels, backward_part(): pl.pallas_call(functools.partial(backward_kernel, plan, blocks), out_shap...  29.1 us
    pallas_call x2, Pallas kernels, forward_part(): pl.pallas_call(functools.partial(forward_kernel, plan), out_shape=(factor...  20.6 us
    all_to_all x1, blocking collectives, dense_local(): lax.all_to_all(by_difference(part.reshape(devices, rows)), everywhere, sp...  11.6 us
    unnamed x109, local copies, waits for them, and re-layouts  9.73 us
    all_to_all x1, starting transfers between devices, dense_local(): lax.all_to_all(sent_probs.astype(jnp.bfloat16), everywhere, split_axis=0,...  4.84 us
  transfers between devices with their start and end apart: 78, of which 27 were waited for; matrix products, arithmetic and copies ran while one was open for 9% of the time, Pallas kernels for 9%

profile of v1, /device:TPU:0, one launch (start us, length us, event | category | flops | bytes accessed | tf_op | source)
XLA Modules:
  0.0 234.6 jit_solution(5696130945803570778)
XLA Ops:
  3.3 4.1 %collective-permute-start.7 = (bf16[64,2048]{1,0:T(8,128)(2,1)S(1)}, bf16[64,2048]{1,0:T(8,128)(2,1)}, u32[]{:S(2)}, u32[]{:S(2)}) collective-permute-start(bf16[64,2048]{1,0:T(8,128)(2,1)S(1)} %pad_maximum_fusion.refs_0_), channel_id=1, source_target_pairs={{0,2},{1,3},{2,0},{3,1},{4,6},{5,7},{6,4},{7,5},{8,10},{9,11},{10,... | collective-permute-start | bytes 786440 | tf_op jit(solution)/shard_map/ppermute | solution.py:298
  9.5 4.8 %all-to-all-start = ((bf16[16,1,64]{2,1,0:T(2,128)(2,1)}), bf16[16,1,64]{2,1,0:T(2,128)(2,1)S(1)}, u32[]{:S(2)}, u32[]{:S(2)}) async-start(bf16[16,1,64]{2,1,0:T(2,128)(2,1)} %copy.52), calls=%async_computation | async-start | bytes 16384 | tf_op jit(solution)/shard_map/all_to_all | solution.py:392
  19.2 4.7 %copy.53 = bf16[1,1,2048,704]{3,2,1,0:T(8,128)(2,1)} copy(bf16[1,1,2048,704]{2,3,1,0:T(8,128)(2,1)} %param.13) | data formatting | bytes 5767168 | tf_op args[5]
  24.0 2.8 %copy.54 = bf16[1,1,2048,704]{3,2,1,0:T(8,128)(2,1)} copy(bf16[1,1,2048,704]{2,3,1,0:T(8,128)(2,1)S(1)} %copy-done) | data formatting | bytes 5767168 | tf_op args[6]
  30.4 3.1 %collective-permute-done.11.refs_12_ = bf16[64,2048]{1,0:T(8,128)(2,1)S(1)} collective-permute-done((bf16[64,2048]{1,0:T(8,128)(2,1)}, bf16[64,2048]{1,0:T(8,128)(2,1)S(1)}, u32[]{:S(2)}, u32[]{:S(2)}) %collective-permute-start.11) | collective-permute-done | bytes 262176 | tf_op jit(solution)/shard_map/ppermute | solution.py:298
  34.0 2.9 %collective-permute-done.8.refs_9_ = bf16[64,2048]{1,0:T(8,128)(2,1)S(1)} collective-permute-done((bf16[64,2048]{1,0:T(8,128)(2,1)}, bf16[64,2048]{1,0:T(8,128)(2,1)S(1)}, u32[]{:S(2)}, u32[]{:S(2)}) %collective-permute-start.8) | collective-permute-done | bytes 262176 | tf_op jit(solution)/shard_map/ppermute | solution.py:298
  37.7 4.4 %collective-permute-done.4.refs_5_ = bf16[64,2048]{1,0:T(8,128)(2,1)S(1)} collective-permute-done((bf16[64,2048]{1,0:T(8,128)(2,1)}, bf16[64,2048]{1,0:T(8,128)(2,1)S(1)}, u32[]{:S(2)}, u32[]{:S(2)}) %collective-permute-start.4) | collective-permute-done | bytes 262176 | tf_op jit(solution)/shard_map/ppermute | solution.py:298
  42.7 2.2 collective-permute-done.12.refs_13_
  51.1 7.4 %collective-permute-done.13.refs_14_ = bf16[64,2048]{1,0:T(8,128)(2,1)S(1)} collective-permute-done((bf16[64,2048]{1,0:T(8,128)(2,1)S(1)}, bf16[64,2048]{1,0:T(8,128)(2,1)S(1)}, u32[]{:S(2)}, u32[]{:S(2)}) %collective-permute-start.13) | collective-permute-done | bytes 262176 | tf_op jit(solution)/shard_map/ppermute | solution.py:298
  62.7 10.3 %forward_part.2 = (f32[512,704]{1,0:T(8,128)}, f32[512,704]{1,0:T(8,128)}, f32[512,704]{1,0:T(8,128)}) custom-call(bf16[64,2048]{1,0:T(8,128)(2,1)} %copy-done.1, bf16[64,2048]{1,0:T(8,128)(2,1)} %copy-done.2, bf16[64,2048]{1,0:T(8,128)(2,1)} %collective-permute-done.1.refs_2_, bf16[32,2048]{1,0:T(8,128)(2,1)} %collective-permute-done.15.refs_3_, ...), custom_call_target="tpu_custom_call" | custom-call | flops 2952790016 | bytes 12189696 | tf_op jit(solution)/shard_map/forward_part/pallas_call | solution.py:251
  73.8 14.6 %backward_part.2 = (bf16[64,2048]{1,0:T(8,128)(2,1)}, bf16[64,2048]{1,0:T(8,128)(2,1)}, bf16[64,2048]{1,0:T(8,128)(2,1)}, bf16[64,2048]{1,0:T(8,128)(2,1)}, bf16...) custom-call(bf16[64,2048]{1,0:T(8,128)(2,1)} %copy-done.1, ...), custom_call_target="tpu_custom_call" | custom-call | flops 4429185024 | bytes 17170432 | tf_op jit(solution)/shard_map/backward_part/pallas_call | solution.py:275
  92.5 3.7 %collective-permute-done.20 = bf16[64,2048]{1,0:T(8,128)(2,1)S(1)} collective-permute-done((bf16[64,2048]{1,0:T(8,128)(2,1)}, bf16[64,2048]{1,0:T(8,128)(2,1)S(1)}, u32[]{:S(2)}, u32[]{:S(2)}) %collective-permute-start.20) | collective-permute-done | bytes 262176 | tf_op jit(solution)/shard_map/ppermute | solution.py:298
  100.9 2.8 %collective-permute-done.21 = bf16[64,2048]{1,0:T(8,128)(2,1)S(1)} collective-permute-done((bf16[64,2048]{1,0:T(8,128)(2,1)S(1)}, bf16[64,2048]{1,0:T(8,128)(2,1)S(1)}, u32[]{:S(2)}, u32[]{:S(2)}) %collective-permute-start.21) | collective-permute-done | bytes 262176 | tf_op jit(solution)/shard_map/ppermute | solution.py:298
  107.3 2.4 %collective-permute-start.57 = (bf16[32,2048]{1,0:T(8,128)(2,1)S(1)}, bf16[32,2048]{1,0:T(8,128)(2,1)S(1)}, u32[]{:S(2)}, u32[]{:S(2)}) collective-permute-start(bf16[32,2048]{1,0:T(8,128)(2,1)S(1)} %bitcast.122), channel_id=1, source_target_pairs={{0,2},{1,3},{2,0},{3,1},{4,6},{5,7},{6,4},{7,5},{8,10},{9,11},{10,... | collective-permute-start | bytes 393224 | tf_op jit(solution)/shard_map/ppermute | solution.py:298
  110.3 3.2 %collective-permute-done.26 = bf16[32,2048]{1,0:T(8,128)(2,1)S(1)} collective-permute-done((bf16[32,2048]{1,0:T(8,128)(2,1)S(1)}, bf16[32,2048]{1,0:T(8,128)(2,1)S(1)}, u32[]{:S(2)}, u32[]{:S(2)}) %collective-permute-start.26) | collective-permute-done | bytes 131104 | tf_op jit(solution)/shard_map/ppermute | solution.py:298
  114.9 2.5 %collective-permute-start.52 = (bf16[32,2048]{1,0:T(8,128)(2,1)S(1)}, bf16[32,2048]{1,0:T(8,128)(2,1)S(1)}, u32[]{:S(2)}, u32[]{:S(2)}) collective-permute-start(bf16[32,2048]{1,0:T(8,128)(2,1)S(1)} %bitcast.123), channel_id=1, source_target_pairs={{0,1},{1,0},{2,3},{3,2},{4,5},{5,4},{6,7},{7,6},{8,9},{9,8},{10,11... | collective-permute-start | bytes 393224 | tf_op jit(solution)/shard_map/ppermute | solution.py:298
  137.9 2.6 %collective-permute-done.55.refs_8_ = bf16[16,2048]{1,0:T(8,128)(2,1)S(1)} collective-permute-done((bf16[16,2048]{1,0:T(8,128)(2,1)S(1)}, bf16[16,2048]{1,0:T(8,128)(2,1)S(1)}, u32[]{:S(2)}, u32[]{:S(2)}) %collective-permute-start.55) | collective-permute-done | bytes 65568 | tf_op jit(solution)/shard_map/ppermute | solution.py:298
  165.0 10.3 %forward_part.3 = (f32[512,704]{1,0:T(8,128)}, f32[512,704]{1,0:T(8,128)}, f32[512,704]{1,0:T(8,128)}) custom-call(bf16[32,2048]{1,0:T(8,128)(2,1)} %bitcast.121, bf16[32,2048]{1,0:T(8,128)(2,1)} %copy-done.21, bf16[32,2048]{1,0:T(8,128)(2,1)} %copy-done.22, bf16[16,2048]{1,0:T(8,128)(2,1)} %copy-done.42, bf16[16,2048]{1,0:T(8,128)(2,1)} %copy-done.43, ...), custom_call_target="tpu_custom_call" | custom-call | flops 2952790016 | bytes 12189696 | tf_op jit(solution)/shard_map/forward_part/pallas_call | solution.py:251
  176.2 14.5 %backward_part.3 = (bf16[64,2048]{1,0:T(8,128)(2,1)}, bf16[64,2048]{1,0:T(8,128)(2,1)}, bf16[64,2048]{1,0:T(8,128)(2,1)}, bf16[64,2048]{1,0:T(8,128)(2,1)}, bf16...) custom-call(bf16[32,2048]{1,0:T(8,128)(2,1)} %copy-done.11, ...), custom_call_target="tpu_custom_call" | custom-call | flops 4429185024 | bytes 17170432 | tf_op jit(solution)/shard_map/backward_part/pallas_call | solution.py:275
  192.6 4.4 %all-to-all-start.1 = ((f32[16,1,32]{2,1,0:T(1,128)}), f32[16,1,32]{2,1,0:T(1,128)S(1)}, u32[]{:S(2)}, u32[]{:S(2)}) async-start(f32[16,1,32]{2,1,0:T(1,128)} %bitcast.35), calls=%async_computation.1 | async-start | bytes 16384 | tf_op jit(solution)/shard_map/all_to_all | solution.py:431
  209.1 2.6 %collective-permute-done.72 = bf16[64,2048]{1,0:T(8,128)(2,1)S(1)} collective-permute-done((bf16[64,2048]{1,0:T(8,128)(2,1)S(1)}, bf16[64,2048]{1,0:T(8,128)(2,1)S(1)}, u32[]{:S(2)}, u32[]{:S(2)}) %collective-permute-start.72) | collective-permute-done | bytes 262176 | tf_op jit(solution)/shard_map/ppermute | solution.py:298
  215.9 2.9 %collective-permute-done.74 = bf16[32,2048]{1,0:T(8,128)(2,1)S(1)} collective-permute-done((bf16[32,2048]{1,0:T(8,128)(2,1)S(1)}, bf16[32,2048]{1,0:T(8,128)(2,1)S(1)}, u32[]{:S(2)}, u32[]{:S(2)}) %collective-permute-start.74) | collective-permute-done | bytes 131104 | tf_op jit(solution)/shard_map/ppermute | solution.py:298
  218.8 2.6 %collective-permute-start.75 = (bf16[32,2048]{1,0:T(8,128)(2,1)S(1)}, bf16[32,2048]{1,0:T(8,128)(2,1)S(1)}, u32[]{:S(2)}, u32[]{:S(2)}) collective-permute-start(bf16[32,2048]{1,0:T(8,128)(2,1)S(1)} %fusion), channel_id=1, source_target_pairs={{0,2},{1,3},{2,0},{3,1},{4,6},{5,7},{6,4},{7,5},{8,10},{9,11},{10,... | collective-permute-start | bytes 393224 | tf_op jit(solution)/shard_map/ppermute | solution.py:298
  221.5 11.6 %all_to_all.18 = f32[16,1,32]{2,1,0:T(1,128)S(1)} all-to-all(f32[16,1,32]{2,1,0:T(1,128)S(1)} %bitcast.138), channel_id=1, replica_groups=mesh['pipe'=2,'group'=4,'local'=4] {'group','local'}, dimensions={0} | all-to-all | bytes 4096 | tf_op jit(solution)/shard_map/all_to_all | solution.py:431
  (343 shorter events, 105.6 us)
Async XLA Ops:
  3.3 23.5 %collective-permute-start.7 = (bf16[64,2048]{1,0:T(8,128)(2,1)S(1)}, bf16[64,2048]{1,0:T(8,128)(2,1)}, u32[]{:S(2)}, u32[]{:S(2)}) collective-permute-start(bf16[64,2048]{1,0:T(8,128)(2,1)S(1)} %pad_maximum_fusion.refs_0_), channel_id=1, source_target_pairs={{0,2},{1,3},{2,0},{3,1},{4,6},{5,7},{6,4},{7,5},{8,10},{9,11},{10,... | collective-permute-start | bytes 786440 | tf_op jit(solution)/shard_map/ppermute | solution.py:298
  9.5 17.2 %all-to-all-start = ((bf16[16,1,64]{2,1,0:T(2,128)(2,1)}), bf16[16,1,64]{2,1,0:T(2,128)(2,1)S(1)}, u32[]{:S(2)}, u32[]{:S(2)}) async-start(bf16[16,1,64]{2,1,0:T(2,128)(2,1)} %copy.52), calls=%async_computation | async-start | bytes 16384 | tf_op jit(solution)/shard_map/all_to_all | solution.py:392
  14.4 13.9 %collective-permute-start.3 = (bf16[64,2048]{1,0:T(8,128)(2,1)S(1)}, bf16[64,2048]{1,0:T(8,128)(2,1)}, u32[]{:S(2)}, u32[]{:S(2)}) collective-permute-start(bf16[64,2048]{1,0:T(8,128)(2,1)S(1)} %pad_maximum_fusion.refs_0_), channel_id=1, source_target_pairs={{0,1},{1,0},{2,3},{3,2},{4,5},{5,4},{6,7},{7,6},{8,9},{9,8},{10,11... | collective-permute-start | bytes 786440 | tf_op jit(solution)/shard_map/ppermute | solution.py:298
  16.3 12.2 %collective-permute-start = (bf16[64,2048]{1,0:T(8,128)(2,1)S(1)}, bf16[64,2048]{1,0:T(8,128)(2,1)S(1)}, u32[]{:S(2)}, u32[]{:S(2)}) collective-permute-start(bf16[64,2048]{1,0:T(8,128)(2,1)S(1)} %pad_maximum_fusion.refs_0_), channel_id=1, source_target_pairs={{0,4},{4,0},{8,12},{12,8},{1,5},{5,1},{9,13},{13,9},{2,6},{6,2},{1... | collective-permute-start | bytes 786440 | tf_op jit(solution)/shard_map/ppermute | solution.py:298
  17.8 27.7 %collective-permute-start.1 = (bf16[64,2048]{1,0:T(8,128)(2,1)S(1)}, bf16[64,2048]{1,0:T(8,128)(2,1)}, u32[]{:S(2)}, u32[]{:S(2)}) collective-permute-start(bf16[64,2048]{1,0:T(8,128)(2,1)S(1)} %pad_maximum_fusion.refs_0_), channel_id=1, source_target_pairs={{0,8},{4,12},{8,0},{12,4},{1,9},{5,13},{9,1},{13,5},{2,10},{6,14},... | collective-permute-start | bytes 786440 | tf_op jit(solution)/shard_map/ppermute | solution.py:298
  28.3 18.7 %collective-permute-start.9 = (bf16[64,2048]{1,0:T(8,128)(2,1)}, bf16[64,2048]{1,0:T(8,128)(2,1)S(1)}, u32[]{:S(2)}, u32[]{:S(2)}) collective-permute-start(bf16[64,2048]{1,0:T(8,128)(2,1)} %collective-permute-done.7.refs_8_), channel_id=1, source_target_pairs={{0,8},{4,12},{8,0},{12,4},{1,9},{5,13},{9,1},{13,5},{2,10},{6,14},... | collective-permute-start | bytes 786440 | tf_op jit(solution)/shard_map/ppermute | solution.py:298
  28.5 13.6 %collective-permute-start.4 = (bf16[64,2048]{1,0:T(8,128)(2,1)}, bf16[64,2048]{1,0:T(8,128)(2,1)S(1)}, u32[]{:S(2)}, u32[]{:S(2)}) collective-permute-start(bf16[64,2048]{1,0:T(8,128)(2,1)} %collective-permute-done.3.refs_4_), channel_id=1, source_target_pairs={{0,4},{4,0},{8,12},{12,8},{1,5},{5,1},{9,13},{13,9},{2,6},{6,2},{1... | collective-permute-start | bytes 786440 | tf_op jit(solution)/shard_map/ppermute | solution.py:298
  33.5 14.1 %collective-permute-start.5 = (bf16[64,2048]{1,0:T(8,128)(2,1)}, bf16[64,2048]{1,0:T(8,128)(2,1)S(1)}, u32[]{:S(2)}, u32[]{:S(2)}) collective-permute-start(bf16[64,2048]{1,0:T(8,128)(2,1)} %collective-permute-done.3.refs_4_), channel_id=1, source_target_pairs={{0,8},{4,12},{8,0},{12,4},{1,9},{5,13},{9,1},{13,5},{2,10},{6,14},... | collective-permute-start | bytes 786440 | tf_op jit(solution)/shard_map/ppermute | solution.py:298
  42.1 16.9 %collective-permute-start.15 = (bf16[32,2048]{1,0:T(8,128)(2,1)S(1)}, bf16[32,2048]{1,0:T(8,128)(2,1)}, u32[]{:S(2)}, u32[]{:S(2)}) collective-permute-start(bf16[32,2048]{1,0:T(8,128)(2,1)S(1)} %slice.181), channel_id=1, source_target_pairs={{0,8},{4,12},{8,0},{12,4},{1,9},{5,13},{9,1},{13,5},{2,10},{6,14},... | collective-permute-start | bytes 393224 | tf_op jit(solution)/shard_map/ppermute | solution.py:298
  44.9 15.6 %collective-permute-start.17 = (bf16[32,2048]{1,0:T(8,128)(2,1)S(1)}, bf16[32,2048]{1,0:T(8,128)(2,1)}, u32[]{:S(2)}, u32[]{:S(2)}) collective-permute-start(bf16[32,2048]{1,0:T(8,128)(2,1)S(1)} %slice.183), channel_id=1, source_target_pairs={{0,8},{4,12},{8,0},{12,4},{1,9},{5,13},{9,1},{13,5},{2,10},{6,14},... | collective-permute-start | bytes 393224 | tf_op jit(solution)/shard_map/ppermute | solution.py:298
  45.5 15.6 %collective-permute-start.16 = (bf16[32,2048]{1,0:T(8,128)(2,1)S(1)}, bf16[32,2048]{1,0:T(8,128)(2,1)}, u32[]{:S(2)}, u32[]{:S(2)}) collective-permute-start(bf16[32,2048]{1,0:T(8,128)(2,1)S(1)} %slice.182), channel_id=1, source_target_pairs={{0,8},{4,12},{8,0},{12,4},{1,9},{5,13},{9,1},{13,5},{2,10},{6,14},... | collective-permute-start | bytes 393224 | tf_op jit(solution)/shard_map/ppermute | solution.py:298
  47.6 15.0 %collective-permute-start.18 = (bf16[32,2048]{1,0:T(8,128)(2,1)S(1)}, bf16[32,2048]{1,0:T(8,128)(2,1)}, u32[]{:S(2)}, u32[]{:S(2)}) collective-permute-start(bf16[32,2048]{1,0:T(8,128)(2,1)S(1)} %slice.184), channel_id=1, source_target_pairs={{0,8},{4,12},{8,0},{12,4},{1,9},{5,13},{9,1},{13,5},{2,10},{6,14},... | collective-permute-start | bytes 393224 | tf_op jit(solution)/shard_map/ppermute | solution.py:298
  58.4 14.5 %collective-permute-start.2 = (bf16[32,2048]{1,0:T(8,128)(2,1)S(1)}, bf16[32,2048]{1,0:T(8,128)(2,1)S(1)}, u32[]{:S(2)}, u32[]{:S(2)}) collective-permute-start(bf16[32,2048]{1,0:T(8,128)(2,1)S(1)} %slice.177), channel_id=1, source_target_pairs={{0,4},{4,0},{8,12},{12,8},{1,5},{5,1},{9,13},{13,9},{2,6},{6,2},{1... | collective-permute-start | bytes 393224 | tf_op jit(solution)/shard_map/ppermute | solution.py:298
  59.0 14.0 %collective-permute-start.10 = (bf16[32,2048]{1,0:T(8,128)(2,1)S(1)}, bf16[32,2048]{1,0:T(8,128)(2,1)S(1)}, u32[]{:S(2)}, u32[]{:S(2)}) collective-permute-start(bf16[32,2048]{1,0:T(8,128)(2,1)S(1)} %slice.179), channel_id=1, source_target_pairs={{0,4},{4,0},{8,12},{12,8},{1,5},{5,1},{9,13},{13,9},{2,6},{6,2},{1... | collective-permute-start | bytes 393224 | tf_op jit(solution)/shard_map/ppermute | solution.py:298
  60.6 12.5 %collective-permute-start.6 = (bf16[32,2048]{1,0:T(8,128)(2,1)S(1)}, bf16[32,2048]{1,0:T(8,128)(2,1)S(1)}, u32[]{:S(2)}, u32[]{:S(2)}) collective-permute-start(bf16[32,2048]{1,0:T(8,128)(2,1)S(1)} %slice.178), channel_id=1, source_target_pairs={{0,4},{4,0},{8,12},{12,8},{1,5},{5,1},{9,13},{13,9},{2,6},{6,2},{1... | collective-permute-start | bytes 393224 | tf_op jit(solution)/shard_map/ppermute | solution.py:298
  61.1 11.9 %collective-permute-start.14 = (bf16[32,2048]{1,0:T(8,128)(2,1)S(1)}, bf16[32,2048]{1,0:T(8,128)(2,1)S(1)}, u32[]{:S(2)}, u32[]{:S(2)}) collective-permute-start(bf16[32,2048]{1,0:T(8,128)(2,1)S(1)} %slice.180), channel_id=1, source_target_pairs={{0,4},{4,0},{8,12},{12,8},{1,5},{5,1},{9,13},{13,9},{2,6},{6,2},{1... | collective-permute-start | bytes 393224 | tf_op jit(solution)/shard_map/ppermute | solution.py:298
  160.4 15.0 %collective-permute-start.37 = (bf16[16,2048]{1,0:T(8,128)(2,1)S(1)}, bf16[16,2048]{1,0:T(8,128)(2,1)S(1)}, u32[]{:S(2)}, u32[]{:S(2)}) collective-permute-start(bf16[16,2048]{1,0:T(8,128)(2,1)S(1)} %slice.193), channel_id=1, source_target_pairs={{0,4},{4,0},{8,12},{12,8},{1,5},{5,1},{9,13},{13,9},{2,6},{6,2},{1... | collective-permute-start | bytes 196616 | tf_op jit(solution)/shard_map/ppermute | solution.py:298
  160.9 14.6 %collective-permute-start.41 = (bf16[16,2048]{1,0:T(8,128)(2,1)S(1)}, bf16[16,2048]{1,0:T(8,128)(2,1)S(1)}, u32[]{:S(2)}, u32[]{:S(2)}) collective-permute-start(bf16[16,2048]{1,0:T(8,128)(2,1)S(1)} %slice.194), channel_id=1, source_target_pairs={{0,8},{4,12},{8,0},{12,4},{1,9},{5,13},{9,1},{13,5},{2,10},{6,14},... | collective-permute-start | bytes 196616 | tf_op jit(solution)/shard_map/ppermute | solution.py:298
  162.1 13.4 %collective-permute-start.42 = (bf16[16,2048]{1,0:T(8,128)(2,1)S(1)}, bf16[16,2048]{1,0:T(8,128)(2,1)S(1)}, u32[]{:S(2)}, u32[]{:S(2)}) collective-permute-start(bf16[16,2048]{1,0:T(8,128)(2,1)S(1)} %slice.195), channel_id=1, source_target_pairs={{0,4},{4,0},{8,12},{12,8},{1,5},{5,1},{9,13},{13,9},{2,6},{6,2},{1... | collective-permute-start | bytes 196616 | tf_op jit(solution)/shard_map/ppermute | solution.py:298
  163.3 12.2 %collective-permute-start.46 = (bf16[16,2048]{1,0:T(8,128)(2,1)S(1)}, bf16[16,2048]{1,0:T(8,128)(2,1)S(1)}, u32[]{:S(2)}, u32[]{:S(2)}) collective-permute-start(bf16[16,2048]{1,0:T(8,128)(2,1)S(1)} %slice.196), channel_id=1, source_target_pairs={{0,8},{4,12},{8,0},{12,4},{1,9},{5,13},{9,1},{13,5},{2,10},{6,14},... | collective-permute-start | bytes 196616 | tf_op jit(solution)/shard_map/ppermute | solution.py:298
  190.7 11.7 %collective-permute-start.71 = (bf16[64,2048]{1,0:T(8,128)(2,1)}, bf16[64,2048]{1,0:T(8,128)(2,1)S(1)}, u32[]{:S(2)}, u32[]{:S(2)}) collective-permute-start(bf16[64,2048]{1,0:T(8,128)(2,1)} %get-tuple-element.44), channel_id=1, source_target_pairs={{0,8},{4,12},{8,0},{12,4},{1,9},{5,13},{9,1},{13,5},{2,10},{6,14},... | collective-permute-start | bytes 786440 | tf_op jit(solution)/shard_map/ppermute | solution.py:298
  192.6 28.9 %all-to-all-start.1 = ((f32[16,1,32]{2,1,0:T(1,128)}), f32[16,1,32]{2,1,0:T(1,128)S(1)}, u32[]{:S(2)}, u32[]{:S(2)}) async-start(f32[16,1,32]{2,1,0:T(1,128)} %bitcast.35), calls=%async_computation.1 | async-start | bytes 16384 | tf_op jit(solution)/shard_map/all_to_all | solution.py:431
  215.5 18.3 %collective-permute-start.70 = (bf16[32,2048]{1,0:T(8,128)(2,1)S(1)}, bf16[32,2048]{1,0:T(8,128)(2,1)S(1)}, u32[]{:S(2)}, u32[]{:S(2)}) collective-permute-start(bf16[32,2048]{1,0:T(8,128)(2,1)S(1)} %slice.248), channel_id=1, source_target_pairs={{0,1},{1,0},{2,3},{3,2},{4,5},{5,4},{6,7},{7,6},{8,9},{9,8},{10,11... | collective-permute-start | bytes 393224 | tf_op jit(solution)/shard_map/ppermute | solution.py:298
  218.8 14.9 %collective-permute-start.75 = (bf16[32,2048]{1,0:T(8,128)(2,1)S(1)}, bf16[32,2048]{1,0:T(8,128)(2,1)S(1)}, u32[]{:S(2)}, u32[]{:S(2)}) collective-permute-start(bf16[32,2048]{1,0:T(8,128)(2,1)S(1)} %fusion), channel_id=1, source_target_pairs={{0,2},{1,3},{2,0},{3,1},{4,6},{5,7},{6,4},{7,5},{8,10},{9,11},{10,... | collective-permute-start | bytes 393224 | tf_op jit(solution)/shard_map/ppermute | solution.py:298
  (107 other events, 1397.6 us)

commit v2 on v0

--- a/solution.py
+++ b/solution.py
@@ -1,6 +1,10 @@
+import functools
+
 import jax
 import jax.numpy as jnp
 from jax import lax
+from jax.experimental import pallas as pl
+from jax.experimental.pallas import tpu as pltpu
 from jax.sharding import PartitionSpec as P
 
 CONTRACT_LAST = (((1,), (1,)), ((), ()))
@@ -46,7 +50,9 @@
     expert_range = jnp.arange(expert_count, dtype=jnp.int32)
     matches = (choice_ids[:, :, None] == expert_range[None, None, :]).astype(jnp.int32)
     chosen = jnp.sum(matches, axis=1)
-    before = jnp.cumsum(chosen, axis=0) - chosen
+    rows = jnp.arange(choice_ids.shape[0])
+    earlier = (rows[:, None] > rows[None, :]).astype(jnp.float32)
+    before = jnp.dot(earlier, chosen.astype(jnp.float32)).astype(jnp.int32)
     slot_range = jnp.arange(capacity, dtype=jnp.int32)
     placed = (before[:, :, None] == slot_range[None, None, :]) & (chosen[:, :, None] > 0)
     slot_map = jnp.transpose(placed, (1, 2, 0)).astype(jnp.float32)
@@ -109,7 +115,7 @@
     return (summed.astype(jnp.bfloat16), gate_values.astype(jnp.bfloat16))
 
 
-def local(
+def routed_local(
     output_grad,
     carried_grad,
     layer_inputs,
@@ -154,6 +160,267 @@
     return (jnp.stack(grads_out)[None], jnp.stack(gates_out)[None])
 
 
+VMEM_LIMIT = 58 * 2**20
+WIDTH_TILE = 512
+LANES = 128
+
+
+def tiles(total, step):
+    return [(start, min(step, total - start)) for start in range(0, total, step)]
+
+
+def whole_lanes(amount):
+    return (amount + LANES - 1) // LANES * LANES
+
+
+def begun(source, target, sem):
+    copy = pltpu.make_async_copy(source, target, sem)
+    copy.start()
+    return copy
+
+
+def pieces_begun(piece_refs, plan, rows_ref, sems):
+    return [
+        begun(
+            ref.at[pl.ds(begin, rows), pl.ds(0, rows_ref.shape[1])],
+            rows_ref.at[pl.ds(place, rows)],
+            sems.at[number],
+        )
+        for number, (ref, (begin, rows, place)) in enumerate(zip(piece_refs, plan))
+    ]
+
+
+def both_begun(gate_hbm, up_hbm, both_ref, sems):
+    hidden = gate_hbm.shape[0]
+    padded = both_ref.shape[0] // 2
+    return [
+        begun(gate_hbm, both_ref.at[pl.ds(0, hidden)], sems.at[0]),
+        begun(up_hbm, both_ref.at[pl.ds(padded, hidden)], sems.at[1]),
+    ]
+
+
+def math_kernel(plan, grad_plan, blocks, expert_ref, *refs):
+    count, grad_count = len(plan), len(grad_plan)
+    row_refs, grad_refs = refs[:count], refs[count : count + grad_count]
+    gate_hbm, up_hbm, down_hbm = refs[count + grad_count : count + grad_count + 3]
+    refs = refs[count + grad_count + 3 :]
+    out_refs, refs = refs[: len(blocks)], refs[len(blocks) :]
+    rows_ref, grad_rows_ref, down_ref, both_ref, grads_ref = refs[:5]
+    piece_sems, grad_sems, sems, both_sems = refs[5:]
+    hidden, width = down_ref.shape
+    padded = both_ref.shape[0] // 2
+    copies = pieces_begun(row_refs, plan, rows_ref, piece_sems)
+    copies += both_begun(gate_hbm, up_hbm, both_ref, both_sems)
+    late_copies = pieces_begun(grad_refs, grad_plan, grad_rows_ref, grad_sems)
+    late_copies.append(begun(down_hbm, down_ref, sems.at[0]))
+    for start in (hidden, padded + hidden):
+        both_ref[pl.ds(start, padded - hidden), :] = jnp.zeros(
+            (padded - hidden, width), jnp.bfloat16
+        )
+        grads_ref[:, pl.ds(start, padded - hidden)] = jnp.zeros(
+            (grads_ref.shape[0], padded - hidden), jnp.bfloat16
+        )
+    for copy in copies:
+        copy.wait()
+    pre = lax.dot_general(
+        rows_ref[...], both_ref[...], CONTRACT_LAST, preferred_element_type=jnp.float32
+    )
+    gate_pre, up_pre = pre[:, :hidden], pre[:, padded : padded + hidden]
+    for copy in late_copies:
+        copy.wait()
+    back_proj = lax.dot_general(
+        grad_rows_ref[:, :width], down_ref[...], CONTRACT_LAST, preferred_element_type=jnp.float32
+    )
+    lanes = lax.broadcasted_iota(jnp.int32, (1, LANES), 1)
+    mine = lanes == expert_ref[0]
+    probs = jnp.sum(
+        jnp.where(mine, grad_rows_ref[:, width:].astype(jnp.float32), 0.0), axis=1, keepdims=True
+    )
+    sigmoid_gate = jax.nn.sigmoid(gate_pre)
+    activated = gate_pre * sigmoid_gate
+    scaled = probs * back_proj
+    grads_ref[:, :hidden] = (
+        scaled * up_pre * sigmoid_gate * (1.0 + gate_pre * (1.0 - sigmoid_gate))
+    ).astype(jnp.bfloat16)
+    grads_ref[:, pl.ds(padded, hidden)] = (scaled * activated).astype(jnp.bfloat16)
+    part = jnp.sum(activated * up_pre * back_proj, axis=1, keepdims=True)
+    part = jnp.where(mine, part, 0.0).astype(jnp.bfloat16)
+    for out_ref, (place, amount) in zip(out_refs, blocks):
+        out_ref[:, width:] = part[place : place + amount]
+    for start, size in tiles(width, WIDTH_TILE):
+        columns = pl.ds(start, size)
+        grads = jnp.dot(
+            grads_ref[...], both_ref[:, columns], preferred_element_type=jnp.float32
+        ).astype(jnp.bfloat16)
+        for out_ref, (place, amount) in zip(out_refs, blocks):
+            out_ref[:, columns] = grads[place : place + amount]
+
+
+ANYWHERE = pl.BlockSpec(memory_space=pl.ANY)
+IN_VMEM = pl.BlockSpec(memory_space=pltpu.VMEM)
+
+
+def expert_math(rows_in, plan, grads_in, grad_plan, blocks, expert, weights):
+    hidden, width = weights[0].shape
+    rows = sum(amount for _, amount in blocks)
+    outs = [jax.ShapeDtypeStruct((amount, width + LANES), jnp.bfloat16) for _, amount in blocks]
+    return pl.pallas_call(
+        functools.partial(math_kernel, plan, grad_plan, blocks),
+        out_shape=tuple(outs),
+        in_specs=[pl.BlockSpec(memory_space=pltpu.SMEM)]
+        + [ANYWHERE] * (len(rows_in) + len(grads_in) + 3),
+        out_specs=(IN_VMEM,) * len(outs),
+        scratch_shapes=[
+            pltpu.VMEM((rows, width), jnp.bfloat16),
+            pltpu.VMEM((rows, width + LANES), jnp.bfloat16),
+            pltpu.VMEM((hidden, width), jnp.bfloat16),
+            pltpu.VMEM((2 * whole_lanes(hidden), width), jnp.bfloat16),
+            pltpu.VMEM((rows, 2 * whole_lanes(hidden)), jnp.bfloat16),
+            pltpu.SemaphoreType.DMA((len(rows_in),)),
+            pltpu.SemaphoreType.DMA((len(grads_in),)),
+            pltpu.SemaphoreType.DMA((1,)),
+            pltpu.SemaphoreType.DMA((2,)),
+        ],
+        compiler_params=pltpu.CompilerParams(vmem_limit_bytes=VMEM_LIMIT),
+        cost_estimate=pl.CostEstimate(
+            flops=10 * rows * width * hidden,
+            bytes_accessed=6 * width * hidden + 6 * rows * width,
+            transcendentals=rows * hidden,
+        ),
+        name="expert_math",
+    )(expert, *rows_in, *grads_in, *weights)
+
+
+def toggled(value, axis, mask):
+    pairs = [(source, source ^ mask) for source in range(lax.axis_size(axis))]
+    return lax.ppermute(value, axis, pairs)
+
+
+def spread(block):
+    near = toggled(block, "local", 1)
+    far = toggled(block, "local", 2)
+    first = [toggled(block, "group", 1)]
+    second = [toggled(block, "group", 2)]
+    corner = toggled(far, "local", 1)
+    first += [toggled(column, "group", 1) for column in (far, corner)]
+    second += [toggled(column, "group", 2) for column in (far, corner)]
+    first.insert(1, toggled(first[0], "local", 1))
+    second.insert(1, toggled(second[0], "local", 1))
+    half = block.shape[0] // 2
+    low = [toggled(column[:half], "group", 2) for column in first]
+    high = [toggled(column[half:], "group", 1) for column in second]
+    return list(zip((block, near, far, corner), first, second, low, high))
+
+
+def piece_plan(found, begin, rows):
+    half = found[0][0].shape[0] // 2
+    arrays, plan = [], []
+    for level, (column, first, second, low, high) in enumerate(found):
+        for slot, array in ((0, column), (1, first), (2, second)):
+            arrays.append(array)
+            plan.append((begin, rows, (4 * slot + level) * rows))
+        place = (12 + level) * rows
+        upto = min(half, begin + rows)
+        if begin < upto:
+            arrays.append(low)
+            plan.append((begin, upto - begin, place))
+        since = max(half, begin)
+        if since < begin + rows:
+            arrays.append(high)
+            plan.append((since - half, begin + rows - since, place + since - begin))
+    return arrays, tuple(plan)
+
+
+def added(*values):
+    total = values[0].astype(jnp.float32)
+    for value in values[1:]:
+        total = total + value.astype(jnp.float32)
+    return total
+
+
+def brought_back(blocks):
+    diag_low, diag_high, first_low, first_high, second_low, second_high, own = blocks
+    rows = own.shape[0] // 4
+    got_low = toggled(diag_low, "group", 1)
+    got_high = toggled(diag_high, "group", 2)
+    from_second_high = toggled(second_high, "group", 2)
+    from_first_low = toggled(first_low, "group", 1)
+    from_first_high = toggled(added(first_high, got_high).astype(jnp.bfloat16), "group", 1)
+    from_second_low = toggled(added(second_low, got_low).astype(jnp.bfloat16), "group", 2)
+    high = added(own[2 * rows :], from_first_high, from_second_high)
+    low = added(own[: 2 * rows], from_first_low, from_second_low)
+    got_corner = toggled(high[rows:].astype(jnp.bfloat16), "local", 1)
+    got_far = toggled(added(high[:rows], got_corner).astype(jnp.bfloat16), "local", 2)
+    got_near = toggled(low[rows:].astype(jnp.bfloat16), "local", 1)
+    return added(low[:rows], got_near, got_far)
+
+
+def dense_local(
+    output_grad,
+    carried_grad,
+    layer_inputs,
+    expert_ids,
+    gate_prob,
+    gate_weight,
+    up_weight,
+    down_weight,
+):
+    expert_count = lax.axis_size("group") * lax.axis_size("local") // 2
+    micro_count, rows, width = output_grad.shape
+    gate_half, up_half, down_half = gate_weight[0, 0].T, up_weight[0, 0].T, down_weight[0, 0]
+    own_index = lax.axis_index("group") * lax.axis_size("local") + lax.axis_index("local")
+    expert = jnp.reshape(own_index // 2, (1,)).astype(jnp.int32)
+    matches = (expert_ids[0][..., None] == jnp.arange(LANES, dtype=jnp.int32)).astype(jnp.float32)
+    token_probs = jnp.sum(matches * gate_prob[0].astype(jnp.float32)[..., None], axis=2)
+    token_probs = token_probs.astype(jnp.bfloat16)
+    last_section = lax.axis_index("pipe") == lax.axis_size("pipe") - 1
+    inputs = layer_inputs[0]
+    quarter = 4 * rows
+    blocks = (
+        (3 * quarter, 2 * rows),
+        (3 * quarter + 2 * rows, 2 * rows),
+        (quarter, 2 * rows),
+        (quarter + 2 * rows, 2 * rows),
+        (2 * quarter, 2 * rows),
+        (2 * quarter + 2 * rows, 2 * rows),
+        (0, quarter),
+    )
+    weights = (gate_half, up_half, down_half)
+    none = jnp.zeros((rows, LANES), jnp.bfloat16)
+    earlier = carried_grad
+    grads_out, gates = [], []
+    for m in range(micro_count):
+        if m > 0:
+            earlier = from_behind(grads_out[-1], "pipe", -1)
+        incoming = jnp.where(last_section, output_grad[m], earlier)
+        sent = jnp.concatenate(
+            [
+                jnp.concatenate([inputs[m], incoming], axis=0),
+                jnp.concatenate([none, token_probs[m]], axis=0),
+            ],
+            axis=1,
+        )
+        found = spread(sent)
+        arrays, plan = piece_plan(found, 0, rows)
+        grad_arrays, grad_plan = piece_plan(found, rows, rows)
+        pieces = expert_math(arrays, plan, grad_arrays, grad_plan, blocks, expert, weights)
+        total = brought_back(pieces)
+        grads_out.append(added(incoming, total[:, :width]).astype(jnp.bfloat16))
+        gates.append(total[:, width:])
+    gates = jnp.sum(matches * jnp.stack(gates)[:, :, None, :], axis=3).astype(jnp.bfloat16)
+    return (jnp.stack(grads_out)[None], gates[None])
+
+
+def local(*arguments):
+    group, ring = lax.axis_size("group"), lax.axis_size("local")
+    top_count = arguments[3].shape[-1]
+    expert_count = group * ring // 2
+    crowded = 3 * expert_count <= 4 * top_count
+    if group == 4 and ring == 4 and crowded and expert_count <= LANES:
+        return dense_local(*arguments)
+    return routed_local(*arguments)
+
+
 def solution(mesh):
     return jax.shard_map(
         local,

time: 431 us -> 216 us (0.50)
  waiting for transfers between devices: 294 us -> 101 us
  matrix products: 62.3 us -> 0 us
  Pallas kernels: 0 us -> 31.9 us
  starting transfers between devices: 37.3 us -> 68 us
  blocking collectives: 29.6 us -> 0 us
  other arithmetic: 1.27 us -> 9.71 us
    all_to_all x7 -> x0, waiting for transfers between devices: 180 us -> none  [the longest x2 83.3 us: layer_backward(): lax.all_to_all(sent_grads, ('group', 'local'), split_axis=0, concat_axis=...]
    ppermute x3 -> x56, starting transfers between devices: 3.95 us -> 66.6 us  [toggled(): return lax.ppermute(value, axis, pairs)]
    dot_general x20 -> x0, matrix products: 62.3 us -> none  [the longest x2 13.1 us: expert_backward(): lax.dot_general(rows_grad, down_full, CONTRACT_LAST, preferred_element_ty...]
    all_to_all x7 -> x0, starting transfers between devices: 32 us -> none  [the longest x2 12.1 us: layer_backward(): lax.all_to_all(sent_inputs, ('group', 'local'), split_axis=0, concat_axis...]
    pallas_call x0 -> x2, Pallas kernels: none -> 31.9 us  [expert_math(): pl.pallas_call(functools.partial(math_kernel, plan, grad_plan, blocks), o...]
    all_to_all x3 -> x0, blocking collectives: 29.6 us -> none  [the longest x2 19.7 us: layer_backward(): lax.all_to_all(sent_probs, ('group', 'local'), split_axis=0, concat_axis=...]
    ppermute x3 -> x56, waiting for transfers between devices: 112 us -> 99.2 us  [toggled(): return lax.ppermute(value, axis, pairs)]
    convert_element_type x8, other arithmetic: 0.25 us -> 4.94 us  [the longest x2 2.1 us: brought_back(): added(first_high, got_high).astype(jnp.bfloat16)]
  transfers between devices with their start and end apart: 11 -> 57, of which waited for: 10 -> 36; matrix products, arithmetic and copies ran while one was open for 6% -> 2% of each run, Pallas kernels for 0% -> 0%
where the time goes in v2:
time: 216 us
  waiting for transfers between devices  101 us (47%)
  starting transfers between devices  68 us (31%)
  Pallas kernels  31.9 us (15%)
  other arithmetic  9.71 us (4%)
  local copies, waits for them, and re-layouts  3.94 us (2%)
    ppermute x56, waiting for transfers between devices, toggled(): return lax.ppermute(value, axis, pairs)  99.2 us
    ppermute x56, starting transfers between devices, toggled(): return lax.ppermute(value, axis, pairs)  66.6 us
    pallas_call x2, Pallas kernels, expert_math(): pl.pallas_call(functools.partial(math_kernel, plan, grad_plan, blocks), o...  31.9 us
  transfers between devices with their start and end apart: 57, of which 36 were waited for; matrix products, arithmetic and copies ran while one was open for 2% of the time, Pallas kernels for 0%

profile of v2, /device:TPU:0, one launch (start us, length us, event | category | flops | bytes accessed | tf_op | source)
XLA Modules:
  0.0 215.8 jit_solution(10799311008694806923)
XLA Ops:
  4.2 4.1 %collective-permute-start.7 = (bf16[64,2176]{1,0:T(8,128)(2,1)S(1)}, bf16[64,2176]{1,0:T(8,128)(2,1)S(1)}, u32[]{:S(2)}, u32[]{:S(2)}) collective-permute-start(bf16[64,2176]{1,0:T(8,128)(2,1)S(1)} %fusion.2.refs_0_.refs_16_), channel_id=1, source_target_pairs={{0,2},{1,3},{2,0},{3,1},{4,6},{5,7},{6,4},{7,5},{8,10},{9,11},{10,... | collective-permute-start | bytes 835592 | tf_op jit(solution)/shard_map/ppermute | solution.py:296
  11.3 9.6 %collective-permute-done.7.refs_8_.refs_24_ = bf16[64,2176]{1,0:T(8,128)(2,1)S(1)} collective-permute-done((bf16[64,2176]{1,0:T(8,128)(2,1)S(1)}, bf16[64,2176]{1,0:T(8,128)(2,1)S(1)}, u32[]{:S(2)}, u32[]{:S(2)}) %collective-permute-start.7) | collective-permute-done | bytes 278560 | tf_op jit(solution)/shard_map/ppermute | solution.py:296
  26.7 3.8 %collective-permute-done.11.refs_12_.refs_28_ = bf16[64,2176]{1,0:T(8,128)(2,1)S(1)} collective-permute-done((bf16[64,2176]{1,0:T(8,128)(2,1)S(1)}, bf16[64,2176]{1,0:T(8,128)(2,1)S(1)}, u32[]{:S(2)}, u32[]{:S(2)}) %collective-permute-start.11) | collective-permute-done | bytes 278560 | tf_op jit(solution)/shard_map/ppermute | solution.py:296
  34.2 2.2 %collective-permute-done.5.refs_6_.refs_22_ = bf16[64,2176]{1,0:T(8,128)(2,1)S(1)} collective-permute-done((bf16[64,2176]{1,0:T(8,128)(2,1)S(1)}, bf16[64,2176]{1,0:T(8,128)(2,1)S(1)}, u32[]{:S(2)}, u32[]{:S(2)}) %collective-permute-start.5) | collective-permute-done | bytes 278560 | tf_op jit(solution)/shard_map/ppermute | solution.py:296
  38.0 4.4 %collective-permute-done.4.refs_5_.refs_21_ = bf16[64,2176]{1,0:T(8,128)(2,1)S(1)} collective-permute-done((bf16[64,2176]{1,0:T(8,128)(2,1)S(1)}, bf16[64,2176]{1,0:T(8,128)(2,1)S(1)}, u32[]{:S(2)}, u32[]{:S(2)}) %collective-permute-start.4) | collective-permute-done | bytes 278560 | tf_op jit(solution)/shard_map/ppermute | solution.py:296
  56.5 16.0 %expert_math.2 = (bf16[64,2176]{1,0:T(8,128)(2,1)}, bf16[64,2176]{1,0:T(8,128)(2,1)}, bf16[64,2176]{1,0:T(8,128)(2,1)}, bf16[64,2176]{1,0:T(8,128)(2,1)}, bf16[6...) custom-call(s32[1]{0:T(128)} %bitcast.1.expert_ref, bf16[64,2176]{1,0:T(8,128)(2,1)} %copy-done, ...), custom_call_target="tpu_custom_call" | custom-call | flops 7381975040 | bytes 14942208 | tf_op jit(solution)/shard_map/expert_math/pallas_call | solution.py:267
  76.6 5.7 %collective-permute-done.20 = bf16[64,2176]{1,0:T(8,128)(2,1)S(1)} collective-permute-done((bf16[64,2176]{1,0:T(8,128)(2,1)}, bf16[64,2176]{1,0:T(8,128)(2,1)S(1)}, u32[]{:S(2)}, u32[]{:S(2)}) %collective-permute-start.20) | collective-permute-done | bytes 278560 | tf_op jit(solution)/shard_map/ppermute | solution.py:296
  89.8 3.0 %collective-permute-done.21 = bf16[64,2176]{1,0:T(8,128)(2,1)S(1)} collective-permute-done((bf16[64,2176]{1,0:T(8,128)(2,1)S(1)}, bf16[64,2176]{1,0:T(8,128)(2,1)S(1)}, u32[]{:S(2)}, u32[]{:S(2)}) %collective-permute-start.21) | collective-permute-done | bytes 278560 | tf_op jit(solution)/shard_map/ppermute | solution.py:296
  96.2 2.9 %collective-permute-done.26 = bf16[32,2176]{1,0:T(8,128)(2,1)S(1)} collective-permute-done((bf16[32,2176]{1,0:T(8,128)(2,1)S(1)}, bf16[32,2176]{1,0:T(8,128)(2,1)S(1)}, u32[]{:S(2)}, u32[]{:S(2)}) %collective-permute-start.26) | collective-permute-done | bytes 139296 | tf_op jit(solution)/shard_map/ppermute | solution.py:296
  99.2 4.9 %collective-permute-start.27 = (bf16[32,2176]{1,0:T(8,128)(2,1)S(1)}, bf16[32,2176]{1,0:T(8,128)(2,1)S(1)}, u32[]{:S(2)}, u32[]{:S(2)}) collective-permute-start(bf16[32,2176]{1,0:T(8,128)(2,1)S(1)} %fusion.6), channel_id=1, source_target_pairs={{0,2},{1,3},{2,0},{3,1},{4,6},{5,7},{6,4},{7,5},{8,10},{9,11},{10,... | collective-permute-start | bytes 417800 | tf_op jit(solution)/shard_map/ppermute | solution.py:296
  104.1 4.5 %collective-permute-done.27 = bf16[32,2176]{1,0:T(8,128)(2,1)S(1)} collective-permute-done((bf16[32,2176]{1,0:T(8,128)(2,1)S(1)}, bf16[32,2176]{1,0:T(8,128)(2,1)S(1)}, u32[]{:S(2)}, u32[]{:S(2)}) %collective-permute-start.27) | collective-permute-done | bytes 139296 | tf_op jit(solution)/shard_map/ppermute | solution.py:296
  116.1 11.6 %collective-permute-done.36.refs_8_.refs_24_ = bf16[64,2176]{1,0:T(8,128)(2,1)S(1)} collective-permute-done((bf16[64,2176]{1,0:T(8,128)(2,1)S(1)}, bf16[64,2176]{1,0:T(8,128)(2,1)S(1)}, u32[]{:S(2)}, u32[]{:S(2)}) %collective-permute-start.36) | collective-permute-done | bytes 278560 | tf_op jit(solution)/shard_map/ppermute | solution.py:296
  127.7 2.5 %collective-permute-start.37 = (bf16[64,2176]{1,0:T(8,128)(2,1)S(1)}, bf16[64,2176]{1,0:T(8,128)(2,1)S(1)}, u32[]{:S(2)}, u32[]{:S(2)}) collective-permute-start(bf16[64,2176]{1,0:T(8,128)(2,1)S(1)} %collective-permute-done.36.refs_8_.refs_24_), channel_id=1, source_target_pairs={{0,4},{4,0},{8,12},{12,8},{1,5},{5,1},{9,13},{13,9},{2,6},{6,2},{1... | collective-permute-start | bytes 835592 | tf_op jit(solution)/shard_map/ppermute | solution.py:296
  132.3 5.0 %collective-permute-done.40.refs_12_.refs_28_ = bf16[64,2176]{1,0:T(8,128)(2,1)S(1)} collective-permute-done((bf16[64,2176]{1,0:T(8,128)(2,1)S(1)}, bf16[64,2176]{1,0:T(8,128)(2,1)S(1)}, u32[]{:S(2)}, u32[]{:S(2)}) %collective-permute-start.40) | collective-permute-done | bytes 278560 | tf_op jit(solution)/shard_map/ppermute | solution.py:296
  137.3 2.5 %collective-permute-start.41 = (bf16[64,2176]{1,0:T(8,128)(2,1)S(1)}, bf16[64,2176]{1,0:T(8,128)(2,1)S(1)}, u32[]{:S(2)}, u32[]{:S(2)}) collective-permute-start(bf16[64,2176]{1,0:T(8,128)(2,1)S(1)} %collective-permute-done.40.refs_12_.refs_28_), channel_id=1, source_target_pairs={{0,4},{4,0},{8,12},{12,8},{1,5},{5,1},{9,13},{13,9},{2,6},{6,2},{1... | collective-permute-start | bytes 835592 | tf_op jit(solution)/shard_map/ppermute | solution.py:296
  139.8 3.4 %collective-permute-done.34.refs_6_.refs_22_ = bf16[64,2176]{1,0:T(8,128)(2,1)S(1)} collective-permute-done((bf16[64,2176]{1,0:T(8,128)(2,1)S(1)}, bf16[64,2176]{1,0:T(8,128)(2,1)S(1)}, u32[]{:S(2)}, u32[]{:S(2)}) %collective-permute-start.34) | collective-permute-done | bytes 278560 | tf_op jit(solution)/shard_map/ppermute | solution.py:296
  143.4 5.8 %collective-permute-done.33.refs_5_.refs_21_ = bf16[64,2176]{1,0:T(8,128)(2,1)S(1)} collective-permute-done((bf16[64,2176]{1,0:T(8,128)(2,1)S(1)}, bf16[64,2176]{1,0:T(8,128)(2,1)S(1)}, u32[]{:S(2)}, u32[]{:S(2)}) %collective-permute-start.33) | collective-permute-done | bytes 278560 | tf_op jit(solution)/shard_map/ppermute | solution.py:296
  149.2 2.5 %collective-permute-start.46 = (bf16[32,2176]{1,0:T(8,128)(2,1)S(1)}, bf16[32,2176]{1,0:T(8,128)(2,1)S(1)}, u32[]{:S(2)}, u32[]{:S(2)}) collective-permute-start(bf16[32,2176]{1,0:T(8,128)(2,1)S(1)} %slice.179), channel_id=1, source_target_pairs={{0,4},{4,0},{8,12},{12,8},{1,5},{5,1},{9,13},{13,9},{2,6},{6,2},{1... | collective-permute-start | bytes 417800 | tf_op jit(solution)/shard_map/ppermute | solution.py:296
  153.7 2.7 %collective-permute-start.35 = (bf16[32,2176]{1,0:T(8,128)(2,1)S(1)}, bf16[32,2176]{1,0:T(8,128)(2,1)S(1)}, u32[]{:S(2)}, u32[]{:S(2)}) collective-permute-start(bf16[32,2176]{1,0:T(8,128)(2,1)S(1)} %slice.174), channel_id=1, source_target_pairs={{0,8},{4,12},{8,0},{12,4},{1,9},{5,13},{9,1},{13,5},{2,10},{6,14},... | collective-permute-start | bytes 417800 | tf_op jit(solution)/shard_map/ppermute | solution.py:296
  163.7 15.9 %expert_math.3 = (bf16[64,2176]{1,0:T(8,128)(2,1)}, bf16[64,2176]{1,0:T(8,128)(2,1)}, bf16[64,2176]{1,0:T(8,128)(2,1)}, bf16[64,2176]{1,0:T(8,128)(2,1)}, bf16[6...) custom-call(s32[1]{0:T(128)} %bitcast.1.expert_ref, bf16[64,2176]{1,0:T(8,128)(2,1)} %copy-done.1, ...), custom_call_target="tpu_custom_call" | custom-call | flops 7381975040 | bytes 14942208 | tf_op jit(solution)/shard_map/expert_math/pallas_call | solution.py:267
  183.7 5.8 %collective-permute-done.49 = bf16[64,2176]{1,0:T(8,128)(2,1)S(1)} collective-permute-done((bf16[64,2176]{1,0:T(8,128)(2,1)}, bf16[64,2176]{1,0:T(8,128)(2,1)S(1)}, u32[]{:S(2)}, u32[]{:S(2)}) %collective-permute-start.49) | collective-permute-done | bytes 278560 | tf_op jit(solution)/shard_map/ppermute | solution.py:296
  197.5 3.3 %collective-permute-done.50 = bf16[64,2176]{1,0:T(8,128)(2,1)S(1)} collective-permute-done((bf16[64,2176]{1,0:T(8,128)(2,1)S(1)}, bf16[64,2176]{1,0:T(8,128)(2,1)S(1)}, u32[]{:S(2)}, u32[]{:S(2)}) %collective-permute-start.50) | collective-permute-done | bytes 278560 | tf_op jit(solution)/shard_map/ppermute | solution.py:296
  204.2 3.0 %collective-permute-done.55 = bf16[32,2176]{1,0:T(8,128)(2,1)S(1)} collective-permute-done((bf16[32,2176]{1,0:T(8,128)(2,1)S(1)}, bf16[32,2176]{1,0:T(8,128)(2,1)S(1)}, u32[]{:S(2)}, u32[]{:S(2)}) %collective-permute-start.55) | collective-permute-done | bytes 139296 | tf_op jit(solution)/shard_map/ppermute | solution.py:296
  210.2 4.0 %collective-permute-done.56 = bf16[32,2176]{1,0:T(8,128)(2,1)S(1)} collective-permute-done((bf16[32,2176]{1,0:T(8,128)(2,1)S(1)}, bf16[32,2176]{1,0:T(8,128)(2,1)S(1)}, u32[]{:S(2)}, u32[]{:S(2)}) %collective-permute-start.56) | collective-permute-done | bytes 139296 | tf_op jit(solution)/shard_map/ppermute | solution.py:296
  (212 shorter events, 85.5 us)
Async XLA Ops:
  4.2 16.7 %collective-permute-start.7 = (bf16[64,2176]{1,0:T(8,128)(2,1)S(1)}, bf16[64,2176]{1,0:T(8,128)(2,1)S(1)}, u32[]{:S(2)}, u32[]{:S(2)}) collective-permute-start(bf16[64,2176]{1,0:T(8,128)(2,1)S(1)} %fusion.2.refs_0_.refs_16_), channel_id=1, source_target_pairs={{0,2},{1,3},{2,0},{3,1},{4,6},{5,7},{6,4},{7,5},{8,10},{9,11},{10,... | collective-permute-start | bytes 835592 | tf_op jit(solution)/shard_map/ppermute | solution.py:296
  8.3 16.3 %collective-permute-start.1 = (bf16[64,2176]{1,0:T(8,128)(2,1)S(1)}, bf16[64,2176]{1,0:T(8,128)(2,1)S(1)}, u32[]{:S(2)}, u32[]{:S(2)}) collective-permute-start(bf16[64,2176]{1,0:T(8,128)(2,1)S(1)} %fusion.2.refs_0_.refs_16_), channel_id=1, source_target_pairs={{0,8},{4,12},{8,0},{12,4},{1,9},{5,13},{9,1},{13,5},{2,10},{6,14},... | collective-permute-start | bytes 835592 | tf_op jit(solution)/shard_map/ppermute | solution.py:296
  9.9 16.1 %collective-permute-start = (bf16[64,2176]{1,0:T(8,128)(2,1)S(1)}, bf16[64,2176]{1,0:T(8,128)(2,1)S(1)}, u32[]{:S(2)}, u32[]{:S(2)}) collective-permute-start(bf16[64,2176]{1,0:T(8,128)(2,1)S(1)} %fusion.2.refs_0_.refs_16_), channel_id=1, source_target_pairs={{0,4},{4,0},{8,12},{12,8},{1,5},{5,1},{9,13},{13,9},{2,6},{6,2},{1... | collective-permute-start | bytes 835592 | tf_op jit(solution)/shard_map/ppermute | solution.py:296
  21.6 10.4 %collective-permute-start.9 = (bf16[64,2176]{1,0:T(8,128)(2,1)S(1)}, bf16[64,2176]{1,0:T(8,128)(2,1)S(1)}, u32[]{:S(2)}, u32[]{:S(2)}) collective-permute-start(bf16[64,2176]{1,0:T(8,128)(2,1)S(1)} %collective-permute-done.7.refs_8_.refs_24_), channel_id=1, source_target_pairs={{0,8},{4,12},{8,0},{12,4},{1,9},{5,13},{9,1},{13,5},{2,10},{6,14},... | collective-permute-start | bytes 835592 | tf_op jit(solution)/shard_map/ppermute | solution.py:296
  23.1 10.4 %collective-permute-start.8 = (bf16[64,2176]{1,0:T(8,128)(2,1)S(1)}, bf16[64,2176]{1,0:T(8,128)(2,1)S(1)}, u32[]{:S(2)}, u32[]{:S(2)}) collective-permute-start(bf16[64,2176]{1,0:T(8,128)(2,1)S(1)} %collective-permute-done.7.refs_8_.refs_24_), channel_id=1, source_target_pairs={{0,4},{4,0},{8,12},{12,8},{1,5},{5,1},{9,13},{13,9},{2,6},{6,2},{1... | collective-permute-start | bytes 835592 | tf_op jit(solution)/shard_map/ppermute | solution.py:296
  24.6 11.8 %collective-permute-start.5 = (bf16[64,2176]{1,0:T(8,128)(2,1)S(1)}, bf16[64,2176]{1,0:T(8,128)(2,1)S(1)}, u32[]{:S(2)}, u32[]{:S(2)}) collective-permute-start(bf16[64,2176]{1,0:T(8,128)(2,1)S(1)} %collective-permute-done.1.refs_2_.refs_18_), channel_id=1, source_target_pairs={{0,1},{1,0},{2,3},{3,2},{4,5},{5,4},{6,7},{7,6},{8,9},{9,8},{10,11... | collective-permute-start | bytes 835592 | tf_op jit(solution)/shard_map/ppermute | solution.py:296
  26.0 16.4 %collective-permute-start.4 = (bf16[64,2176]{1,0:T(8,128)(2,1)S(1)}, bf16[64,2176]{1,0:T(8,128)(2,1)S(1)}, u32[]{:S(2)}, u32[]{:S(2)}) collective-permute-start(bf16[64,2176]{1,0:T(8,128)(2,1)S(1)} %collective-permute-done.refs_1_.refs_17_), channel_id=1, source_target_pairs={{0,1},{1,0},{2,3},{3,2},{4,5},{5,4},{6,7},{7,6},{8,9},{9,8},{10,11... | collective-permute-start | bytes 835592 | tf_op jit(solution)/shard_map/ppermute | solution.py:296
  30.5 13.5 %collective-permute-start.13 = (bf16[64,2176]{1,0:T(8,128)(2,1)S(1)}, bf16[64,2176]{1,0:T(8,128)(2,1)S(1)}, u32[]{:S(2)}, u32[]{:S(2)}) collective-permute-start(bf16[64,2176]{1,0:T(8,128)(2,1)S(1)} %collective-permute-done.11.refs_12_.refs_28_), channel_id=1, source_target_pairs={{0,8},{4,12},{8,0},{12,4},{1,9},{5,13},{9,1},{13,5},{2,10},{6,14},... | collective-permute-start | bytes 835592 | tf_op jit(solution)/shard_map/ppermute | solution.py:296
  32.1 13.5 %collective-permute-start.12 = (bf16[64,2176]{1,0:T(8,128)(2,1)S(1)}, bf16[64,2176]{1,0:T(8,128)(2,1)S(1)}, u32[]{:S(2)}, u32[]{:S(2)}) collective-permute-start(bf16[64,2176]{1,0:T(8,128)(2,1)S(1)} %collective-permute-done.11.refs_12_.refs_28_), channel_id=1, source_target_pairs={{0,4},{4,0},{8,12},{12,8},{1,5},{5,1},{9,13},{13,9},{2,6},{6,2},{1... | collective-permute-start | bytes 835592 | tf_op jit(solution)/shard_map/ppermute | solution.py:296
  33.6 13.0 %collective-permute-start.3 = (bf16[64,2176]{1,0:T(8,128)(2,1)S(1)}, bf16[64,2176]{1,0:T(8,128)(2,1)S(1)}, u32[]{:S(2)}, u32[]{:S(2)}) collective-permute-start(bf16[64,2176]{1,0:T(8,128)(2,1)S(1)} %fusion.2.refs_0_.refs_16_), channel_id=1, source_target_pairs={{0,1},{1,0},{2,3},{3,2},{4,5},{5,4},{6,7},{7,6},{8,9},{9,8},{10,11... | collective-permute-start | bytes 835592 | tf_op jit(solution)/shard_map/ppermute | solution.py:296
  36.5 11.4 %collective-permute-start.15 = (bf16[32,2176]{1,0:T(8,128)(2,1)S(1)}, bf16[32,2176]{1,0:T(8,128)(2,1)S(1)}, u32[]{:S(2)}, u32[]{:S(2)}) collective-permute-start(bf16[32,2176]{1,0:T(8,128)(2,1)S(1)} %slice.163), channel_id=1, source_target_pairs={{0,4},{4,0},{8,12},{12,8},{1,5},{5,1},{9,13},{13,9},{2,6},{6,2},{1... | collective-permute-start | bytes 417800 | tf_op jit(solution)/shard_map/ppermute | solution.py:296
  74.0 14.1 %collective-permute-start.19 = (bf16[64,2176]{1,0:T(8,128)(2,1)}, bf16[64,2176]{1,0:T(8,128)(2,1)S(1)}, u32[]{:S(2)}, u32[]{:S(2)}) collective-permute-start(bf16[64,2176]{1,0:T(8,128)(2,1)} %get-tuple-element.17), channel_id=1, source_target_pairs={{0,4},{4,0},{8,12},{12,8},{1,5},{5,1},{9,13},{13,9},{2,6},{6,2},{1... | collective-permute-start | bytes 835592 | tf_op jit(solution)/shard_map/ppermute | solution.py:296
  75.5 14.3 %collective-permute-start.25 = (bf16[64,2176]{1,0:T(8,128)(2,1)}, bf16[64,2176]{1,0:T(8,128)(2,1)S(1)}, u32[]{:S(2)}, u32[]{:S(2)}) collective-permute-start(bf16[64,2176]{1,0:T(8,128)(2,1)} %get-tuple-element.22), channel_id=1, source_target_pairs={{0,8},{4,12},{8,0},{12,4},{1,9},{5,13},{9,1},{13,5},{2,10},{6,14},... | collective-permute-start | bytes 835592 | tf_op jit(solution)/shard_map/ppermute | solution.py:296
  112.0 15.6 %collective-permute-start.36 = (bf16[64,2176]{1,0:T(8,128)(2,1)S(1)}, bf16[64,2176]{1,0:T(8,128)(2,1)S(1)}, u32[]{:S(2)}, u32[]{:S(2)}) collective-permute-start(bf16[64,2176]{1,0:T(8,128)(2,1)S(1)} %fusion.3.refs_0_.refs_16_), channel_id=1, source_target_pairs={{0,2},{1,3},{2,0},{3,1},{4,6},{5,7},{6,4},{7,5},{8,10},{9,11},{10,... | collective-permute-start | bytes 835592 | tf_op jit(solution)/shard_map/ppermute | solution.py:296
  113.6 16.5 %collective-permute-start.30 = (bf16[64,2176]{1,0:T(8,128)(2,1)S(1)}, bf16[64,2176]{1,0:T(8,128)(2,1)S(1)}, u32[]{:S(2)}, u32[]{:S(2)}) collective-permute-start(bf16[64,2176]{1,0:T(8,128)(2,1)S(1)} %fusion.3.refs_0_.refs_16_), channel_id=1, source_target_pairs={{0,8},{4,12},{8,0},{12,4},{1,9},{5,13},{9,1},{13,5},{2,10},{6,14},... | collective-permute-start | bytes 835592 | tf_op jit(solution)/shard_map/ppermute | solution.py:296
  114.0 18.2 %collective-permute-start.29 = (bf16[64,2176]{1,0:T(8,128)(2,1)S(1)}, bf16[64,2176]{1,0:T(8,128)(2,1)S(1)}, u32[]{:S(2)}, u32[]{:S(2)}) collective-permute-start(bf16[64,2176]{1,0:T(8,128)(2,1)S(1)} %fusion.3.refs_0_.refs_16_), channel_id=1, source_target_pairs={{0,4},{4,0},{8,12},{12,8},{1,5},{5,1},{9,13},{13,9},{2,6},{6,2},{1... | collective-permute-start | bytes 835592 | tf_op jit(solution)/shard_map/ppermute | solution.py:296
  127.7 12.1 %collective-permute-start.37 = (bf16[64,2176]{1,0:T(8,128)(2,1)S(1)}, bf16[64,2176]{1,0:T(8,128)(2,1)S(1)}, u32[]{:S(2)}, u32[]{:S(2)}) collective-permute-start(bf16[64,2176]{1,0:T(8,128)(2,1)S(1)} %collective-permute-done.36.refs_8_.refs_24_), channel_id=1, source_target_pairs={{0,4},{4,0},{8,12},{12,8},{1,5},{5,1},{9,13},{13,9},{2,6},{6,2},{1... | collective-permute-start | bytes 835592 | tf_op jit(solution)/shard_map/ppermute | solution.py:296
  130.2 13.1 %collective-permute-start.34 = (bf16[64,2176]{1,0:T(8,128)(2,1)S(1)}, bf16[64,2176]{1,0:T(8,128)(2,1)S(1)}, u32[]{:S(2)}, u32[]{:S(2)}) collective-permute-start(bf16[64,2176]{1,0:T(8,128)(2,1)S(1)} %collective-permute-done.30.refs_2_.refs_18_), channel_id=1, source_target_pairs={{0,1},{1,0},{2,3},{3,2},{4,5},{5,4},{6,7},{7,6},{8,9},{9,8},{10,11... | collective-permute-start | bytes 835592 | tf_op jit(solution)/shard_map/ppermute | solution.py:296
  132.2 17.0 %collective-permute-start.33 = (bf16[64,2176]{1,0:T(8,128)(2,1)S(1)}, bf16[64,2176]{1,0:T(8,128)(2,1)S(1)}, u32[]{:S(2)}, u32[]{:S(2)}) collective-permute-start(bf16[64,2176]{1,0:T(8,128)(2,1)S(1)} %collective-permute-done.29.refs_1_.refs_17_), channel_id=1, source_target_pairs={{0,1},{1,0},{2,3},{3,2},{4,5},{5,4},{6,7},{7,6},{8,9},{9,8},{10,11... | collective-permute-start | bytes 835592 | tf_op jit(solution)/shard_map/ppermute | solution.py:296
  137.3 11.9 %collective-permute-start.42 = (bf16[64,2176]{1,0:T(8,128)(2,1)S(1)}, bf16[64,2176]{1,0:T(8,128)(2,1)S(1)}, u32[]{:S(2)}, u32[]{:S(2)}) collective-permute-start(bf16[64,2176]{1,0:T(8,128)(2,1)S(1)} %collective-permute-done.40.refs_12_.refs_28_), channel_id=1, source_target_pairs={{0,8},{4,12},{8,0},{12,4},{1,9},{5,13},{9,1},{13,5},{2,10},{6,14},... | collective-permute-start | bytes 835592 | tf_op jit(solution)/shard_map/ppermute | solution.py:296
  137.3 14.5 %collective-permute-start.41 = (bf16[64,2176]{1,0:T(8,128)(2,1)S(1)}, bf16[64,2176]{1,0:T(8,128)(2,1)S(1)}, u32[]{:S(2)}, u32[]{:S(2)}) collective-permute-start(bf16[64,2176]{1,0:T(8,128)(2,1)S(1)} %collective-permute-done.40.refs_12_.refs_28_), channel_id=1, source_target_pairs={{0,4},{4,0},{8,12},{12,8},{1,5},{5,1},{9,13},{13,9},{2,6},{6,2},{1... | collective-permute-start | bytes 835592 | tf_op jit(solution)/shard_map/ppermute | solution.py:296
  139.8 13.9 %collective-permute-start.32 = (bf16[64,2176]{1,0:T(8,128)(2,1)S(1)}, bf16[64,2176]{1,0:T(8,128)(2,1)S(1)}, u32[]{:S(2)}, u32[]{:S(2)}) collective-permute-start(bf16[64,2176]{1,0:T(8,128)(2,1)S(1)} %fusion.3.refs_0_.refs_16_), channel_id=1, source_target_pairs={{0,1},{1,0},{2,3},{3,2},{4,5},{5,4},{6,7},{7,6},{8,9},{9,8},{10,11... | collective-permute-start | bytes 835592 | tf_op jit(solution)/shard_map/ppermute | solution.py:296
  180.3 15.2 %collective-permute-start.48 = (bf16[64,2176]{1,0:T(8,128)(2,1)}, bf16[64,2176]{1,0:T(8,128)(2,1)S(1)}, u32[]{:S(2)}, u32[]{:S(2)}) collective-permute-start(bf16[64,2176]{1,0:T(8,128)(2,1)} %get-tuple-element.24), channel_id=1, source_target_pairs={{0,4},{4,0},{8,12},{12,8},{1,5},{5,1},{9,13},{13,9},{2,6},{6,2},{1... | collective-permute-start | bytes 835592 | tf_op jit(solution)/shard_map/ppermute | solution.py:296
  182.3 15.2 %collective-permute-start.54 = (bf16[64,2176]{1,0:T(8,128)(2,1)}, bf16[64,2176]{1,0:T(8,128)(2,1)S(1)}, u32[]{:S(2)}, u32[]{:S(2)}) collective-permute-start(bf16[64,2176]{1,0:T(8,128)(2,1)} %get-tuple-element.29), channel_id=1, source_target_pairs={{0,8},{4,12},{8,0},{12,4},{1,9},{5,13},{9,1},{13,5},{2,10},{6,14},... | collective-permute-start | bytes 835592 | tf_op jit(solution)/shard_map/ppermute | solution.py:296
  (69 other events, 875.7 us)

commit v3 on v2

--- a/solution.py
+++ b/solution.py
@@ -338,21 +338,42 @@
     return total
 
 
+def result_blocks(rows):
+    quarter = 4 * rows
+    diag = [(3 * quarter + level * rows, rows) for level in range(4)]
+    sides = []
+    for start in (quarter, 2 * quarter):
+        sides += [(start + level * rows, rows) for level in range(4)]
+    own = [(0, 2 * rows), (2 * rows, rows), (3 * rows, rows)]
+    return tuple(diag + sides + own)
+
+
+def narrowed(value):
+    return value.astype(jnp.bfloat16)
+
+
 def brought_back(blocks):
-    diag_low, diag_high, first_low, first_high, second_low, second_high, own = blocks
-    rows = own.shape[0] // 4
-    got_low = toggled(diag_low, "group", 1)
-    got_high = toggled(diag_high, "group", 2)
-    from_second_high = toggled(second_high, "group", 2)
+    diag_0, diag_1, diag_2, diag_3 = blocks[:4]
+    first_0, first_1, first_2, first_3, second_0, second_1, second_2, second_3 = blocks[4:12]
+    own_low, own_2, own_3 = blocks[12:]
+    rows = diag_0.shape[0]
+    got_2 = toggled(diag_2, "group", 1)
+    got_3 = toggled(diag_3, "group", 2)
+    got_0 = toggled(diag_0, "group", 1)
+    got_1 = toggled(diag_1, "group", 2)
+    from_first_2 = toggled(first_2, "group", 1)
+    from_second_3 = toggled(second_3, "group", 2)
+    from_first_3 = toggled(narrowed(added(first_3, got_3)), "group", 1)
+    from_second_2 = toggled(narrowed(added(second_2, got_2)), "group", 2)
+    from_far = toggled(narrowed(added(own_2, from_first_2, from_second_2)), "local", 2)
+    from_corner = toggled(narrowed(added(own_3, from_first_3, from_second_3)), "local", 3)
+    first_low = jnp.concatenate([first_0, narrowed(added(first_1, got_1))])
+    second_low = jnp.concatenate([narrowed(added(second_0, got_0)), second_1])
     from_first_low = toggled(first_low, "group", 1)
-    from_first_high = toggled(added(first_high, got_high).astype(jnp.bfloat16), "group", 1)
-    from_second_low = toggled(added(second_low, got_low).astype(jnp.bfloat16), "group", 2)
-    high = added(own[2 * rows :], from_first_high, from_second_high)
-    low = added(own[: 2 * rows], from_first_low, from_second_low)
-    got_corner = toggled(high[rows:].astype(jnp.bfloat16), "local", 1)
-    got_far = toggled(added(high[:rows], got_corner).astype(jnp.bfloat16), "local", 2)
-    got_near = toggled(low[rows:].astype(jnp.bfloat16), "local", 1)
-    return added(low[:rows], got_near, got_far)
+    from_second_low = toggled(second_low, "group", 2)
+    low = added(own_low, from_first_low, from_second_low)
+    from_near = toggled(narrowed(low[rows:]), "local", 1)
+    return added(low[:rows], from_near, from_far, from_corner)
 
 
 def dense_local(
@@ -375,16 +396,7 @@
     token_probs = token_probs.astype(jnp.bfloat16)
     last_section = lax.axis_index("pipe") == lax.axis_size("pipe") - 1
     inputs = layer_inputs[0]
-    quarter = 4 * rows
-    blocks = (
-        (3 * quarter, 2 * rows),
-        (3 * quarter + 2 * rows, 2 * rows),
-        (quarter, 2 * rows),
-        (quarter + 2 * rows, 2 * rows),
-        (2 * quarter, 2 * rows),
-        (2 * quarter + 2 * rows, 2 * rows),
-        (0, quarter),
-    )
+    blocks = result_blocks(rows)
     weights = (gate_half, up_half, down_half)
     none = jnp.zeros((rows, LANES), jnp.bfloat16)
     earlier = carried_grad

time: 216 us -> 208 us (0.963)
  waiting for transfers between devices: 101 us -> 80.5 us
  starting transfers between devices: 68 us -> 74.9 us
  other arithmetic: 9.71 us -> 14.8 us
    ppermute x56 -> x64, waiting for transfers between devices: 99.2 us -> 78.8 us  [toggled(): return lax.ppermute(value, axis, pairs)]
    ppermute x56 -> x64, starting transfers between devices: 66.6 us -> 73.4 us  [toggled(): return lax.ppermute(value, axis, pairs)]
    concatenate x0 -> x4, other arithmetic: none -> 3.76 us  [the longest x2 1.9 us: brought_back(): second_low = jnp.concatenate([narrowed(added(second_0, got_0)), second_1])]
    convert_element_type x6 -> x12, other arithmetic: 4.23 us -> 7.76 us  [narrowed(): return value.astype(jnp.bfloat16)]
    add x4, other arithmetic: 2.54 us -> 0.31 us  [added(): total = total + value.astype(jnp.float32)]
  transfers between devices with their start and end apart: 57 -> 65, of which waited for: 36 -> 33; matrix products, arithmetic and copies ran while one was open for 2% -> 6% of each run, Pallas kernels for 0% -> 0%
where the time goes in v3:
time: 208 us; the launch traced here: 207 us
  waiting for transfers between devices  80.5 us (39%)
  starting transfers between devices  74.9 us (36%)
  Pallas kernels  31.9 us (15%)
  other arithmetic  14.8 us (7%)
  local copies, waits for them, and re-layouts  3.97 us (2%)
    ppermute x64, waiting for transfers between devices, toggled(): return lax.ppermute(value, axis, pairs)  78.8 us
    ppermute x64, starting transfers between devices, toggled(): return lax.ppermute(value, axis, pairs)  73.4 us
    pallas_call x2, Pallas kernels, expert_math(): pl.pallas_call(functools.partial(math_kernel, plan, grad_plan, blocks), o...  31.9 us
    convert_element_type x12, other arithmetic, narrowed(): return value.astype(jnp.bfloat16)  7.76 us
  transfers between devices with their start and end apart: 65, of which 33 were waited for; matrix products, arithmetic and copies ran while one was open for 6% of the time, Pallas kernels for 0%

profile of v3, /device:TPU:0, one launch (start us, length us, event | category | flops | bytes accessed | tf_op | source)
XLA Modules:
  0.0 207.4 jit_solution(2671854871258389401)
XLA Ops:
  4.2 4.1 %collective-permute-start.7 = (bf16[64,2176]{1,0:T(8,128)(2,1)S(1)}, bf16[64,2176]{1,0:T(8,128)(2,1)S(1)}, u32[]{:S(2)}, u32[]{:S(2)}) collective-permute-start(bf16[64,2176]{1,0:T(8,128)(2,1)S(1)} %fusion.2.refs_0_.refs_16_), channel_id=1, source_target_pairs={{0,2},{1,3},{2,0},{3,1},{4,6},{5,7},{6,4},{7,5},{8,10},{9,11},{10,... | collective-permute-start | bytes 835592 | tf_op jit(solution)/shard_map/ppermute | solution.py:296
  11.3 9.6 %collective-permute-done.7.refs_8_.refs_24_ = bf16[64,2176]{1,0:T(8,128)(2,1)S(1)} collective-permute-done((bf16[64,2176]{1,0:T(8,128)(2,1)S(1)}, bf16[64,2176]{1,0:T(8,128)(2,1)S(1)}, u32[]{:S(2)}, u32[]{:S(2)}) %collective-permute-start.7) | collective-permute-done | bytes 278560 | tf_op jit(solution)/shard_map/ppermute | solution.py:296
  26.7 3.8 %collective-permute-done.11.refs_12_.refs_28_ = bf16[64,2176]{1,0:T(8,128)(2,1)S(1)} collective-permute-done((bf16[64,2176]{1,0:T(8,128)(2,1)S(1)}, bf16[64,2176]{1,0:T(8,128)(2,1)S(1)}, u32[]{:S(2)}, u32[]{:S(2)}) %collective-permute-start.11) | collective-permute-done | bytes 278560 | tf_op jit(solution)/shard_map/ppermute | solution.py:296
  34.2 2.2 %collective-permute-done.5.refs_6_.refs_22_ = bf16[64,2176]{1,0:T(8,128)(2,1)S(1)} collective-permute-done((bf16[64,2176]{1,0:T(8,128)(2,1)S(1)}, bf16[64,2176]{1,0:T(8,128)(2,1)S(1)}, u32[]{:S(2)}, u32[]{:S(2)}) %collective-permute-start.5) | collective-permute-done | bytes 278560 | tf_op jit(solution)/shard_map/ppermute | solution.py:296
  38.0 4.4 %collective-permute-done.4.refs_5_.refs_21_ = bf16[64,2176]{1,0:T(8,128)(2,1)S(1)} collective-permute-done((bf16[64,2176]{1,0:T(8,128)(2,1)S(1)}, bf16[64,2176]{1,0:T(8,128)(2,1)S(1)}, u32[]{:S(2)}, u32[]{:S(2)}) %collective-permute-start.4) | collective-permute-done | bytes 278560 | tf_op jit(solution)/shard_map/ppermute | solution.py:296
  56.5 16.0 %expert_math.2 = (bf16[32,2176]{1,0:T(8,128)(2,1)}, bf16[32,2176]{1,0:T(8,128)(2,1)}, bf16[32,2176]{1,0:T(8,128)(2,1)}, bf16[32,2176]{1,0:T(8,128)(2,1)}, bf16[3...) custom-call(s32[1]{0:T(128)} %bitcast.1.expert_ref, ...), custom_call_target="tpu_custom_call" | custom-call | flops 7381975040 | bytes 14942208 | tf_op jit(solution)/shard_map/expert_math/pallas_call | solution.py:267
  76.3 1.8 collective-permute-start.28
  81.2 2.6 %collective-permute-done.28 = bf16[32,2176]{1,0:T(8,128)(2,1)S(1)} collective-permute-done((bf16[32,2176]{1,0:T(8,128)(2,1)}, bf16[32,2176]{1,0:T(8,128)(2,1)S(1)}, u32[]{:S(2)}, u32[]{:S(2)}) %collective-permute-start.28) | collective-permute-done | bytes 139296 | tf_op jit(solution)/shard_map/ppermute | solution.py:296
  92.9 2.7 %collective-permute-start.27 = (bf16[32,2176]{1,0:T(8,128)(2,1)S(1)}, bf16[32,2176]{1,0:T(8,128)(2,1)S(1)}, u32[]{:S(2)}, u32[]{:S(2)}) collective-permute-start(bf16[32,2176]{1,0:T(8,128)(2,1)S(1)} %add_convert_fusion.8), channel_id=1, source_target_pairs={{0,2},{1,3},{2,0},{3,1},{4,6},{5,7},{6,4},{7,5},{8,10},{9,11},{10,... | collective-permute-start | bytes 417800 | tf_op jit(solution)/shard_map/ppermute | solution.py:296
  100.4 2.6 %collective-permute-done.31 = bf16[32,2176]{1,0:T(8,128)(2,1)S(1)} collective-permute-done((bf16[32,2176]{1,0:T(8,128)(2,1)S(1)}, bf16[32,2176]{1,0:T(8,128)(2,1)S(1)}, u32[]{:S(2)}, u32[]{:S(2)}) %collective-permute-start.31) | collective-permute-done | bytes 139296 | tf_op jit(solution)/shard_map/ppermute | solution.py:296
  106.0 1.8 collective-permute-done.32
  107.8 2.0 collective-permute-start.40
  111.7 11.8 %collective-permute-done.40.refs_8_.refs_24_ = bf16[64,2176]{1,0:T(8,128)(2,1)S(1)} collective-permute-done((bf16[64,2176]{1,0:T(8,128)(2,1)S(1)}, bf16[64,2176]{1,0:T(8,128)(2,1)S(1)}, u32[]{:S(2)}, u32[]{:S(2)}) %collective-permute-start.40) | collective-permute-done | bytes 278560 | tf_op jit(solution)/shard_map/ppermute | solution.py:296
  125.4 2.0 collective-permute-start.38
  127.5 5.4 %collective-permute-done.44.refs_12_.refs_28_ = bf16[64,2176]{1,0:T(8,128)(2,1)S(1)} collective-permute-done((bf16[64,2176]{1,0:T(8,128)(2,1)S(1)}, bf16[64,2176]{1,0:T(8,128)(2,1)S(1)}, u32[]{:S(2)}, u32[]{:S(2)}) %collective-permute-start.44) | collective-permute-done | bytes 278560 | tf_op jit(solution)/shard_map/ppermute | solution.py:296
  135.1 3.9 %collective-permute-done.38.refs_6_.refs_22_ = bf16[64,2176]{1,0:T(8,128)(2,1)S(1)} collective-permute-done((bf16[64,2176]{1,0:T(8,128)(2,1)S(1)}, bf16[64,2176]{1,0:T(8,128)(2,1)S(1)}, u32[]{:S(2)}, u32[]{:S(2)}) %collective-permute-start.38) | collective-permute-done | bytes 278560 | tf_op jit(solution)/shard_map/ppermute | solution.py:296
  139.9 5.0 %collective-permute-done.37.refs_5_.refs_21_ = bf16[64,2176]{1,0:T(8,128)(2,1)S(1)} collective-permute-done((bf16[64,2176]{1,0:T(8,128)(2,1)S(1)}, bf16[64,2176]{1,0:T(8,128)(2,1)S(1)}, u32[]{:S(2)}, u32[]{:S(2)}) %collective-permute-start.37) | collective-permute-done | bytes 278560 | tf_op jit(solution)/shard_map/ppermute | solution.py:296
  153.9 2.0 collective-permute-done.49.refs_23_
  159.0 15.9 %expert_math.3 = (bf16[32,2176]{1,0:T(8,128)(2,1)}, bf16[32,2176]{1,0:T(8,128)(2,1)}, bf16[32,2176]{1,0:T(8,128)(2,1)}, bf16[32,2176]{1,0:T(8,128)(2,1)}, bf16[3...) custom-call(s32[1]{0:T(128)} %bitcast.1.expert_ref, ...), custom_call_target="tpu_custom_call" | custom-call | flops 7381975040 | bytes 14942208 | tf_op jit(solution)/shard_map/expert_math/pallas_call | solution.py:267
  180.0 1.8 collective-permute-done.58
  183.7 2.1 %collective-permute-done.61 = bf16[32,2176]{1,0:T(8,128)(2,1)S(1)} collective-permute-done((bf16[32,2176]{1,0:T(8,128)(2,1)}, bf16[32,2176]{1,0:T(8,128)(2,1)S(1)}, u32[]{:S(2)}, u32[]{:S(2)}) %collective-permute-start.61) | collective-permute-done | bytes 139296 | tf_op jit(solution)/shard_map/ppermute | solution.py:296
  194.9 2.2 %collective-permute-start.60 = (bf16[32,2176]{1,0:T(8,128)(2,1)S(1)}, bf16[32,2176]{1,0:T(8,128)(2,1)S(1)}, u32[]{:S(2)}, u32[]{:S(2)}) collective-permute-start(bf16[32,2176]{1,0:T(8,128)(2,1)S(1)} %add_convert_fusion.2), channel_id=1, source_target_pairs={{0,2},{1,3},{2,0},{3,1},{4,6},{5,7},{6,4},{7,5},{8,10},{9,11},{10,... | collective-permute-start | bytes 417800 | tf_op jit(solution)/shard_map/ppermute | solution.py:296
  198.3 2.0 collective-permute-done.53
  202.4 1.8 collective-permute-done.64
  (248 shorter events, 96.3 us)
Async XLA Ops:
  4.2 16.7 %collective-permute-start.7 = (bf16[64,2176]{1,0:T(8,128)(2,1)S(1)}, bf16[64,2176]{1,0:T(8,128)(2,1)S(1)}, u32[]{:S(2)}, u32[]{:S(2)}) collective-permute-start(bf16[64,2176]{1,0:T(8,128)(2,1)S(1)} %fusion.2.refs_0_.refs_16_), channel_id=1, source_target_pairs={{0,2},{1,3},{2,0},{3,1},{4,6},{5,7},{6,4},{7,5},{8,10},{9,11},{10,... | collective-permute-start | bytes 835592 | tf_op jit(solution)/shard_map/ppermute | solution.py:296
  8.3 16.3 %collective-permute-start.1 = (bf16[64,2176]{1,0:T(8,128)(2,1)S(1)}, bf16[64,2176]{1,0:T(8,128)(2,1)S(1)}, u32[]{:S(2)}, u32[]{:S(2)}) collective-permute-start(bf16[64,2176]{1,0:T(8,128)(2,1)S(1)} %fusion.2.refs_0_.refs_16_), channel_id=1, source_target_pairs={{0,8},{4,12},{8,0},{12,4},{1,9},{5,13},{9,1},{13,5},{2,10},{6,14},... | collective-permute-start | bytes 835592 | tf_op jit(solution)/shard_map/ppermute | solution.py:296
  9.9 16.1 %collective-permute-start = (bf16[64,2176]{1,0:T(8,128)(2,1)S(1)}, bf16[64,2176]{1,0:T(8,128)(2,1)S(1)}, u32[]{:S(2)}, u32[]{:S(2)}) collective-permute-start(bf16[64,2176]{1,0:T(8,128)(2,1)S(1)} %fusion.2.refs_0_.refs_16_), channel_id=1, source_target_pairs={{0,4},{4,0},{8,12},{12,8},{1,5},{5,1},{9,13},{13,9},{2,6},{6,2},{1... | collective-permute-start | bytes 835592 | tf_op jit(solution)/shard_map/ppermute | solution.py:296
  24.6 11.8 %collective-permute-start.5 = (bf16[64,2176]{1,0:T(8,128)(2,1)S(1)}, bf16[64,2176]{1,0:T(8,128)(2,1)S(1)}, u32[]{:S(2)}, u32[]{:S(2)}) collective-permute-start(bf16[64,2176]{1,0:T(8,128)(2,1)S(1)} %collective-permute-done.1.refs_2_.refs_18_), channel_id=1, source_target_pairs={{0,1},{1,0},{2,3},{3,2},{4,5},{5,4},{6,7},{7,6},{8,9},{9,8},{10,11... | collective-permute-start | bytes 835592 | tf_op jit(solution)/shard_map/ppermute | solution.py:296
  26.0 16.4 %collective-permute-start.4 = (bf16[64,2176]{1,0:T(8,128)(2,1)S(1)}, bf16[64,2176]{1,0:T(8,128)(2,1)S(1)}, u32[]{:S(2)}, u32[]{:S(2)}) collective-permute-start(bf16[64,2176]{1,0:T(8,128)(2,1)S(1)} %collective-permute-done.refs_1_.refs_17_), channel_id=1, source_target_pairs={{0,1},{1,0},{2,3},{3,2},{4,5},{5,4},{6,7},{7,6},{8,9},{9,8},{10,11... | collective-permute-start | bytes 835592 | tf_op jit(solution)/shard_map/ppermute | solution.py:296
  30.5 13.5 %collective-permute-start.13 = (bf16[64,2176]{1,0:T(8,128)(2,1)S(1)}, bf16[64,2176]{1,0:T(8,128)(2,1)S(1)}, u32[]{:S(2)}, u32[]{:S(2)}) collective-permute-start(bf16[64,2176]{1,0:T(8,128)(2,1)S(1)} %collective-permute-done.11.refs_12_.refs_28_), channel_id=1, source_target_pairs={{0,8},{4,12},{8,0},{12,4},{1,9},{5,13},{9,1},{13,5},{2,10},{6,14},... | collective-permute-start | bytes 835592 | tf_op jit(solution)/shard_map/ppermute | solution.py:296
  32.1 13.5 %collective-permute-start.12 = (bf16[64,2176]{1,0:T(8,128)(2,1)S(1)}, bf16[64,2176]{1,0:T(8,128)(2,1)S(1)}, u32[]{:S(2)}, u32[]{:S(2)}) collective-permute-start(bf16[64,2176]{1,0:T(8,128)(2,1)S(1)} %collective-permute-done.11.refs_12_.refs_28_), channel_id=1, source_target_pairs={{0,4},{4,0},{8,12},{12,8},{1,5},{5,1},{9,13},{13,9},{2,6},{6,2},{1... | collective-permute-start | bytes 835592 | tf_op jit(solution)/shard_map/ppermute | solution.py:296
  33.6 13.0 %collective-permute-start.3 = (bf16[64,2176]{1,0:T(8,128)(2,1)S(1)}, bf16[64,2176]{1,0:T(8,128)(2,1)S(1)}, u32[]{:S(2)}, u32[]{:S(2)}) collective-permute-start(bf16[64,2176]{1,0:T(8,128)(2,1)S(1)} %fusion.2.refs_0_.refs_16_), channel_id=1, source_target_pairs={{0,1},{1,0},{2,3},{3,2},{4,5},{5,4},{6,7},{7,6},{8,9},{9,8},{10,11... | collective-permute-start | bytes 835592 | tf_op jit(solution)/shard_map/ppermute | solution.py:296
  36.5 11.4 %collective-permute-start.15 = (bf16[32,2176]{1,0:T(8,128)(2,1)S(1)}, bf16[32,2176]{1,0:T(8,128)(2,1)S(1)}, u32[]{:S(2)}, u32[]{:S(2)}) collective-permute-start(bf16[32,2176]{1,0:T(8,128)(2,1)S(1)} %slice.129), channel_id=1, source_target_pairs={{0,4},{4,0},{8,12},{12,8},{1,5},{5,1},{9,13},{13,9},{2,6},{6,2},{1... | collective-permute-start | bytes 417800 | tf_op jit(solution)/shard_map/ppermute | solution.py:296
  74.1 14.4 %collective-permute-start.19 = (bf16[32,2176]{1,0:T(8,128)(2,1)}, bf16[32,2176]{1,0:T(8,128)(2,1)S(1)}, u32[]{:S(2)}, u32[]{:S(2)}) collective-permute-start(bf16[32,2176]{1,0:T(8,128)(2,1)} %get-tuple-element.35), channel_id=1, source_target_pairs={{0,8},{4,12},{8,0},{12,4},{1,9},{5,13},{9,1},{13,5},{2,10},{6,14},... | collective-permute-start | bytes 417800 | tf_op jit(solution)/shard_map/ppermute | solution.py:296
  75.5 15.8 %collective-permute-start.24 = (bf16[32,2176]{1,0:T(8,128)(2,1)}, bf16[32,2176]{1,0:T(8,128)(2,1)S(1)}, u32[]{:S(2)}, u32[]{:S(2)}) collective-permute-start(bf16[32,2176]{1,0:T(8,128)(2,1)} %get-tuple-element.40), channel_id=1, source_target_pairs={{0,4},{4,0},{8,12},{12,8},{1,5},{5,1},{9,13},{13,9},{2,6},{6,2},{1... | collective-permute-start | bytes 417800 | tf_op jit(solution)/shard_map/ppermute | solution.py:296
  79.4 16.3 %collective-permute-start.30 = (bf16[32,2176]{1,0:T(8,128)(2,1)}, bf16[32,2176]{1,0:T(8,128)(2,1)S(1)}, u32[]{:S(2)}, u32[]{:S(2)}) collective-permute-start(bf16[32,2176]{1,0:T(8,128)(2,1)} %get-tuple-element.46), channel_id=1, source_target_pairs={{0,8},{4,12},{8,0},{12,4},{1,9},{5,13},{9,1},{13,5},{2,10},{6,14},... | collective-permute-start | bytes 417800 | tf_op jit(solution)/shard_map/ppermute | solution.py:296
  107.8 15.6 %collective-permute-start.40 = (bf16[64,2176]{1,0:T(8,128)(2,1)S(1)}, bf16[64,2176]{1,0:T(8,128)(2,1)S(1)}, u32[]{:S(2)}, u32[]{:S(2)}) collective-permute-start(bf16[64,2176]{1,0:T(8,128)(2,1)S(1)} %fusion.3.refs_0_.refs_16_), channel_id=1, source_target_pairs={{0,2},{1,3},{2,0},{3,1},{4,6},{5,7},{6,4},{7,5},{8,10},{9,11},{10,... | collective-permute-start | bytes 835592 | tf_op jit(solution)/shard_map/ppermute | solution.py:296
  109.8 15.6 %collective-permute-start.34 = (bf16[64,2176]{1,0:T(8,128)(2,1)S(1)}, bf16[64,2176]{1,0:T(8,128)(2,1)S(1)}, u32[]{:S(2)}, u32[]{:S(2)}) collective-permute-start(bf16[64,2176]{1,0:T(8,128)(2,1)S(1)} %fusion.3.refs_0_.refs_16_), channel_id=1, source_target_pairs={{0,8},{4,12},{8,0},{12,4},{1,9},{5,13},{9,1},{13,5},{2,10},{6,14},... | collective-permute-start | bytes 835592 | tf_op jit(solution)/shard_map/ppermute | solution.py:296
  110.9 16.6 %collective-permute-start.33 = (bf16[64,2176]{1,0:T(8,128)(2,1)S(1)}, bf16[64,2176]{1,0:T(8,128)(2,1)S(1)}, u32[]{:S(2)}, u32[]{:S(2)}) collective-permute-start(bf16[64,2176]{1,0:T(8,128)(2,1)S(1)} %fusion.3.refs_0_.refs_16_), channel_id=1, source_target_pairs={{0,4},{4,0},{8,12},{12,8},{1,5},{5,1},{9,13},{13,9},{2,6},{6,2},{1... | collective-permute-start | bytes 835592 | tf_op jit(solution)/shard_map/ppermute | solution.py:296
  125.4 13.5 %collective-permute-start.38 = (bf16[64,2176]{1,0:T(8,128)(2,1)S(1)}, bf16[64,2176]{1,0:T(8,128)(2,1)S(1)}, u32[]{:S(2)}, u32[]{:S(2)}) collective-permute-start(bf16[64,2176]{1,0:T(8,128)(2,1)S(1)} %collective-permute-done.34.refs_2_.refs_18_), channel_id=1, source_target_pairs={{0,1},{1,0},{2,3},{3,2},{4,5},{5,4},{6,7},{7,6},{8,9},{9,8},{10,11... | collective-permute-start | bytes 835592 | tf_op jit(solution)/shard_map/ppermute | solution.py:296
  127.5 17.5 %collective-permute-start.37 = (bf16[64,2176]{1,0:T(8,128)(2,1)S(1)}, bf16[64,2176]{1,0:T(8,128)(2,1)S(1)}, u32[]{:S(2)}, u32[]{:S(2)}) collective-permute-start(bf16[64,2176]{1,0:T(8,128)(2,1)S(1)} %collective-permute-done.33.refs_1_.refs_17_), channel_id=1, source_target_pairs={{0,1},{1,0},{2,3},{3,2},{4,5},{5,4},{6,7},{7,6},{8,9},{9,8},{10,11... | collective-permute-start | bytes 835592 | tf_op jit(solution)/shard_map/ppermute | solution.py:296
  133.0 12.9 %collective-permute-start.46 = (bf16[64,2176]{1,0:T(8,128)(2,1)S(1)}, bf16[64,2176]{1,0:T(8,128)(2,1)S(1)}, u32[]{:S(2)}, u32[]{:S(2)}) collective-permute-start(bf16[64,2176]{1,0:T(8,128)(2,1)S(1)} %collective-permute-done.44.refs_12_.refs_28_), channel_id=1, source_target_pairs={{0,8},{4,12},{8,0},{12,4},{1,9},{5,13},{9,1},{13,5},{2,10},{6,14},... | collective-permute-start | bytes 835592 | tf_op jit(solution)/shard_map/ppermute | solution.py:296
  133.9 13.1 %collective-permute-start.45 = (bf16[64,2176]{1,0:T(8,128)(2,1)S(1)}, bf16[64,2176]{1,0:T(8,128)(2,1)S(1)}, u32[]{:S(2)}, u32[]{:S(2)}) collective-permute-start(bf16[64,2176]{1,0:T(8,128)(2,1)S(1)} %collective-permute-done.44.refs_12_.refs_28_), channel_id=1, source_target_pairs={{0,4},{4,0},{8,12},{12,8},{1,5},{5,1},{9,13},{13,9},{2,6},{6,2},{1... | collective-permute-start | bytes 835592 | tf_op jit(solution)/shard_map/ppermute | solution.py:296
  135.0 14.8 %collective-permute-start.36 = (bf16[64,2176]{1,0:T(8,128)(2,1)S(1)}, bf16[64,2176]{1,0:T(8,128)(2,1)S(1)}, u32[]{:S(2)}, u32[]{:S(2)}) collective-permute-start(bf16[64,2176]{1,0:T(8,128)(2,1)S(1)} %fusion.3.refs_0_.refs_16_), channel_id=1, source_target_pairs={{0,1},{1,0},{2,3},{3,2},{4,5},{5,4},{6,7},{7,6},{8,9},{9,8},{10,11... | collective-permute-start | bytes 835592 | tf_op jit(solution)/shard_map/ppermute | solution.py:296
  139.0 11.3 %collective-permute-start.48 = (bf16[32,2176]{1,0:T(8,128)(2,1)S(1)}, bf16[32,2176]{1,0:T(8,128)(2,1)S(1)}, u32[]{:S(2)}, u32[]{:S(2)}) collective-permute-start(bf16[32,2176]{1,0:T(8,128)(2,1)S(1)} %slice.141), channel_id=1, source_target_pairs={{0,4},{4,0},{8,12},{12,8},{1,5},{5,1},{9,13},{13,9},{2,6},{6,2},{1... | collective-permute-start | bytes 417800 | tf_op jit(solution)/shard_map/ppermute | solution.py:296
  175.9 14.8 %collective-permute-start.52 = (bf16[32,2176]{1,0:T(8,128)(2,1)}, bf16[32,2176]{1,0:T(8,128)(2,1)S(1)}, u32[]{:S(2)}, u32[]{:S(2)}) collective-permute-start(bf16[32,2176]{1,0:T(8,128)(2,1)} %get-tuple-element.50), channel_id=1, source_target_pairs={{0,8},{4,12},{8,0},{12,4},{1,9},{5,13},{9,1},{13,5},{2,10},{6,14},... | collective-permute-start | bytes 417800 | tf_op jit(solution)/shard_map/ppermute | solution.py:296
  178.0 15.7 %collective-permute-start.57 = (bf16[32,2176]{1,0:T(8,128)(2,1)}, bf16[32,2176]{1,0:T(8,128)(2,1)S(1)}, u32[]{:S(2)}, u32[]{:S(2)}) collective-permute-start(bf16[32,2176]{1,0:T(8,128)(2,1)} %get-tuple-element.55), channel_id=1, source_target_pairs={{0,4},{4,0},{8,12},{12,8},{1,5},{5,1},{9,13},{13,9},{2,6},{6,2},{1... | collective-permute-start | bytes 417800 | tf_op jit(solution)/shard_map/ppermute | solution.py:296
  181.8 15.3 %collective-permute-start.63 = (bf16[32,2176]{1,0:T(8,128)(2,1)}, bf16[32,2176]{1,0:T(8,128)(2,1)S(1)}, u32[]{:S(2)}, u32[]{:S(2)}) collective-permute-start(bf16[32,2176]{1,0:T(8,128)(2,1)} %get-tuple-element.61), channel_id=1, source_target_pairs={{0,8},{4,12},{8,0},{12,4},{1,9},{5,13},{9,1},{13,5},{2,10},{6,14},... | collective-permute-start | bytes 417800 | tf_op jit(solution)/shard_map/ppermute | solution.py:296
  (83 other events, 1055.7 us)

commit v4 on v3

--- a/solution.py
+++ b/solution.py
@@ -160,7 +160,7 @@
     return (jnp.stack(grads_out)[None], jnp.stack(gates_out)[None])
 
 
-VMEM_LIMIT = 58 * 2**20
+VMEM_LIMIT = 50 * 2**20
 WIDTH_TILE = 512
 LANES = 128
 

time: 208 us -> 196 us (0.942)
  other arithmetic: 14.8 us -> 3.84 us
  Pallas kernels: 31.9 us -> 28.2 us
  starting transfers between devices: 74.9 us -> 78.6 us
    convert_element_type x12, other arithmetic: 7.76 us -> 0.5 us  [narrowed(): return value.astype(jnp.bfloat16)]
    ppermute x64, starting transfers between devices: 73.4 us -> 77.1 us  [toggled(): return lax.ppermute(value, axis, pairs)]
    pallas_call x2, Pallas kernels: 31.9 us -> 28.2 us  [expert_math(): pl.pallas_call(functools.partial(math_kernel, plan, grad_plan, blocks), o...]
  transfers between devices with their start and end apart: 65 -> 65, of which waited for: 33 -> 33; matrix products, arithmetic and copies ran while one was open for 6% -> 1% of each run, Pallas kernels for 0% -> 0%
where the time goes in v4:
time: 196 us
  waiting for transfers between devices  81.6 us (42%)
  starting transfers between devices  78.6 us (40%)
  Pallas kernels  28.2 us (14%)
  other arithmetic  3.84 us (2%)
  local copies, waits for them, and re-layouts  2.58 us (1%)
    ppermute x64, waiting for transfers between devices, toggled(): return lax.ppermute(value, axis, pairs)  79.8 us
    ppermute x64, starting transfers between devices, toggled(): return lax.ppermute(value, axis, pairs)  77.1 us
    pallas_call x2, Pallas kernels, expert_math(): pl.pallas_call(functools.partial(math_kernel, plan, grad_plan, blocks), o...  28.2 us
  transfers between devices with their start and end apart: 65, of which 33 were waited for; matrix products, arithmetic and copies ran while one was open for 1% of the time, Pallas kernels for 0%

profile of v4, /device:TPU:0, one launch (start us, length us, event | category | flops | bytes accessed | tf_op | source)
XLA Modules:
  0.0 196.0 jit_solution(1372326796777463117)
XLA Ops:
  4.2 4.1 %collective-permute-start.7 = (bf16[64,2176]{1,0:T(8,128)(2,1)S(1)}, bf16[64,2176]{1,0:T(8,128)(2,1)S(1)}, u32[]{:S(2)}, u32[]{:S(2)}) collective-permute-start(bf16[64,2176]{1,0:T(8,128)(2,1)S(1)} %fusion.2.refs_0_.refs_16_), channel_id=1, source_target_pairs={{0,2},{1,3},{2,0},{3,1},{4,6},{5,7},{6,4},{7,5},{8,10},{9,11},{10,... | collective-permute-start | bytes 835592 | tf_op jit(solution)/shard_map/ppermute | solution.py:296
  11.3 9.6 %collective-permute-done.7.refs_8_.refs_24_ = bf16[64,2176]{1,0:T(8,128)(2,1)S(1)} collective-permute-done((bf16[64,2176]{1,0:T(8,128)(2,1)S(1)}, bf16[64,2176]{1,0:T(8,128)(2,1)S(1)}, u32[]{:S(2)}, u32[]{:S(2)}) %collective-permute-start.7) | collective-permute-done | bytes 278560 | tf_op jit(solution)/shard_map/ppermute | solution.py:296
  26.7 3.8 %collective-permute-done.11.refs_12_.refs_28_ = bf16[64,2176]{1,0:T(8,128)(2,1)S(1)} collective-permute-done((bf16[64,2176]{1,0:T(8,128)(2,1)S(1)}, bf16[64,2176]{1,0:T(8,128)(2,1)S(1)}, u32[]{:S(2)}, u32[]{:S(2)}) %collective-permute-start.11) | collective-permute-done | bytes 278560 | tf_op jit(solution)/shard_map/ppermute | solution.py:296
  34.2 2.2 %collective-permute-done.5.refs_6_.refs_22_ = bf16[64,2176]{1,0:T(8,128)(2,1)S(1)} collective-permute-done((bf16[64,2176]{1,0:T(8,128)(2,1)S(1)}, bf16[64,2176]{1,0:T(8,128)(2,1)S(1)}, u32[]{:S(2)}, u32[]{:S(2)}) %collective-permute-start.5) | collective-permute-done | bytes 278560 | tf_op jit(solution)/shard_map/ppermute | solution.py:296
  38.0 4.4 %collective-permute-done.4.refs_5_.refs_21_ = bf16[64,2176]{1,0:T(8,128)(2,1)S(1)} collective-permute-done((bf16[64,2176]{1,0:T(8,128)(2,1)S(1)}, bf16[64,2176]{1,0:T(8,128)(2,1)S(1)}, u32[]{:S(2)}, u32[]{:S(2)}) %collective-permute-start.4) | collective-permute-done | bytes 278560 | tf_op jit(solution)/shard_map/ppermute | solution.py:296
  56.1 14.1 %expert_math.2 = (bf16[32,2176]{1,0:T(8,128)(2,1)S(1)}, bf16[32,2176]{1,0:T(8,128)(2,1)S(1)}, bf16[32,2176]{1,0:T(8,128)(2,1)S(1)}, bf16[32,2176]{1,0:T(8,128)(2...) custom-call(s32[1]{0:T(128)} %bitcast.1.expert_ref, ...), custom_call_target="tpu_custom_call" | custom-call | flops 7381975040 | bytes 14942208 | tf_op jit(solution)/shard_map/expert_math/pallas_call | solution.py:267
  78.0 2.8 %collective-permute-done.28 = bf16[32,2176]{1,0:T(8,128)(2,1)S(1)} collective-permute-done((bf16[32,2176]{1,0:T(8,128)(2,1)S(1)}, bf16[32,2176]{1,0:T(8,128)(2,1)S(1)}, u32[]{:S(2)}, u32[]{:S(2)}) %collective-permute-start.28) | collective-permute-done | bytes 139296 | tf_op jit(solution)/shard_map/ppermute | solution.py:296
  85.3 2.1 %collective-permute-done.26 = bf16[32,2176]{1,0:T(8,128)(2,1)S(1)} collective-permute-done((bf16[32,2176]{1,0:T(8,128)(2,1)S(1)}, bf16[32,2176]{1,0:T(8,128)(2,1)S(1)}, u32[]{:S(2)}, u32[]{:S(2)}) %collective-permute-start.26) | collective-permute-done | bytes 139296 | tf_op jit(solution)/shard_map/ppermute | solution.py:296
  87.5 3.0 %collective-permute-start.27 = (bf16[32,2176]{1,0:T(8,128)(2,1)S(1)}, bf16[32,2176]{1,0:T(8,128)(2,1)S(1)}, u32[]{:S(2)}, u32[]{:S(2)}) collective-permute-start(bf16[32,2176]{1,0:T(8,128)(2,1)S(1)} %add_convert_fusion.8), channel_id=1, source_target_pairs={{0,2},{1,3},{2,0},{3,1},{4,6},{5,7},{6,4},{7,5},{8,10},{9,11},{10,... | collective-permute-start | bytes 417800 | tf_op jit(solution)/shard_map/ppermute | solution.py:296
  92.5 3.1 %collective-permute-done.27 = bf16[32,2176]{1,0:T(8,128)(2,1)S(1)} collective-permute-done((bf16[32,2176]{1,0:T(8,128)(2,1)S(1)}, bf16[32,2176]{1,0:T(8,128)(2,1)S(1)}, u32[]{:S(2)}, u32[]{:S(2)}) %collective-permute-start.27) | collective-permute-done | bytes 139296 | tf_op jit(solution)/shard_map/ppermute | solution.py:296
  95.6 2.1 %collective-permute-done.31 = bf16[32,2176]{1,0:T(8,128)(2,1)S(1)} collective-permute-done((bf16[32,2176]{1,0:T(8,128)(2,1)S(1)}, bf16[32,2176]{1,0:T(8,128)(2,1)S(1)}, u32[]{:S(2)}, u32[]{:S(2)}) %collective-permute-start.31) | collective-permute-done | bytes 139296 | tf_op jit(solution)/shard_map/ppermute | solution.py:296
  101.8 2.5 %collective-permute-start.40 = (bf16[64,2176]{1,0:T(8,128)(2,1)S(1)}, bf16[64,2176]{1,0:T(8,128)(2,1)S(1)}, u32[]{:S(2)}, u32[]{:S(2)}) collective-permute-start(bf16[64,2176]{1,0:T(8,128)(2,1)S(1)} %fusion.3.refs_0_.refs_16_), channel_id=1, source_target_pairs={{0,2},{1,3},{2,0},{3,1},{4,6},{5,7},{6,4},{7,5},{8,10},{9,11},{10,... | collective-permute-start | bytes 835592 | tf_op jit(solution)/shard_map/ppermute | solution.py:296
  106.6 10.8 %collective-permute-done.40.refs_8_.refs_24_ = bf16[64,2176]{1,0:T(8,128)(2,1)S(1)} collective-permute-done((bf16[64,2176]{1,0:T(8,128)(2,1)S(1)}, bf16[64,2176]{1,0:T(8,128)(2,1)S(1)}, u32[]{:S(2)}, u32[]{:S(2)}) %collective-permute-start.40) | collective-permute-done | bytes 278560 | tf_op jit(solution)/shard_map/ppermute | solution.py:296
  122.3 4.8 %collective-permute-done.44.refs_12_.refs_28_ = bf16[64,2176]{1,0:T(8,128)(2,1)S(1)} collective-permute-done((bf16[64,2176]{1,0:T(8,128)(2,1)S(1)}, bf16[64,2176]{1,0:T(8,128)(2,1)S(1)}, u32[]{:S(2)}, u32[]{:S(2)}) %collective-permute-start.44) | collective-permute-done | bytes 278560 | tf_op jit(solution)/shard_map/ppermute | solution.py:296
  129.8 3.2 %collective-permute-done.38.refs_6_.refs_22_ = bf16[64,2176]{1,0:T(8,128)(2,1)S(1)} collective-permute-done((bf16[64,2176]{1,0:T(8,128)(2,1)S(1)}, bf16[64,2176]{1,0:T(8,128)(2,1)S(1)}, u32[]{:S(2)}, u32[]{:S(2)}) %collective-permute-start.38) | collective-permute-done | bytes 278560 | tf_op jit(solution)/shard_map/ppermute | solution.py:296
  134.5 4.5 %collective-permute-done.37.refs_5_.refs_21_ = bf16[64,2176]{1,0:T(8,128)(2,1)S(1)} collective-permute-done((bf16[64,2176]{1,0:T(8,128)(2,1)S(1)}, bf16[64,2176]{1,0:T(8,128)(2,1)S(1)}, u32[]{:S(2)}, u32[]{:S(2)}) %collective-permute-start.37) | collective-permute-done | bytes 278560 | tf_op jit(solution)/shard_map/ppermute | solution.py:296
  147.4 2.2 %collective-permute-done.49.refs_23_ = bf16[32,2176]{1,0:T(8,128)(2,1)S(1)} collective-permute-done((bf16[32,2176]{1,0:T(8,128)(2,1)S(1)}, bf16[32,2176]{1,0:T(8,128)(2,1)S(1)}, u32[]{:S(2)}, u32[]{:S(2)}) %collective-permute-start.49) | collective-permute-done | bytes 139296 | tf_op jit(solution)/shard_map/ppermute | solution.py:296
  152.4 14.1 %expert_math.3 = (bf16[32,2176]{1,0:T(8,128)(2,1)S(1)}, bf16[32,2176]{1,0:T(8,128)(2,1)S(1)}, bf16[32,2176]{1,0:T(8,128)(2,1)S(1)}, bf16[32,2176]{1,0:T(8,128)(2...) custom-call(s32[1]{0:T(128)} %bitcast.1.expert_ref, ...), custom_call_target="tpu_custom_call" | custom-call | flops 7381975040 | bytes 14942208 | tf_op jit(solution)/shard_map/expert_math/pallas_call | solution.py:267
  174.5 2.6 %collective-permute-done.61 = bf16[32,2176]{1,0:T(8,128)(2,1)S(1)} collective-permute-done((bf16[32,2176]{1,0:T(8,128)(2,1)S(1)}, bf16[32,2176]{1,0:T(8,128)(2,1)S(1)}, u32[]{:S(2)}, u32[]{:S(2)}) %collective-permute-start.61) | collective-permute-done | bytes 139296 | tf_op jit(solution)/shard_map/ppermute | solution.py:296
  178.8 1.8 collective-permute-start.55
  181.6 2.2 %collective-permute-done.59 = bf16[32,2176]{1,0:T(8,128)(2,1)S(1)} collective-permute-done((bf16[32,2176]{1,0:T(8,128)(2,1)S(1)}, bf16[32,2176]{1,0:T(8,128)(2,1)S(1)}, u32[]{:S(2)}, u32[]{:S(2)}) %collective-permute-start.59) | collective-permute-done | bytes 139296 | tf_op jit(solution)/shard_map/ppermute | solution.py:296
  183.8 2.9 %collective-permute-start.60 = (bf16[32,2176]{1,0:T(8,128)(2,1)S(1)}, bf16[32,2176]{1,0:T(8,128)(2,1)S(1)}, u32[]{:S(2)}, u32[]{:S(2)}) collective-permute-start(bf16[32,2176]{1,0:T(8,128)(2,1)S(1)} %add_convert_fusion.2), channel_id=1, source_target_pairs={{0,2},{1,3},{2,0},{3,1},{4,6},{5,7},{6,4},{7,5},{8,10},{9,11},{10,... | collective-permute-start | bytes 417800 | tf_op jit(solution)/shard_map/ppermute | solution.py:296
  188.4 3.0 %collective-permute-done.60 = bf16[32,2176]{1,0:T(8,128)(2,1)S(1)} collective-permute-done((bf16[32,2176]{1,0:T(8,128)(2,1)S(1)}, bf16[32,2176]{1,0:T(8,128)(2,1)S(1)}, u32[]{:S(2)}, u32[]{:S(2)}) %collective-permute-start.60) | collective-permute-done | bytes 139296 | tf_op jit(solution)/shard_map/ppermute | solution.py:296
  191.3 2.5 %collective-permute-done.64 = bf16[32,2176]{1,0:T(8,128)(2,1)S(1)} collective-permute-done((bf16[32,2176]{1,0:T(8,128)(2,1)S(1)}, bf16[32,2176]{1,0:T(8,128)(2,1)S(1)}, u32[]{:S(2)}, u32[]{:S(2)}) %collective-permute-start.64) | collective-permute-done | bytes 139296 | tf_op jit(solution)/shard_map/ppermute | solution.py:296
  (206 shorter events, 86.5 us)
Async XLA Ops:
  4.2 16.7 %collective-permute-start.7 = (bf16[64,2176]{1,0:T(8,128)(2,1)S(1)}, bf16[64,2176]{1,0:T(8,128)(2,1)S(1)}, u32[]{:S(2)}, u32[]{:S(2)}) collective-permute-start(bf16[64,2176]{1,0:T(8,128)(2,1)S(1)} %fusion.2.refs_0_.refs_16_), channel_id=1, source_target_pairs={{0,2},{1,3},{2,0},{3,1},{4,6},{5,7},{6,4},{7,5},{8,10},{9,11},{10,... | collective-permute-start | bytes 835592 | tf_op jit(solution)/shard_map/ppermute | solution.py:296
  8.3 16.3 %collective-permute-start.1 = (bf16[64,2176]{1,0:T(8,128)(2,1)S(1)}, bf16[64,2176]{1,0:T(8,128)(2,1)S(1)}, u32[]{:S(2)}, u32[]{:S(2)}) collective-permute-start(bf16[64,2176]{1,0:T(8,128)(2,1)S(1)} %fusion.2.refs_0_.refs_16_), channel_id=1, source_target_pairs={{0,8},{4,12},{8,0},{12,4},{1,9},{5,13},{9,1},{13,5},{2,10},{6,14},... | collective-permute-start | bytes 835592 | tf_op jit(solution)/shard_map/ppermute | solution.py:296
  9.8 16.1 %collective-permute-start = (bf16[64,2176]{1,0:T(8,128)(2,1)S(1)}, bf16[64,2176]{1,0:T(8,128)(2,1)S(1)}, u32[]{:S(2)}, u32[]{:S(2)}) collective-permute-start(bf16[64,2176]{1,0:T(8,128)(2,1)S(1)} %fusion.2.refs_0_.refs_16_), channel_id=1, source_target_pairs={{0,4},{4,0},{8,12},{12,8},{1,5},{5,1},{9,13},{13,9},{2,6},{6,2},{1... | collective-permute-start | bytes 835592 | tf_op jit(solution)/shard_map/ppermute | solution.py:296
  24.6 11.8 %collective-permute-start.5 = (bf16[64,2176]{1,0:T(8,128)(2,1)S(1)}, bf16[64,2176]{1,0:T(8,128)(2,1)S(1)}, u32[]{:S(2)}, u32[]{:S(2)}) collective-permute-start(bf16[64,2176]{1,0:T(8,128)(2,1)S(1)} %collective-permute-done.1.refs_2_.refs_18_), channel_id=1, source_target_pairs={{0,1},{1,0},{2,3},{3,2},{4,5},{5,4},{6,7},{7,6},{8,9},{9,8},{10,11... | collective-permute-start | bytes 835592 | tf_op jit(solution)/shard_map/ppermute | solution.py:296
  26.0 16.4 %collective-permute-start.4 = (bf16[64,2176]{1,0:T(8,128)(2,1)S(1)}, bf16[64,2176]{1,0:T(8,128)(2,1)S(1)}, u32[]{:S(2)}, u32[]{:S(2)}) collective-permute-start(bf16[64,2176]{1,0:T(8,128)(2,1)S(1)} %collective-permute-done.refs_1_.refs_17_), channel_id=1, source_target_pairs={{0,1},{1,0},{2,3},{3,2},{4,5},{5,4},{6,7},{7,6},{8,9},{9,8},{10,11... | collective-permute-start | bytes 835592 | tf_op jit(solution)/shard_map/ppermute | solution.py:296
  30.5 13.5 %collective-permute-start.13 = (bf16[64,2176]{1,0:T(8,128)(2,1)S(1)}, bf16[64,2176]{1,0:T(8,128)(2,1)S(1)}, u32[]{:S(2)}, u32[]{:S(2)}) collective-permute-start(bf16[64,2176]{1,0:T(8,128)(2,1)S(1)} %collective-permute-done.11.refs_12_.refs_28_), channel_id=1, source_target_pairs={{0,8},{4,12},{8,0},{12,4},{1,9},{5,13},{9,1},{13,5},{2,10},{6,14},... | collective-permute-start | bytes 835592 | tf_op jit(solution)/shard_map/ppermute | solution.py:296
  32.1 13.5 %collective-permute-start.12 = (bf16[64,2176]{1,0:T(8,128)(2,1)S(1)}, bf16[64,2176]{1,0:T(8,128)(2,1)S(1)}, u32[]{:S(2)}, u32[]{:S(2)}) collective-permute-start(bf16[64,2176]{1,0:T(8,128)(2,1)S(1)} %collective-permute-done.11.refs_12_.refs_28_), channel_id=1, source_target_pairs={{0,4},{4,0},{8,12},{12,8},{1,5},{5,1},{9,13},{13,9},{2,6},{6,2},{1... | collective-permute-start | bytes 835592 | tf_op jit(solution)/shard_map/ppermute | solution.py:296
  33.6 13.0 %collective-permute-start.3 = (bf16[64,2176]{1,0:T(8,128)(2,1)S(1)}, bf16[64,2176]{1,0:T(8,128)(2,1)S(1)}, u32[]{:S(2)}, u32[]{:S(2)}) collective-permute-start(bf16[64,2176]{1,0:T(8,128)(2,1)S(1)} %fusion.2.refs_0_.refs_16_), channel_id=1, source_target_pairs={{0,1},{1,0},{2,3},{3,2},{4,5},{5,4},{6,7},{7,6},{8,9},{9,8},{10,11... | collective-permute-start | bytes 835592 | tf_op jit(solution)/shard_map/ppermute | solution.py:296
  36.5 11.4 %collective-permute-start.15 = (bf16[32,2176]{1,0:T(8,128)(2,1)S(1)}, bf16[32,2176]{1,0:T(8,128)(2,1)S(1)}, u32[]{:S(2)}, u32[]{:S(2)}) collective-permute-start(bf16[32,2176]{1,0:T(8,128)(2,1)S(1)} %slice.129), channel_id=1, source_target_pairs={{0,4},{4,0},{8,12},{12,8},{1,5},{5,1},{9,13},{13,9},{2,6},{6,2},{1... | collective-permute-start | bytes 417800 | tf_op jit(solution)/shard_map/ppermute | solution.py:296
  71.4 11.8 %collective-permute-start.19 = (bf16[32,2176]{1,0:T(8,128)(2,1)S(1)}, bf16[32,2176]{1,0:T(8,128)(2,1)S(1)}, u32[]{:S(2)}, u32[]{:S(2)}) collective-permute-start(bf16[32,2176]{1,0:T(8,128)(2,1)S(1)} %get-tuple-element.35), channel_id=1, source_target_pairs={{0,8},{4,12},{8,0},{12,4},{1,9},{5,13},{9,1},{13,5},{2,10},{6,14},... | collective-permute-start | bytes 417800 | tf_op jit(solution)/shard_map/ppermute | solution.py:296
  73.4 11.0 %collective-permute-start.24 = (bf16[32,2176]{1,0:T(8,128)(2,1)S(1)}, bf16[32,2176]{1,0:T(8,128)(2,1)S(1)}, u32[]{:S(2)}, u32[]{:S(2)}) collective-permute-start(bf16[32,2176]{1,0:T(8,128)(2,1)S(1)} %get-tuple-element.40), channel_id=1, source_target_pairs={{0,4},{4,0},{8,12},{12,8},{1,5},{5,1},{9,13},{13,9},{2,6},{6,2},{1... | collective-permute-start | bytes 417800 | tf_op jit(solution)/shard_map/ppermute | solution.py:296
  76.8 13.7 %collective-permute-start.30 = (bf16[32,2176]{1,0:T(8,128)(2,1)S(1)}, bf16[32,2176]{1,0:T(8,128)(2,1)S(1)}, u32[]{:S(2)}, u32[]{:S(2)}) collective-permute-start(bf16[32,2176]{1,0:T(8,128)(2,1)S(1)} %get-tuple-element.46), channel_id=1, source_target_pairs={{0,8},{4,12},{8,0},{12,4},{1,9},{5,13},{9,1},{13,5},{2,10},{6,14},... | collective-permute-start | bytes 417800 | tf_op jit(solution)/shard_map/ppermute | solution.py:296
  101.8 15.6 %collective-permute-start.40 = (bf16[64,2176]{1,0:T(8,128)(2,1)S(1)}, bf16[64,2176]{1,0:T(8,128)(2,1)S(1)}, u32[]{:S(2)}, u32[]{:S(2)}) collective-permute-start(bf16[64,2176]{1,0:T(8,128)(2,1)S(1)} %fusion.3.refs_0_.refs_16_), channel_id=1, source_target_pairs={{0,2},{1,3},{2,0},{3,1},{4,6},{5,7},{6,4},{7,5},{8,10},{9,11},{10,... | collective-permute-start | bytes 835592 | tf_op jit(solution)/shard_map/ppermute | solution.py:296
  104.3 16.0 %collective-permute-start.34 = (bf16[64,2176]{1,0:T(8,128)(2,1)S(1)}, bf16[64,2176]{1,0:T(8,128)(2,1)S(1)}, u32[]{:S(2)}, u32[]{:S(2)}) collective-permute-start(bf16[64,2176]{1,0:T(8,128)(2,1)S(1)} %fusion.3.refs_0_.refs_16_), channel_id=1, source_target_pairs={{0,8},{4,12},{8,0},{12,4},{1,9},{5,13},{9,1},{13,5},{2,10},{6,14},... | collective-permute-start | bytes 835592 | tf_op jit(solution)/shard_map/ppermute | solution.py:296
  105.4 16.2 %collective-permute-start.33 = (bf16[64,2176]{1,0:T(8,128)(2,1)S(1)}, bf16[64,2176]{1,0:T(8,128)(2,1)S(1)}, u32[]{:S(2)}, u32[]{:S(2)}) collective-permute-start(bf16[64,2176]{1,0:T(8,128)(2,1)S(1)} %fusion.3.refs_0_.refs_16_), channel_id=1, source_target_pairs={{0,4},{4,0},{8,12},{12,8},{1,5},{5,1},{9,13},{13,9},{2,6},{6,2},{1... | collective-permute-start | bytes 835592 | tf_op jit(solution)/shard_map/ppermute | solution.py:296
  120.2 12.8 %collective-permute-start.38 = (bf16[64,2176]{1,0:T(8,128)(2,1)S(1)}, bf16[64,2176]{1,0:T(8,128)(2,1)S(1)}, u32[]{:S(2)}, u32[]{:S(2)}) collective-permute-start(bf16[64,2176]{1,0:T(8,128)(2,1)S(1)} %collective-permute-done.34.refs_2_.refs_18_), channel_id=1, source_target_pairs={{0,1},{1,0},{2,3},{3,2},{4,5},{5,4},{6,7},{7,6},{8,9},{9,8},{10,11... | collective-permute-start | bytes 835592 | tf_op jit(solution)/shard_map/ppermute | solution.py:296
  121.6 17.4 %collective-permute-start.37 = (bf16[64,2176]{1,0:T(8,128)(2,1)S(1)}, bf16[64,2176]{1,0:T(8,128)(2,1)S(1)}, u32[]{:S(2)}, u32[]{:S(2)}) collective-permute-start(bf16[64,2176]{1,0:T(8,128)(2,1)S(1)} %collective-permute-done.33.refs_1_.refs_17_), channel_id=1, source_target_pairs={{0,1},{1,0},{2,3},{3,2},{4,5},{5,4},{6,7},{7,6},{8,9},{9,8},{10,11... | collective-permute-start | bytes 835592 | tf_op jit(solution)/shard_map/ppermute | solution.py:296
  127.0 13.0 %collective-permute-start.46 = (bf16[64,2176]{1,0:T(8,128)(2,1)S(1)}, bf16[64,2176]{1,0:T(8,128)(2,1)S(1)}, u32[]{:S(2)}, u32[]{:S(2)}) collective-permute-start(bf16[64,2176]{1,0:T(8,128)(2,1)S(1)} %collective-permute-done.44.refs_12_.refs_28_), channel_id=1, source_target_pairs={{0,8},{4,12},{8,0},{12,4},{1,9},{5,13},{9,1},{13,5},{2,10},{6,14},... | collective-permute-start | bytes 835592 | tf_op jit(solution)/shard_map/ppermute | solution.py:296
  128.1 13.1 %collective-permute-start.45 = (bf16[64,2176]{1,0:T(8,128)(2,1)S(1)}, bf16[64,2176]{1,0:T(8,128)(2,1)S(1)}, u32[]{:S(2)}, u32[]{:S(2)}) collective-permute-start(bf16[64,2176]{1,0:T(8,128)(2,1)S(1)} %collective-permute-done.44.refs_12_.refs_28_), channel_id=1, source_target_pairs={{0,4},{4,0},{8,12},{12,8},{1,5},{5,1},{9,13},{13,9},{2,6},{6,2},{1... | collective-permute-start | bytes 835592 | tf_op jit(solution)/shard_map/ppermute | solution.py:296
  129.2 14.1 %collective-permute-start.36 = (bf16[64,2176]{1,0:T(8,128)(2,1)S(1)}, bf16[64,2176]{1,0:T(8,128)(2,1)S(1)}, u32[]{:S(2)}, u32[]{:S(2)}) collective-permute-start(bf16[64,2176]{1,0:T(8,128)(2,1)S(1)} %fusion.3.refs_0_.refs_16_), channel_id=1, source_target_pairs={{0,1},{1,0},{2,3},{3,2},{4,5},{5,4},{6,7},{7,6},{8,9},{9,8},{10,11... | collective-permute-start | bytes 835592 | tf_op jit(solution)/shard_map/ppermute | solution.py:296
  133.0 11.9 %collective-permute-start.48 = (bf16[32,2176]{1,0:T(8,128)(2,1)S(1)}, bf16[32,2176]{1,0:T(8,128)(2,1)S(1)}, u32[]{:S(2)}, u32[]{:S(2)}) collective-permute-start(bf16[32,2176]{1,0:T(8,128)(2,1)S(1)} %slice.141), channel_id=1, source_target_pairs={{0,4},{4,0},{8,12},{12,8},{1,5},{5,1},{9,13},{13,9},{2,6},{6,2},{1... | collective-permute-start | bytes 417800 | tf_op jit(solution)/shard_map/ppermute | solution.py:296
  167.5 11.3 %collective-permute-start.52 = (bf16[32,2176]{1,0:T(8,128)(2,1)S(1)}, bf16[32,2176]{1,0:T(8,128)(2,1)S(1)}, u32[]{:S(2)}, u32[]{:S(2)}) collective-permute-start(bf16[32,2176]{1,0:T(8,128)(2,1)S(1)} %get-tuple-element.50), channel_id=1, source_target_pairs={{0,8},{4,12},{8,0},{12,4},{1,9},{5,13},{9,1},{13,5},{2,10},{6,14},... | collective-permute-start | bytes 417800 | tf_op jit(solution)/shard_map/ppermute | solution.py:296
  169.9 10.8 %collective-permute-start.57 = (bf16[32,2176]{1,0:T(8,128)(2,1)S(1)}, bf16[32,2176]{1,0:T(8,128)(2,1)S(1)}, u32[]{:S(2)}, u32[]{:S(2)}) collective-permute-start(bf16[32,2176]{1,0:T(8,128)(2,1)S(1)} %get-tuple-element.55), channel_id=1, source_target_pairs={{0,4},{4,0},{8,12},{12,8},{1,5},{5,1},{9,13},{13,9},{2,6},{6,2},{1... | collective-permute-start | bytes 417800 | tf_op jit(solution)/shard_map/ppermute | solution.py:296
  173.1 13.6 %collective-permute-start.63 = (bf16[32,2176]{1,0:T(8,128)(2,1)S(1)}, bf16[32,2176]{1,0:T(8,128)(2,1)S(1)}, u32[]{:S(2)}, u32[]{:S(2)}) collective-permute-start(bf16[32,2176]{1,0:T(8,128)(2,1)S(1)} %get-tuple-element.61), channel_id=1, source_target_pairs={{0,8},{4,12},{8,0},{12,4},{1,9},{5,13},{9,1},{13,5},{2,10},{6,14},... | collective-permute-start | bytes 417800 | tf_op jit(solution)/shard_map/ppermute | solution.py:296
  (62 other events, 668.9 us)

commit v5 on v4

--- a/solution.py
+++ b/solution.py
@@ -296,14 +296,15 @@
     return lax.ppermute(value, axis, pairs)
 
 
-def spread(block):
-    near = toggled(block, "local", 1)
+def along_local(block):
     far = toggled(block, "local", 2)
-    first = [toggled(block, "group", 1)]
-    second = [toggled(block, "group", 2)]
-    corner = toggled(far, "local", 1)
-    first += [toggled(column, "group", 1) for column in (far, corner)]
-    second += [toggled(column, "group", 2) for column in (far, corner)]
+    return block, toggled(block, "local", 1), far, toggled(far, "local", 1)
+
+
+def spread(columns):
+    block, near, far, corner = columns
+    first = [toggled(column, "group", 1) for column in (block, far, corner)]
+    second = [toggled(column, "group", 2) for column in (block, far, corner)]
     first.insert(1, toggled(first[0], "local", 1))
     second.insert(1, toggled(second[0], "local", 1))
     half = block.shape[0] // 2
@@ -398,21 +399,23 @@
     inputs = layer_inputs[0]
     blocks = result_blocks(rows)
     weights = (gate_half, up_half, down_half)
-    none = jnp.zeros((rows, LANES), jnp.bfloat16)
+    wide_inputs = jnp.pad(inputs, ((0, 0), (0, 0), (0, LANES)))
+    later_inputs = [along_local(wide_inputs[m]) for m in range(1, micro_count)]
     earlier = carried_grad
     grads_out, gates = [], []
     for m in range(micro_count):
         if m > 0:
             earlier = from_behind(grads_out[-1], "pipe", -1)
         incoming = jnp.where(last_section, output_grad[m], earlier)
-        sent = jnp.concatenate(
-            [
-                jnp.concatenate([inputs[m], incoming], axis=0),
-                jnp.concatenate([none, token_probs[m]], axis=0),
-            ],
-            axis=1,
-        )
-        found = spread(sent)
+        wide_incoming = jnp.concatenate([incoming, token_probs[m]], axis=1)
+        if m == 0:
+            columns = along_local(jnp.concatenate([wide_inputs[m], wide_incoming], axis=0))
+        else:
+            columns = [
+                jnp.concatenate(pair, axis=0)
+                for pair in zip(later_inputs[m - 1], along_local(wide_incoming))
+            ]
+        found = spread(columns)
         arrays, plan = piece_plan(found, 0, rows)
         grad_arrays, grad_plan = piece_plan(found, rows, rows)
         pieces = expert_math(arrays, plan, grad_arrays, grad_plan, blocks, expert, weights)

time: 196 us -> 194 us (0.990)
  waiting for transfers between devices: 81.6 us -> 74.5 us
  starting transfers between devices: 78.6 us -> 82.4 us
    ppermute x64 -> x67, waiting for transfers between devices: 79.8 us -> 72.7 us  [toggled(): return lax.ppermute(value, axis, pairs)]
    ppermute x64 -> x67, starting transfers between devices: 77.1 us -> 81 us  [toggled(): return lax.ppermute(value, axis, pairs)]
  transfers between devices with their start and end apart: 65 -> 68, of which waited for: 33 -> 34; matrix products, arithmetic and copies ran while one was open for 1% -> 1% of each run, Pallas kernels for 0% -> 7%
where the time goes in v5:
time: 194 us
  starting transfers between devices  82.4 us (42%)
  waiting for transfers between devices  74.5 us (38%)
  Pallas kernels  28.2 us (15%)
  other arithmetic  4.6 us (2%)
  local copies, waits for them, and re-layouts  2.63 us (1%)
    ppermute x67, starting transfers between devices, toggled(): return lax.ppermute(value, axis, pairs)  81 us
    ppermute x67, waiting for transfers between devices, toggled(): return lax.ppermute(value, axis, pairs)  72.7 us
    pallas_call x2, Pallas kernels, expert_math(): pl.pallas_call(functools.partial(math_kernel, plan, grad_plan, blocks), o...  28.2 us
  transfers between devices with their start and end apart: 68, of which 34 were waited for; matrix products, arithmetic and copies ran while one was open for 1% of the time, Pallas kernels for 7%

profile of v5, /device:TPU:0, one launch (start us, length us, event | category | flops | bytes accessed | tf_op | source)
XLA Modules:
  0.0 193.5 jit_solution(9319286704642951743)
XLA Ops:
  4.2 4.1 %collective-permute-start.7 = (bf16[64,2176]{1,0:T(8,128)(2,1)S(1)}, bf16[64,2176]{1,0:T(8,128)(2,1)S(1)}, u32[]{:S(2)}, u32[]{:S(2)}) collective-permute-start(bf16[64,2176]{1,0:T(8,128)(2,1)S(1)} %maximum_maximum_fusion.refs_0_.refs_16_), channel_id=1, source_target_pairs={{0,2},{1,3},{2,0},{3,1},{4,6},{5,7},{6,4},{7,5},{8,10},{9,11},{10,... | collective-permute-start | bytes 835592 | tf_op jit(solution)/shard_map/ppermute | solution.py:296
  11.3 9.6 %collective-permute-done.7.refs_8_.refs_24_ = bf16[64,2176]{1,0:T(8,128)(2,1)S(1)} collective-permute-done((bf16[64,2176]{1,0:T(8,128)(2,1)S(1)}, bf16[64,2176]{1,0:T(8,128)(2,1)S(1)}, u32[]{:S(2)}, u32[]{:S(2)}) %collective-permute-start.7) | collective-permute-done | bytes 278560 | tf_op jit(solution)/shard_map/ppermute | solution.py:296
  26.7 3.8 %collective-permute-done.11.refs_12_.refs_28_ = bf16[64,2176]{1,0:T(8,128)(2,1)S(1)} collective-permute-done((bf16[64,2176]{1,0:T(8,128)(2,1)S(1)}, bf16[64,2176]{1,0:T(8,128)(2,1)S(1)}, u32[]{:S(2)}, u32[]{:S(2)}) %collective-permute-start.11) | collective-permute-done | bytes 278560 | tf_op jit(solution)/shard_map/ppermute | solution.py:296
  34.2 2.2 %collective-permute-done.5.refs_6_.refs_22_ = bf16[64,2176]{1,0:T(8,128)(2,1)S(1)} collective-permute-done((bf16[64,2176]{1,0:T(8,128)(2,1)S(1)}, bf16[64,2176]{1,0:T(8,128)(2,1)S(1)}, u32[]{:S(2)}, u32[]{:S(2)}) %collective-permute-start.5) | collective-permute-done | bytes 278560 | tf_op jit(solution)/shard_map/ppermute | solution.py:296
  38.0 4.4 %collective-permute-done.4.refs_5_.refs_21_ = bf16[64,2176]{1,0:T(8,128)(2,1)S(1)} collective-permute-done((bf16[64,2176]{1,0:T(8,128)(2,1)S(1)}, bf16[64,2176]{1,0:T(8,128)(2,1)S(1)}, u32[]{:S(2)}, u32[]{:S(2)}) %collective-permute-start.4) | collective-permute-done | bytes 278560 | tf_op jit(solution)/shard_map/ppermute | solution.py:296
  50.0 2.0 %collective-permute-start.18 = (bf16[32,2176]{1,0:T(8,128)(2,1)S(1)}, bf16[32,2176]{1,0:T(8,128)(2,1)S(1)}, u32[]{:S(2)}, u32[]{:S(2)}) collective-permute-start(bf16[32,2176]{1,0:T(8,128)(2,1)S(1)} %slice.130), channel_id=1, source_target_pairs={{0,4},{4,0},{8,12},{12,8},{1,5},{5,1},{9,13},{13,9},{2,6},{6,2},{1... | collective-permute-start | bytes 417800 | tf_op jit(solution)/shard_map/ppermute | solution.py:296
  52.0 1.9 collective-permute-start.41
  55.1 14.1 %expert_math.2 = (bf16[32,2176]{1,0:T(8,128)(2,1)S(1)}, bf16[32,2176]{1,0:T(8,128)(2,1)S(1)}, bf16[32,2176]{1,0:T(8,128)(2,1)S(1)}, bf16[32,2176]{1,0:T(8,128)(2...) custom-call(s32[1]{0:T(128)} %bitcast.1.expert_ref, ...), custom_call_target="tpu_custom_call" | custom-call | flops 7381975040 | bytes 14942208 | tf_op jit(solution)/shard_map/expert_math/pallas_call | solution.py:267
  69.2 2.0 %collective-permute-start.25 = (bf16[32,2176]{1,0:T(8,128)(2,1)S(1)}, bf16[32,2176]{1,0:T(8,128)(2,1)S(1)}, u32[]{:S(2)}, u32[]{:S(2)}) collective-permute-start(bf16[32,2176]{1,0:T(8,128)(2,1)S(1)} %get-tuple-element.42), channel_id=1, source_target_pairs={{0,4},{4,0},{8,12},{12,8},{1,5},{5,1},{9,13},{13,9},{2,6},{6,2},{1... | collective-permute-start | bytes 417800 | tf_op jit(solution)/shard_map/ppermute | solution.py:296
  80.5 2.6 %collective-permute-done.19 = bf16[32,2176]{1,0:T(8,128)(2,1)S(1)} collective-permute-done((bf16[32,2176]{1,0:T(8,128)(2,1)S(1)}, bf16[32,2176]{1,0:T(8,128)(2,1)S(1)}, u32[]{:S(2)}, u32[]{:S(2)}) %collective-permute-start.19) | collective-permute-done | bytes 139296 | tf_op jit(solution)/shard_map/ppermute | solution.py:296
  87.6 1.9 collective-permute-done.26
  91.1 3.5 %collective-permute-start.27 = (bf16[32,2176]{1,0:T(8,128)(2,1)S(1)}, bf16[32,2176]{1,0:T(8,128)(2,1)S(1)}, u32[]{:S(2)}, u32[]{:S(2)}) collective-permute-start(bf16[32,2176]{1,0:T(8,128)(2,1)S(1)} %add_convert_fusion.8), channel_id=1, source_target_pairs={{0,2},{1,3},{2,0},{3,1},{4,6},{5,7},{6,4},{7,5},{8,10},{9,11},{10,... | collective-permute-start | bytes 417800 | tf_op jit(solution)/shard_map/ppermute | solution.py:296
  96.5 2.7 %collective-permute-done.27 = bf16[32,2176]{1,0:T(8,128)(2,1)S(1)} collective-permute-done((bf16[32,2176]{1,0:T(8,128)(2,1)S(1)}, bf16[32,2176]{1,0:T(8,128)(2,1)S(1)}, u32[]{:S(2)}, u32[]{:S(2)}) %collective-permute-start.27) | collective-permute-done | bytes 139296 | tf_op jit(solution)/shard_map/ppermute | solution.py:296
  99.1 2.6 %collective-permute-done.31 = bf16[32,2176]{1,0:T(8,128)(2,1)S(1)} collective-permute-done((bf16[32,2176]{1,0:T(8,128)(2,1)S(1)}, bf16[32,2176]{1,0:T(8,128)(2,1)S(1)}, u32[]{:S(2)}, u32[]{:S(2)}) %collective-permute-start.31) | collective-permute-done | bytes 139296 | tf_op jit(solution)/shard_map/ppermute | solution.py:296
  106.2 2.0 %collective-permute-start.42 = (bf16[32,2176]{1,0:T(8,128)(2,1)S(1)}, bf16[32,2176]{1,0:T(8,128)(2,1)S(1)}, u32[]{:S(2)}, u32[]{:S(2)}) collective-permute-start(bf16[32,2176]{1,0:T(8,128)(2,1)S(1)} %pad_maximum_fusion.5), channel_id=1, source_target_pairs={{0,2},{1,3},{2,0},{3,1},{4,6},{5,7},{6,4},{7,5},{8,10},{9,11},{10,... | collective-permute-start | bytes 417800 | tf_op jit(solution)/shard_map/ppermute | solution.py:296
  110.3 5.2 %collective-permute-done.42 = bf16[32,2176]{1,0:T(8,128)(2,1)S(1)} collective-permute-done((bf16[32,2176]{1,0:T(8,128)(2,1)S(1)}, bf16[32,2176]{1,0:T(8,128)(2,1)S(1)}, u32[]{:S(2)}, u32[]{:S(2)}) %collective-permute-start.42) | collective-permute-done | bytes 139296 | tf_op jit(solution)/shard_map/ppermute | solution.py:296
  117.4 3.8 %collective-permute-done.47 = bf16[32,2176]{1,0:T(8,128)(2,1)S(1)} collective-permute-done((bf16[32,2176]{1,0:T(8,128)(2,1)S(1)}, bf16[32,2176]{1,0:T(8,128)(2,1)S(1)}, u32[]{:S(2)}, u32[]{:S(2)}) %collective-permute-start.47) | collective-permute-done | bytes 139296 | tf_op jit(solution)/shard_map/ppermute | solution.py:296
  123.2 1.9 collective-permute-done.43.refs_9_.refs_25_
  125.2 2.1 %collective-permute-start.39 = (bf16[64,2176]{1,0:T(8,128)(2,1)S(1)}, bf16[64,2176]{1,0:T(8,128)(2,1)S(1)}, u32[]{:S(2)}, u32[]{:S(2)}) collective-permute-start(bf16[64,2176]{1,0:T(8,128)(2,1)S(1)} %collective-permute-done.34.refs_2_.refs_18_), channel_id=1, source_target_pairs={{0,1},{1,0},{2,3},{3,2},{4,5},{5,4},{6,7},{7,6},{8,9},{9,8},{10,11... | collective-permute-start | bytes 835592 | tf_op jit(solution)/shard_map/ppermute | solution.py:296
  127.7 2.5 %collective-permute-done.48.refs_13_.refs_29_ = bf16[64,2176]{1,0:T(8,128)(2,1)S(1)} collective-permute-done((bf16[64,2176]{1,0:T(8,128)(2,1)S(1)}, bf16[64,2176]{1,0:T(8,128)(2,1)S(1)}, u32[]{:S(2)}, u32[]{:S(2)}) %collective-permute-start.48) | collective-permute-done | bytes 278560 | tf_op jit(solution)/shard_map/ppermute | solution.py:296
  134.0 4.5 %collective-permute-done.39.refs_6_.refs_22_ = bf16[64,2176]{1,0:T(8,128)(2,1)S(1)} collective-permute-done((bf16[64,2176]{1,0:T(8,128)(2,1)S(1)}, bf16[64,2176]{1,0:T(8,128)(2,1)S(1)}, u32[]{:S(2)}, u32[]{:S(2)}) %collective-permute-start.39) | collective-permute-done | bytes 278560 | tf_op jit(solution)/shard_map/ppermute | solution.py:296
  150.7 14.1 %expert_math.3 = (bf16[32,2176]{1,0:T(8,128)(2,1)S(1)}, bf16[32,2176]{1,0:T(8,128)(2,1)S(1)}, bf16[32,2176]{1,0:T(8,128)(2,1)S(1)}, bf16[32,2176]{1,0:T(8,128)(2...) custom-call(s32[1]{0:T(128)} %bitcast.1.expert_ref, ...), custom_call_target="tpu_custom_call" | custom-call | flops 7381975040 | bytes 14942208 | tf_op jit(solution)/shard_map/expert_math/pallas_call | solution.py:267
  174.4 3.3 %collective-permute-done.55 = bf16[32,2176]{1,0:T(8,128)(2,1)S(1)} collective-permute-done((bf16[32,2176]{1,0:T(8,128)(2,1)S(1)}, bf16[32,2176]{1,0:T(8,128)(2,1)S(1)}, u32[]{:S(2)}, u32[]{:S(2)}) %collective-permute-start.55) | collective-permute-done | bytes 139296 | tf_op jit(solution)/shard_map/ppermute | solution.py:296
  187.5 2.7 %collective-permute-done.63 = bf16[32,2176]{1,0:T(8,128)(2,1)S(1)} collective-permute-done((bf16[32,2176]{1,0:T(8,128)(2,1)S(1)}, bf16[32,2176]{1,0:T(8,128)(2,1)S(1)}, u32[]{:S(2)}, u32[]{:S(2)}) %collective-permute-start.63) | collective-permute-done | bytes 139296 | tf_op jit(solution)/shard_map/ppermute | solution.py:296
  (216 shorter events, 92.8 us)
Async XLA Ops:
  4.2 16.7 %collective-permute-start.7 = (bf16[64,2176]{1,0:T(8,128)(2,1)S(1)}, bf16[64,2176]{1,0:T(8,128)(2,1)S(1)}, u32[]{:S(2)}, u32[]{:S(2)}) collective-permute-start(bf16[64,2176]{1,0:T(8,128)(2,1)S(1)} %maximum_maximum_fusion.refs_0_.refs_16_), channel_id=1, source_target_pairs={{0,2},{1,3},{2,0},{3,1},{4,6},{5,7},{6,4},{7,5},{8,10},{9,11},{10,... | collective-permute-start | bytes 835592 | tf_op jit(solution)/shard_map/ppermute | solution.py:296
  8.3 16.3 %collective-permute-start.1 = (bf16[64,2176]{1,0:T(8,128)(2,1)S(1)}, bf16[64,2176]{1,0:T(8,128)(2,1)S(1)}, u32[]{:S(2)}, u32[]{:S(2)}) collective-permute-start(bf16[64,2176]{1,0:T(8,128)(2,1)S(1)} %maximum_maximum_fusion.refs_0_.refs_16_), channel_id=1, source_target_pairs={{0,8},{4,12},{8,0},{12,4},{1,9},{5,13},{9,1},{13,5},{2,10},{6,14},... | collective-permute-start | bytes 835592 | tf_op jit(solution)/shard_map/ppermute | solution.py:296
  9.8 16.1 %collective-permute-start = (bf16[64,2176]{1,0:T(8,128)(2,1)S(1)}, bf16[64,2176]{1,0:T(8,128)(2,1)S(1)}, u32[]{:S(2)}, u32[]{:S(2)}) collective-permute-start(bf16[64,2176]{1,0:T(8,128)(2,1)S(1)} %maximum_maximum_fusion.refs_0_.refs_16_), channel_id=1, source_target_pairs={{0,4},{4,0},{8,12},{12,8},{1,5},{5,1},{9,13},{13,9},{2,6},{6,2},{1... | collective-permute-start | bytes 835592 | tf_op jit(solution)/shard_map/ppermute | solution.py:296
  23.1 10.5 %collective-permute-start.9 = (bf16[64,2176]{1,0:T(8,128)(2,1)S(1)}, bf16[64,2176]{1,0:T(8,128)(2,1)S(1)}, u32[]{:S(2)}, u32[]{:S(2)}) collective-permute-start(bf16[64,2176]{1,0:T(8,128)(2,1)S(1)} %collective-permute-done.7.refs_8_.refs_24_), channel_id=1, source_target_pairs={{0,8},{4,12},{8,0},{12,4},{1,9},{5,13},{9,1},{13,5},{2,10},{6,14},... | collective-permute-start | bytes 835592 | tf_op jit(solution)/shard_map/ppermute | solution.py:296
  24.6 11.8 %collective-permute-start.5 = (bf16[64,2176]{1,0:T(8,128)(2,1)S(1)}, bf16[64,2176]{1,0:T(8,128)(2,1)S(1)}, u32[]{:S(2)}, u32[]{:S(2)}) collective-permute-start(bf16[64,2176]{1,0:T(8,128)(2,1)S(1)} %collective-permute-done.1.refs_2_.refs_18_), channel_id=1, source_target_pairs={{0,1},{1,0},{2,3},{3,2},{4,5},{5,4},{6,7},{7,6},{8,9},{9,8},{10,11... | collective-permute-start | bytes 835592 | tf_op jit(solution)/shard_map/ppermute | solution.py:296
  26.0 16.4 %collective-permute-start.4 = (bf16[64,2176]{1,0:T(8,128)(2,1)S(1)}, bf16[64,2176]{1,0:T(8,128)(2,1)S(1)}, u32[]{:S(2)}, u32[]{:S(2)}) collective-permute-start(bf16[64,2176]{1,0:T(8,128)(2,1)S(1)} %collective-permute-done.refs_1_.refs_17_), channel_id=1, source_target_pairs={{0,1},{1,0},{2,3},{3,2},{4,5},{5,4},{6,7},{7,6},{8,9},{9,8},{10,11... | collective-permute-start | bytes 835592 | tf_op jit(solution)/shard_map/ppermute | solution.py:296
  30.5 13.5 %collective-permute-start.12 = (bf16[64,2176]{1,0:T(8,128)(2,1)S(1)}, bf16[64,2176]{1,0:T(8,128)(2,1)S(1)}, u32[]{:S(2)}, u32[]{:S(2)}) collective-permute-start(bf16[64,2176]{1,0:T(8,128)(2,1)S(1)} %collective-permute-done.11.refs_12_.refs_28_), channel_id=1, source_target_pairs={{0,4},{4,0},{8,12},{12,8},{1,5},{5,1},{9,13},{13,9},{2,6},{6,2},{1... | collective-permute-start | bytes 835592 | tf_op jit(solution)/shard_map/ppermute | solution.py:296
  32.0 12.5 %collective-permute-start.13 = (bf16[64,2176]{1,0:T(8,128)(2,1)S(1)}, bf16[64,2176]{1,0:T(8,128)(2,1)S(1)}, u32[]{:S(2)}, u32[]{:S(2)}) collective-permute-start(bf16[64,2176]{1,0:T(8,128)(2,1)S(1)} %collective-permute-done.11.refs_12_.refs_28_), channel_id=1, source_target_pairs={{0,8},{4,12},{8,0},{12,4},{1,9},{5,13},{9,1},{13,5},{2,10},{6,14},... | collective-permute-start | bytes 835592 | tf_op jit(solution)/shard_map/ppermute | solution.py:296
  33.6 13.0 %collective-permute-start.3 = (bf16[64,2176]{1,0:T(8,128)(2,1)S(1)}, bf16[64,2176]{1,0:T(8,128)(2,1)S(1)}, u32[]{:S(2)}, u32[]{:S(2)}) collective-permute-start(bf16[64,2176]{1,0:T(8,128)(2,1)S(1)} %maximum_maximum_fusion.refs_0_.refs_16_), channel_id=1, source_target_pairs={{0,1},{1,0},{2,3},{3,2},{4,5},{5,4},{6,7},{7,6},{8,9},{9,8},{10,11... | collective-permute-start | bytes 835592 | tf_op jit(solution)/shard_map/ppermute | solution.py:296
  36.5 11.4 %collective-permute-start.15 = (bf16[32,2176]{1,0:T(8,128)(2,1)S(1)}, bf16[32,2176]{1,0:T(8,128)(2,1)S(1)}, u32[]{:S(2)}, u32[]{:S(2)}) collective-permute-start(bf16[32,2176]{1,0:T(8,128)(2,1)S(1)} %slice.127), channel_id=1, source_target_pairs={{0,4},{4,0},{8,12},{12,8},{1,5},{5,1},{9,13},{13,9},{2,6},{6,2},{1... | collective-permute-start | bytes 417800 | tf_op jit(solution)/shard_map/ppermute | solution.py:296
  52.0 19.2 %collective-permute-start.41 = (bf16[32,2176]{1,0:T(8,128)(2,1)S(1)}, bf16[32,2176]{1,0:T(8,128)(2,1)S(1)}, u32[]{:S(2)}, u32[]{:S(2)}) collective-permute-start(bf16[32,2176]{1,0:T(8,128)(2,1)S(1)} %get-tuple-element.64), channel_id=1, source_target_pairs={{0,2},{1,3},{2,0},{3,1},{4,6},{5,7},{6,4},{7,5},{8,10},{9,11},{10,... | collective-permute-start | bytes 417800 | tf_op jit(solution)/shard_map/ppermute | solution.py:296
  71.2 33.2 %collective-permute-start.46 = (bf16[32,2176]{1,0:T(8,128)(2,1)S(1)}, bf16[32,2176]{1,0:T(8,128)(2,1)S(1)}, u32[]{:S(2)}, u32[]{:S(2)}) collective-permute-start(bf16[32,2176]{1,0:T(8,128)(2,1)S(1)} %collective-permute-done.41), channel_id=1, source_target_pairs={{0,1},{1,0},{2,3},{3,2},{4,5},{5,4},{6,7},{7,6},{8,9},{9,8},{10,11... | collective-permute-start | bytes 417800 | tf_op jit(solution)/shard_map/ppermute | solution.py:296
  72.0 14.8 %collective-permute-start.24 = (bf16[32,2176]{1,0:T(8,128)(2,1)S(1)}, bf16[32,2176]{1,0:T(8,128)(2,1)S(1)}, u32[]{:S(2)}, u32[]{:S(2)}) collective-permute-start(bf16[32,2176]{1,0:T(8,128)(2,1)S(1)} %get-tuple-element.40), channel_id=1, source_target_pairs={{0,4},{4,0},{8,12},{12,8},{1,5},{5,1},{9,13},{13,9},{2,6},{6,2},{1... | collective-permute-start | bytes 417800 | tf_op jit(solution)/shard_map/ppermute | solution.py:296
  74.8 16.3 %collective-permute-start.30 = (bf16[32,2176]{1,0:T(8,128)(2,1)S(1)}, bf16[32,2176]{1,0:T(8,128)(2,1)S(1)}, u32[]{:S(2)}, u32[]{:S(2)}) collective-permute-start(bf16[32,2176]{1,0:T(8,128)(2,1)S(1)} %get-tuple-element.46), channel_id=1, source_target_pairs={{0,8},{4,12},{8,0},{12,4},{1,9},{5,13},{9,1},{13,5},{2,10},{6,14},... | collective-permute-start | bytes 417800 | tf_op jit(solution)/shard_map/ppermute | solution.py:296
  108.2 13.5 %collective-permute-start.33 = (bf16[64,2176]{1,0:T(8,128)(2,1)S(1)}, bf16[64,2176]{1,0:T(8,128)(2,1)S(1)}, u32[]{:S(2)}, u32[]{:S(2)}) collective-permute-start(bf16[64,2176]{1,0:T(8,128)(2,1)S(1)} %maximum_maximum_fusion.1.refs_0_.refs_16_), channel_id=1, source_target_pairs={{0,4},{4,0},{8,12},{12,8},{1,5},{5,1},{9,13},{13,9},{2,6},{6,2},{1... | collective-permute-start | bytes 835592 | tf_op jit(solution)/shard_map/ppermute | solution.py:296
  108.8 14.1 %collective-permute-start.34 = (bf16[64,2176]{1,0:T(8,128)(2,1)S(1)}, bf16[64,2176]{1,0:T(8,128)(2,1)S(1)}, u32[]{:S(2)}, u32[]{:S(2)}) collective-permute-start(bf16[64,2176]{1,0:T(8,128)(2,1)S(1)} %maximum_maximum_fusion.1.refs_0_.refs_16_), channel_id=1, source_target_pairs={{0,8},{4,12},{8,0},{12,4},{1,9},{5,13},{9,1},{13,5},{2,10},{6,14},... | collective-permute-start | bytes 835592 | tf_op jit(solution)/shard_map/ppermute | solution.py:296
  116.1 11.2 %collective-permute-start.44 = (bf16[64,2176]{1,0:T(8,128)(2,1)S(1)}, bf16[64,2176]{1,0:T(8,128)(2,1)S(1)}, u32[]{:S(2)}, u32[]{:S(2)}) collective-permute-start(bf16[64,2176]{1,0:T(8,128)(2,1)S(1)} %constant_dynamic-update-slice_fusion.refs_8_.refs_24_), channel_id=1, source_target_pairs={{0,8},{4,12},{8,0},{12,4},{1,9},{5,13},{9,1},{13,5},{2,10},{6,14},... | collective-permute-start | bytes 835592 | tf_op jit(solution)/shard_map/ppermute | solution.py:296
  125.2 13.4 %collective-permute-start.39 = (bf16[64,2176]{1,0:T(8,128)(2,1)S(1)}, bf16[64,2176]{1,0:T(8,128)(2,1)S(1)}, u32[]{:S(2)}, u32[]{:S(2)}) collective-permute-start(bf16[64,2176]{1,0:T(8,128)(2,1)S(1)} %collective-permute-done.34.refs_2_.refs_18_), channel_id=1, source_target_pairs={{0,1},{1,0},{2,3},{3,2},{4,5},{5,4},{6,7},{7,6},{8,9},{9,8},{10,11... | collective-permute-start | bytes 835592 | tf_op jit(solution)/shard_map/ppermute | solution.py:296
  127.3 13.2 %collective-permute-start.36 = (bf16[32,2176]{1,0:T(8,128)(2,1)S(1)}, bf16[32,2176]{1,0:T(8,128)(2,1)S(1)}, u32[]{:S(2)}, u32[]{:S(2)}) collective-permute-start(bf16[32,2176]{1,0:T(8,128)(2,1)S(1)} %get-tuple-element.64), channel_id=1, source_target_pairs={{0,1},{1,0},{2,3},{3,2},{4,5},{5,4},{6,7},{7,6},{8,9},{9,8},{10,11... | collective-permute-start | bytes 417800 | tf_op jit(solution)/shard_map/ppermute | solution.py:296
  130.2 11.8 %collective-permute-start.37 = (bf16[32,2176]{1,0:T(8,128)(2,1)S(1)}, bf16[32,2176]{1,0:T(8,128)(2,1)S(1)}, u32[]{:S(2)}, u32[]{:S(2)}) collective-permute-start(bf16[32,2176]{1,0:T(8,128)(2,1)S(1)} %pad_maximum_fusion.5), channel_id=1, source_target_pairs={{0,1},{1,0},{2,3},{3,2},{4,5},{5,4},{6,7},{7,6},{8,9},{9,8},{10,11... | collective-permute-start | bytes 417800 | tf_op jit(solution)/shard_map/ppermute | solution.py:296
  132.0 11.0 %collective-permute-start.35 = (bf16[32,2176]{1,0:T(8,128)(2,1)S(1)}, bf16[32,2176]{1,0:T(8,128)(2,1)S(1)}, u32[]{:S(2)}, u32[]{:S(2)}) collective-permute-start(bf16[32,2176]{1,0:T(8,128)(2,1)S(1)} %slice.135), channel_id=1, source_target_pairs={{0,8},{4,12},{8,0},{12,4},{1,9},{5,13},{9,1},{13,5},{2,10},{6,14},... | collective-permute-start | bytes 417800 | tf_op jit(solution)/shard_map/ppermute | solution.py:296
  133.1 11.4 %collective-permute-start.51 = (bf16[32,2176]{1,0:T(8,128)(2,1)S(1)}, bf16[32,2176]{1,0:T(8,128)(2,1)S(1)}, u32[]{:S(2)}, u32[]{:S(2)}) collective-permute-start(bf16[32,2176]{1,0:T(8,128)(2,1)S(1)} %slice.139), channel_id=1, source_target_pairs={{0,4},{4,0},{8,12},{12,8},{1,5},{5,1},{9,13},{13,9},{2,6},{6,2},{1... | collective-permute-start | bytes 417800 | tf_op jit(solution)/shard_map/ppermute | solution.py:296
  166.2 13.8 %collective-permute-start.60 = (bf16[32,2176]{1,0:T(8,128)(2,1)S(1)}, bf16[32,2176]{1,0:T(8,128)(2,1)S(1)}, u32[]{:S(2)}, u32[]{:S(2)}) collective-permute-start(bf16[32,2176]{1,0:T(8,128)(2,1)S(1)} %get-tuple-element.55), channel_id=1, source_target_pairs={{0,4},{4,0},{8,12},{12,8},{1,5},{5,1},{9,13},{13,9},{2,6},{6,2},{1... | collective-permute-start | bytes 417800 | tf_op jit(solution)/shard_map/ppermute | solution.py:296
  167.8 13.5 %collective-permute-start.66 = (bf16[32,2176]{1,0:T(8,128)(2,1)S(1)}, bf16[32,2176]{1,0:T(8,128)(2,1)S(1)}, u32[]{:S(2)}, u32[]{:S(2)}) collective-permute-start(bf16[32,2176]{1,0:T(8,128)(2,1)S(1)} %get-tuple-element.61), channel_id=1, source_target_pairs={{0,8},{4,12},{8,0},{12,4},{1,9},{5,13},{9,1},{13,5},{2,10},{6,14},... | collective-permute-start | bytes 417800 | tf_op jit(solution)/shard_map/ppermute | solution.py:296
  (64 other events, 679.9 us)
